TPU v7x, 32 devices: a whole 2x2x4 slice. The times are simulated.
32 devices in a mesh: mat: 4 (over y, x), gr: 4 (over z), gc: 2 (over core).
Axes of the slice: x: 2, y: 2, z: 4, core: 2. Of those that a mesh axis runs over, the one named last changes fastest.
Arguments:
- iterate: bfloat16 [2, 4, 512, 7168], P(None, 'gr', ('mat', 'gc')), may hold values from -3 to 3
Outputs:
- next_iterate: bfloat16 [2, 2048, 7168], P(None, 'gr', ('mat', 'gc'))
All inputs are finite; a program needn't handle non-finite values.
Results may differ from a plain program's by a relative error of at most 0.0055.
Values may be sent and summed in bfloat16 or wider, within the bound.
No kernel may reach another device: no remote copies, remote signals or barrier semaphores. Data moves between devices by JAX's collectives and lax.ppermute only.
A program may use at most 64 MiB of HBM per device.

v0:
```python
import jax
import jax.numpy as jnp
from jax import lax
from jax.sharding import PartitionSpec as P

N = 7168


linear_coef = 3.4445
cubic_coef = -4.775
quintic_coef = 2.0315


def body(iterate):
    regrouped = lax.all_to_all(iterate, ("mat", "gc"), split_axis=3, concat_axis=2, tiled=True)
    row_block = regrouped[:, 0]
    panel_rows = lax.all_gather(row_block, "gr", axis=1, tiled=True)
    total_rows = panel_rows.shape[1]
    groups = lax.axis_size(("mat", "gc"))
    gram_width = total_rows // groups
    inv_cols = 1.0 / N
    partial_value = jnp.einsum(
        "irc,ijc->irj", row_block, panel_rows, preferred_element_type=jnp.float32
    )
    gram_rows = (lax.psum(partial_value, ("mat", "gc")) * inv_cols).astype(jnp.bfloat16)
    own_block = lax.dynamic_slice_in_dim(
        gram_rows, lax.axis_index(("mat", "gc")) * gram_width, gram_width, 2
    )
    square = jnp.einsum(
        "irk,ikj->irj",
        gram_rows,
        lax.all_gather(own_block, "gr", axis=1, tiled=True),
        preferred_element_type=jnp.float32,
    )
    poly_block = (cubic_coef * own_block.astype(jnp.float32) + quintic_coef * square).astype(
        jnp.bfloat16
    )
    mixed_sum = jnp.einsum(
        "irk,ikc->irc",
        lax.all_gather(poly_block, ("mat", "gc"), axis=2, tiled=True),
        panel_rows,
        preferred_element_type=jnp.float32,
    )
    result = linear_coef * row_block.astype(jnp.float32) + mixed_sum
    return result.astype(jnp.bfloat16)


def solution(mesh):
    return jax.shard_map(
        body,
        mesh=mesh,
        in_specs=(P(None, "gr", ("mat", "gc"), None),),
        out_specs=P(None, "gr", ("mat", "gc")),
        check_vma=False,
    )
```

profile of v0, /device:TPU:0, one launch (start us, length us, event | category | flops | bytes accessed | tf_op | source)
XLA Modules:
  0.0 446.6 jit_solution(4680133679463440846)
XLA Ops:
  6.5 0.0 all-gather.4.cloned.1.call-start
  6.5 8.6 %copy.8 = bf16[2,1,64,7168]{2,0,1,3:T(2,128)(2,1)} copy(bf16[2,1,64,7168]{3,2,1,0:T(8,128)(2,1)} %param.1) | data formatting | bytes 3670016 | tf_op args[0]
  15.1 6.1 %reshape.1 = bf16[8,2,57344]{2,1,0:T(2,128)(2,1)S(1)} reshape(bf16[7168,1,2,64]{3,2,1,0:T(2,128)(2,1)} %bitcast.14) | data formatting | bytes 3670016
  21.2 28.9 %all_to_all.15 = bf16[8,2,57344]{2,1,0:T(2,128)(2,1)} all-to-all(bf16[8,2,57344]{2,1,0:T(2,128)(2,1)S(1)} %reshape.1), channel_id=1, replica_groups=mesh['mat'=4,'gr'=4,'gc'=2] {'mat','gc'}, dimensions={0} | all-to-all | bytes 3670016 | tf_op jit(solution)/shard_map/all_to_all | solution.py:15
  50.1 7.1 %reshape.2 = bf16[7168,1,2,64]{3,2,1,0:T(2,128)(2,1)} reshape(bf16[8,2,57344]{2,1,0:T(2,128)(2,1)} %all_to_all.15) | data formatting | bytes 3670016
  57.2 9.4 %copy.12 = bf16[2,1,64,8,896]{4,2,3,0,1:T(8,128)(2,1)} copy(bf16[2,1,64,8,896]{2,0,4,3,1:T(2,128)(2,1)} %bitcast.13) | data formatting | bytes 3670016 | tf_op jit(solution)/shard_map/all_to_all | solution.py:15
  66.6 0.0 all-gather.4.cloned.1.call-update
  66.6 0.0 all-reduce.2.cloned.1.call-start
  66.6 132.0 %all-gather.4.cloned.1.call-done = bf16[2,2048,896]{2,1,0:T(8,128)(2,1)} async-done(((bf16[2,512,896]{2,1,0:T(8,128)(2,1)}), bf16[2,2048,896]{2,1,0:T(8,128)(2,1)}) %all-gather.4.cloned.1.call-update) | async-done | bytes 7340048 | tf_op jit(solution)/shard_map/all_gather | solution.py:17
  198.6 11.4 %fusion.2 = f32[2,512,2048]{2,1,0:T(8,128)} fusion(bf16[2,512,896]{2,1,0:T(8,128)(2,1)} %bitcast.16, bf16[2,2048,896]{2,1,0:T(8,128)(2,1)} %all-gather.4.cloned.1.call-done), kind=kOutput, calls=%fused_computation.6 | convolution fusion | flops 3758096384 | bytes 17563648 | tf_op jit(solution)/shard_map/irc,ijc->irj/dot_general | solution.py:22
  210.0 0.0 all-reduce.2.cloned.1.call-update
  210.1 0.0 all-gather.6.cloned.1.call-start
  210.1 124.9 %all-reduce.2.cloned.1.call-done = f32[2,512,2048]{2,1,0:T(8,128)} async-done(((f32[2,512,2048]{2,1,0:T(8,128)}), f32[2,512,2048]{2,1,0:T(8,128)}) %all-reduce.2.cloned.1.call-update) | async-done | bytes 8388624 | tf_op jit(solution)/shard_map/psum | solution.py:25
  335.0 4.6 %multiply_convert_fusion = bf16[2,512,2048]{2,1,0:T(8,128)(2,1)S(1)} fusion(f32[2,512,2048]{2,1,0:T(8,128)} %all-reduce.2.cloned.1.call-done), kind=kLoop, calls=%fused_computation | loop fusion | flops 4194304 | bytes 12582912 | tf_op jit(solution)/shard_map/convert_element_type | solution.py:25
  339.5 1.9 copy-done.1
  341.5 0.9 constant_dynamic-slice_fusion
  342.4 0.0 all-gather.6.cloned.1.call-update
  342.4 0.0 copy-start
  342.4 0.0 all-gather.8.cloned.1.call-start
  342.5 46.2 %all-gather.6.cloned.1.call-done = bf16[2,2048,256]{2,1,0:T(8,128)(2,1)} async-done(((bf16[2,512,256]{2,1,0:T(8,128)(2,1)}), bf16[2,2048,256]{2,1,0:T(8,128)(2,1)}) %all-gather.6.cloned.1.call-update) | async-done | bytes 2097168 | tf_op jit(solution)/shard_map/all_gather | solution.py:32
  388.7 5.0 %fusion.1 = bf16[2,512,256]{2,1,0:T(8,128)(2,1)} fusion(bf16[2,512,2048]{2,1,0:T(8,128)(2,1)} %copy-done.1, bf16[2,2048,256]{2,1,0:T(8,128)(2,1)} %all-gather.6.cloned.1.call-done, bf16[2,512,256]{2,1,0:T(8,128)(2,1)} %constant_dynamic-slice_fusion), kind=kOutput, calls=%fused_computation.4 | convolution fusion | flops 1075052544 | bytes 7340032 | tf_op jit(solution)/shard_map/irk,ikj->irj/dot_general | solution.py:29
  393.6 0.0 all-gather.8.cloned.1.call-update
  393.7 36.3 %all-gather.8.cloned.1.call-done = bf16[2,512,2048]{2,1,0:T(8,128)(2,1)} async-done(((bf16[2,512,256]{2,1,0:T(8,128)(2,1)}), bf16[2,512,2048]{2,1,0:T(8,128)(2,1)}) %all-gather.8.cloned.1.call-update) | async-done | bytes 4194320 | tf_op jit(solution)/shard_map/all_gather | solution.py:40
  430.0 10.1 %add_convert_fusion = bf16[2,512,896]{2,1,0:T(8,128)(2,1)} fusion(bf16[2,512,896]{2,1,0:T(8,128)(2,1)S(1)} %bitcast.17, bf16[2,512,2048]{2,1,0:T(8,128)(2,1)} %all-gather.8.cloned.1.call-done, bf16[2,2048,896]{2,1,0:T(8,128)(2,1)} %all-gather.4.cloned.1.call-done), kind=kOutput, calls=%fused_computation.1 | convolution fusion | flops 3761766400 | bytes 15204352 | tf_op jit(solution)/shard_map/irk,ikc->irc/dot_general | solution.py:38
  (2 shorter events, 0.0 us)
Async XLA Ops:
  6.5 192.1 %all-gather.4.cloned.1.call-start = ((), (), s32[]{:S(2)}) async-start(), calls=%async_computation.1 | async-start | bytes 9175040 | tf_op jit(solution)/shard_map/all_gather | solution.py:17
  66.6 268.4 %all-reduce.2.cloned.1.call-start = ((), (), s32[]{:S(2)}) async-start(), calls=%async_computation.2 | async-start | bytes 16777216 | tf_op jit(solution)/shard_map/psum | solution.py:25
  210.1 178.6 %all-gather.6.cloned.1.call-start = ((), (), s32[]{:S(2)}) async-start(), calls=%async_computation.3 | async-start | bytes 2621440 | tf_op jit(solution)/shard_map/all_gather | solution.py:32
  339.5 2.0 copy-start.1
  342.4 87.6 %copy-start = (bf16[2,1,64,8,896]{4,2,3,0,1:T(8,128)(2,1)S(1)}, bf16[2,1,64,8,896]{4,2,3,0,1:T(8,128)(2,1)}, u32[]{:S(2)}) copy-start(bf16[2,1,64,8,896]{4,2,3,0,1:T(8,128)(2,1)} %copy.12) | copy-start | bytes 5505028
  342.4 87.6 %all-gather.8.cloned.1.call-start = ((), (), s32[]{:S(2)}) async-start(), calls=%async_computation.4 | async-start | bytes 4718592 | tf_op jit(solution)/shard_map/all_gather | solution.py:40
Sparse Core Ops, SparseCore 0:
  66.7 131.8 all-gather.3
  210.2 124.7 all-reduce.1
  342.5 46.1 all-gather.5
  393.8 36.1 all-gather.7
where the time goes:
time: 447 us
  waiting for transfers between devices  339 us (76%)
  local copies, waits for them, and re-layouts  34 us (8%)
  blocking collectives  28.9 us (6%)
  matrix products  26.5 us (6%)
  between operations  13.2 us (3%)
  other arithmetic  4.55 us (1%)
    all_gather x1, waiting for transfers between devices, body(): panel_rows = lax.all_gather(row_block, 'gr', axis=1, tiled=True)  132 us
    psum x1, waiting for transfers between devices, body(): lax.psum(partial_value, ('mat', 'gc')) * inv_cols  125 us
    all_gather x1, waiting for transfers between devices, body(): lax.all_gather(own_block, 'gr', axis=1, tiled=True)  46.2 us
    all_gather x1, waiting for transfers between devices, body(): lax.all_gather(poly_block, ('mat', 'gc'), axis=2, tiled=True)  36.3 us
    all_to_all x1, blocking collectives, body(): lax.all_to_all(iterate, ('mat', 'gc'), split_axis=3, concat_axis=2, tiled...  28.9 us
    unnamed x7, local copies, waits for them, and re-layouts  23.7 us
    dot_general x1, matrix products, body(): jnp.einsum('irc,ijc->irj', row_block, panel_rows, preferred_element_type=...  11.4 us
    dot_general x1, matrix products, body(): jnp.einsum('irk,ikc->irc', lax.all_gather(poly_block, ('mat', 'gc'), axis...  10.1 us
  transfers between devices with their start and end apart: 4, of which 4 were waited for; matrix products, arithmetic and copies ran while one was open for 0% of the time, Pallas kernels for 0%

commit v1 on v0

--- a/solution.py
+++ b/solution.py
@@ -1,24 +1,27 @@
+import functools
+
 import jax
 import jax.numpy as jnp
 from jax import lax
+from jax.experimental import pallas as pl
+from jax.experimental.pallas import tpu as pltpu
 from jax.sharding import PartitionSpec as P
-
-N = 7168
-
 
 linear_coef = 3.4445
 cubic_coef = -4.775
 quintic_coef = 2.0315
 
-
-def body(iterate):
+AXES = ("mat", "gr", "gc")
+
+
+def plain_body(iterate):
     regrouped = lax.all_to_all(iterate, ("mat", "gc"), split_axis=3, concat_axis=2, tiled=True)
     row_block = regrouped[:, 0]
     panel_rows = lax.all_gather(row_block, "gr", axis=1, tiled=True)
     total_rows = panel_rows.shape[1]
     groups = lax.axis_size(("mat", "gc"))
     gram_width = total_rows // groups
-    inv_cols = 1.0 / N
+    inv_cols = 1.0 / iterate.shape[-1]
     partial_value = jnp.einsum(
         "irc,ijc->irj", row_block, panel_rows, preferred_element_type=jnp.float32
     )
@@ -45,9 +48,212 @@
     return result.astype(jnp.bfloat16)
 
 
+CHIPS = 8
+BLOCK = 128
+STRIP = 9 * BLOCK
+PARAMS = dict(vmem_limit_bytes=48 * 1024 * 1024)
+
+
+def send(value, move):
+    perm = []
+    for m in range(4):
+        for r in range(4):
+            for c in range(2):
+                to = move(m, r, c)
+                perm.append((m * 8 + r * 2 + c, to[0] * 8 + to[1] * 2 + to[2]))
+    return lax.ppermute(value, AXES, perm)
+
+
+def across(d):
+    return lambda m, r, c: (m ^ (d >> 1), r ^ (d & 1), c)
+
+
+def other_core(m, r, c):
+    return m, r, 1 - c
+
+
+def cut_kernel(x_ref, o_ref, sems):
+    copies = []
+    width = o_ref.shape[-1]
+    for q in range(2):
+        for k in range(CHIPS):
+            copies.append(
+                pltpu.make_async_copy(
+                    x_ref.at[q, :, pl.ds(k * width, width)],
+                    o_ref.at[q, k % 2, k // 2],
+                    sems.at[q * CHIPS + k],
+                )
+            )
+    for copy in copies:
+        copy.start()
+    for copy in copies:
+        copy.wait()
+
+
+def cut(x):
+    _, rows, cols = x.shape
+    return pl.pallas_call(
+        cut_kernel,
+        out_shape=jax.ShapeDtypeStruct((2, 2, 4, rows, cols // CHIPS), x.dtype),
+        in_specs=[pl.BlockSpec(memory_space=pl.ANY)],
+        out_specs=pl.BlockSpec(memory_space=pl.ANY),
+        scratch_shapes=[pltpu.SemaphoreType.DMA((16,))],
+        compiler_params=pltpu.CompilerParams(**PARAMS),
+        name="cut_columns",
+    )(x)
+
+
+def gram_kernel(p_ref, own_ref, other_ref, *rest):
+    outs, strips = rest[:CHIPS], rest[CHIPS]
+    dims = (((1,), (1,)), ((), ()))
+    for t in range(4):
+        lo = 256 * t
+        rows = own_ref[lo : lo + 256, :]
+        mine = lax.dot_general(rows, own_ref[lo:1024, :], dims, preferred_element_type=jnp.float32)
+        theirs = lax.dot_general(
+            rows, other_ref[0 : lo + 256, :], dims, preferred_element_type=jnp.float32
+        )
+        both = jnp.concatenate([mine, theirs], axis=1).astype(jnp.bfloat16)
+        strips[2 * t] = both[:128, :STRIP]
+        strips[2 * t + 1] = both[128:, 128 : 128 + STRIP]
+    p = p_ref[0]
+    for d in range(CHIPS):
+        outs[d][...] = strips[p ^ d]
+
+
+def gram_strips(p, own, other):
+    return pl.pallas_call(
+        gram_kernel,
+        out_shape=[jax.ShapeDtypeStruct((BLOCK, STRIP), jnp.bfloat16)] * CHIPS,
+        in_specs=[pl.BlockSpec(memory_space=pltpu.SMEM)]
+        + [pl.BlockSpec(memory_space=pltpu.VMEM)] * 2,
+        out_specs=[pl.BlockSpec(memory_space=pltpu.VMEM)] * CHIPS,
+        scratch_shapes=[pltpu.VMEM((CHIPS, BLOCK, STRIP), jnp.bfloat16)],
+        compiler_params=pltpu.CompilerParams(**PARAMS),
+        name="gram_strips",
+    )(p, own, other)
+
+
+def add_kernel(scale, *refs):
+    total = refs[0][...].astype(jnp.float32)
+    for ref in refs[1:-1]:
+        total += ref[...].astype(jnp.float32)
+    refs[-1][...] = (total * scale).astype(jnp.bfloat16)
+
+
+def add_strips(parts, scale):
+    return pl.pallas_call(
+        functools.partial(add_kernel, scale),
+        out_shape=jax.ShapeDtypeStruct((BLOCK, STRIP), jnp.bfloat16),
+        in_specs=[pl.BlockSpec(memory_space=pltpu.VMEM)] * CHIPS,
+        out_specs=pl.BlockSpec(memory_space=pltpu.VMEM),
+        compiler_params=pltpu.CompilerParams(**PARAMS),
+        name="add_strips",
+    )(*parts)
+
+
+def stack_kernel(p_ref, *refs):
+    parts, out, sems = refs[:CHIPS], refs[CHIPS], refs[CHIPS + 1]
+    p = p_ref[0]
+    copies = [
+        pltpu.make_async_copy(parts[d], out.at[p ^ d], sems.at[d]) for d in range(CHIPS)
+    ]
+    for copy in copies:
+        copy.start()
+    for copy in copies:
+        copy.wait()
+
+
+def stack_strips(p, parts):
+    return pl.pallas_call(
+        stack_kernel,
+        out_shape=jax.ShapeDtypeStruct((CHIPS, BLOCK, STRIP), jnp.bfloat16),
+        in_specs=[pl.BlockSpec(memory_space=pltpu.SMEM)]
+        + [pl.BlockSpec(memory_space=pl.ANY)] * CHIPS,
+        out_specs=pl.BlockSpec(memory_space=pl.ANY),
+        scratch_shapes=[pltpu.SemaphoreType.DMA((CHIPS,))],
+        compiler_params=pltpu.CompilerParams(**PARAMS),
+        name="stack_strips",
+    )(p, *parts)
+
+
+def poly_kernel(
+    s_ref, a_ref, b_ref, own_ref, other_ref, far_ref, near_ref, gram, poly
+):
+    for i in range(CHIPS):
+        lo = BLOCK * i
+        gram[lo : lo + BLOCK, lo : lo + STRIP] = a_ref[i]
+        gram[lo + BLOCK : lo + 1024, lo : lo + BLOCK] = a_ref[i][:, BLOCK:1024].T
+        rows = slice(1024 + lo, 1024 + lo + BLOCK)
+        left = 1024 - lo
+        gram[rows, 1024 + lo : 2048] = b_ref[i][:, :left]
+        gram[rows, 0 : BLOCK + lo] = b_ref[i][:, left:]
+        if left > BLOCK:
+            gram[1024 + lo + BLOCK : 2048, rows] = b_ref[i][:, BLOCK:left].T
+        if i:
+            gram[0:lo, rows] = b_ref[i][:, left:1024].T
+    core = s_ref[1]
+    for out, place in ((far_ref, s_ref[2]), (near_ref, s_ref[3])):
+        for half, (panel, sub) in enumerate(((own_ref, core), (other_ref, 1 - core))):
+            start = pl.multiple_of(place * 256, 256)
+            rows = gram[pl.ds(1024 * half + start, 256), :]
+            for n in range(0, 2048, 512):
+                square = jnp.dot(rows, gram[:, n : n + 512], preferred_element_type=jnp.float32)
+                poly[:, n : n + 512] = (
+                    cubic_coef * rows[:, n : n + 512].astype(jnp.float32) + quintic_coef * square
+                ).astype(jnp.bfloat16)
+            mixed = jnp.dot(poly[:, :1024], own_ref[...], preferred_element_type=jnp.float32)
+            mixed += jnp.dot(poly[:, 1024:], other_ref[...], preferred_element_type=jnp.float32)
+            result = linear_coef * panel[pl.ds(start, 256), :].astype(jnp.float32) + mixed
+            result = result.astype(jnp.bfloat16).reshape(8, 1, 32, result.shape[-1])
+            out[:, pl.ds(sub, 1)] = result
+
+
+def poly_rows(scalars, strips, strips_other, own, other):
+    width = own.shape[-1]
+    piece = jax.ShapeDtypeStruct((8, 2, 32, width), jnp.bfloat16)
+    return pl.pallas_call(
+        poly_kernel,
+        out_shape=[piece, piece],
+        in_specs=[pl.BlockSpec(memory_space=pltpu.SMEM)]
+        + [pl.BlockSpec(memory_space=pltpu.VMEM)] * 4,
+        out_specs=[pl.BlockSpec(memory_space=pltpu.VMEM)] * 2,
+        scratch_shapes=[
+            pltpu.VMEM((2048, 2048), jnp.bfloat16),
+            pltpu.VMEM((256, 2048), jnp.bfloat16),
+        ],
+        compiler_params=pltpu.CompilerParams(**PARAMS),
+        name="poly_rows",
+    )(scalars, strips, strips_other, own, other)
+
+
+def fast_body(iterate):
+    x = iterate[:, 0]
+    mats, rows, cols = x.shape
+    m, r, c = (lax.axis_index(axis) for axis in AXES)
+    q, b = r // 2, r % 2
+    scalars = jnp.stack([2 * m + b, c, 2 * (1 - q) + c, 2 * q + c]).astype(jnp.int32)
+    pieces = cut(x).reshape(32, rows // 2, cols // CHIPS)
+    own = lax.all_to_all(pieces, ("gr", "mat", "gc"), 0, 0, tiled=True)
+    own = own.reshape(1024, cols // CHIPS)
+    other = send(own, other_core)
+    parts = gram_strips(scalars, own, other)
+    parts = [parts[0]] + [send(parts[d], across(d)) for d in range(1, CHIPS)]
+    strip = add_strips(parts, 1.0 / cols)
+    strips = stack_strips(scalars, [strip] + [send(strip, across(d)) for d in range(1, CHIPS)])
+    strips_other = send(strips, other_core)
+    far, near = poly_rows(scalars, strips, strips_other, own, other)
+    far = send(far, lambda m, r, c: (m, (1 - r // 2) * 2 + c, r % 2))
+    near = send(near, lambda m, r, c: (m, (r // 2) * 2 + c, r % 2))
+    far, near = (v.reshape(1, 512, cols // CHIPS) for v in (far, near))
+    first, second = lax.cond(q == 0, lambda: (near, far), lambda: (far, near))
+    return jnp.concatenate([first, second], axis=0)
+
+
 def solution(mesh):
+    fast = tuple(mesh.shape[axis] for axis in AXES) == (4, 4, 2)
     return jax.shard_map(
-        body,
+        fast_body if fast else plain_body,
         mesh=mesh,
         in_specs=(P(None, "gr", ("mat", "gc"), None),),
         out_specs=P(None, "gr", ("mat", "gc")),

time: 447 us -> 205 us (0.46)
  waiting for transfers between devices: 339 us -> 99.7 us
  local copies, waits for them, and re-layouts: 34 us -> 5.12 us
  matrix products: 26.5 us -> 0 us
  Pallas kernels: 0 us -> 25 us
  starting transfers between devices: 0.13 us -> 23.5 us
  blocking collectives: 28.9 us -> 50.2 us
  between operations: 13.2 us -> 0.08 us
    all_gather x3 -> x0, waiting for transfers between devices: 214 us -> none  [the longest x1 132 us: body(): panel_rows = lax.all_gather(row_block, 'gr', axis=1, tiled=True)]
    psum x1 -> x0, waiting for transfers between devices: 125 us -> none  [body(): lax.psum(partial_value, ('mat', 'gc')) * inv_cols]
    ppermute x0 -> x18, waiting for transfers between devices: none -> 99.7 us  [send(): return lax.ppermute(value, AXES, perm)]
    dot_general x3 -> x0, matrix products: 26.5 us -> none  [the longest x1 11.4 us: body(): jnp.einsum('irc,ijc->irj', row_block, panel_rows, preferred_element_type=...]
    pallas_call x0 -> x5, Pallas kernels: none -> 25 us  [the longest x1 18.3 us: poly_rows(): pl.pallas_call(poly_kernel, out_shape=[piece, piece], in_specs=[pl.BlockS...]
    ppermute x0 -> x18, starting transfers between devices: none -> 23.5 us  [send(): return lax.ppermute(value, AXES, perm)]
    all_to_all x1, blocking collectives: 28.9 us -> 50.2 us  [fast_body(): own = lax.all_to_all(pieces, ('gr', 'mat', 'gc'), 0, 0, tiled=True)]
    unnamed x7 -> x6, local copies, waits for them, and re-layouts: 23.7 us -> 2.95 us
  transfers between devices with their start and end apart: 4 -> 18, of which waited for: 4 -> 12; matrix products, arithmetic and copies ran while one was open for 0% -> 0% of each run, Pallas kernels for 0% -> 0%
where the time goes in v1:
time: 205 us
  waiting for transfers between devices  99.7 us (49%)
  blocking collectives  50.2 us (24%)
  Pallas kernels  25 us (12%)
  starting transfers between devices  23.5 us (11%)
  local copies, waits for them, and re-layouts  5.12 us (2%)
    ppermute x18, waiting for transfers between devices, send(): return lax.ppermute(value, AXES, perm)  99.7 us
    all_to_all x1, blocking collectives, fast_body(): own = lax.all_to_all(pieces, ('gr', 'mat', 'gc'), 0, 0, tiled=True)  50.2 us
    ppermute x18, starting transfers between devices, send(): return lax.ppermute(value, AXES, perm)  23.5 us
    pallas_call x1, Pallas kernels, poly_rows(): pl.pallas_call(poly_kernel, out_shape=[piece, piece], in_specs=[pl.BlockS...  18.3 us
    pallas_call x1, Pallas kernels, gram_strips(): pl.pallas_call(gram_kernel, out_shape=[jax.ShapeDtypeStruct((BLOCK, STRIP...  4.58 us
  transfers between devices with their start and end apart: 18, of which 12 were waited for; matrix products, arithmetic and copies ran while one was open for 0% of the time, Pallas kernels for 0%

profile of v1, /device:TPU:0, one launch (start us, length us, event | category | flops | bytes accessed | tf_op | source)
XLA Modules:
  0.0 205.1 jit_solution(4953521282652430565)
XLA Ops:
  0.0 1.5 copy-done.1
  2.0 50.2 %all_to_all.5 = bf16[32,32,896]{2,1,0:T(8,128)(2,1)S(1)} all-to-all(bf16[32,32,896]{2,1,0:T(8,128)(2,1)S(1)} %bitcast.12), channel_id=1, replica_groups=mesh['mat'=4,'gr'=4,'gc'=2] {'gr','mat','gc'}, dimensions={0} | all-to-all | bytes 3670016 | tf_op jit(solution)/shard_map/all_to_all | solution.py:237
  52.2 3.8 %collective-permute-done.other_ref = bf16[1024,896]{1,0:T(8,128)(2,1)} collective-permute-done((bf16[1024,896]{1,0:T(8,128)(2,1)S(1)}, bf16[1024,896]{1,0:T(8,128)(2,1)}, u32[]{:S(2)}, u32[]{:S(2)}) %collective-permute-start) | collective-permute-done | bytes 1835040 | tf_op jit(solution)/shard_map/ppermute | solution.py:64
  56.1 4.6 %gram_strips.1 = (bf16[128,1152]{1,0:T(8,128)(2,1)S(1)}, bf16[128,1152]{1,0:T(8,128)(2,1)S(1)}, bf16[128,1152]{1,0:T(8,128)(2,1)S(1)}, bf16[128,1152]{1,0:T(8,12...) custom-call(s32[4]{0:T(128)S(1)} %pad_add_fusion.p_ref.s_ref, ...), custom_call_target="tpu_custom_call" | custom-call | tf_op jit(solution)/shard_map/gram_strips/pallas_call | solution.py:125
  60.7 1.4 collective-permute-start.1
  64.2 1.5 collective-permute-start.4
  67.0 3.5 %collective-permute-done.1.refs_1_ = bf16[128,1152]{1,0:T(8,128)(2,1)S(1)} collective-permute-done((bf16[128,1152]{1,0:T(8,128)(2,1)S(1)}, bf16[128,1152]{1,0:T(8,128)(2,1)S(1)}, u32[]{:S(2)}, u32[]{:S(2)}) %collective-permute-start.1) | collective-permute-done | bytes 294944 | tf_op jit(solution)/shard_map/ppermute | solution.py:64
  70.6 2.4 %collective-permute-start.6 = (bf16[128,1152]{1,0:T(8,128)(2,1)S(1)}, bf16[128,1152]{1,0:T(8,128)(2,1)S(1)}, u32[]{:S(2)}, u32[]{:S(2)}) collective-permute-start(bf16[128,1152]{1,0:T(8,128)(2,1)S(1)} %get-tuple-element.31), channel_id=1, source_target_pairs={{0,24},{1,25},{2,26},{3,27},{4,28},{5,29},{6,30},{7,31},{8,16},{9,... | collective-permute-start | bytes 884744 | tf_op jit(solution)/shard_map/ppermute | solution.py:64
  73.0 3.5 %collective-permute-done.2.refs_2_ = bf16[128,1152]{1,0:T(8,128)(2,1)S(1)} collective-permute-done((bf16[128,1152]{1,0:T(8,128)(2,1)S(1)}, bf16[128,1152]{1,0:T(8,128)(2,1)S(1)}, u32[]{:S(2)}, u32[]{:S(2)}) %collective-permute-start.2) | collective-permute-done | bytes 294944 | tf_op jit(solution)/shard_map/ppermute | solution.py:64
  76.5 3.9 %collective-permute-start.7 = (bf16[128,1152]{1,0:T(8,128)(2,1)S(1)}, bf16[128,1152]{1,0:T(8,128)(2,1)S(1)}, u32[]{:S(2)}, u32[]{:S(2)}) collective-permute-start(bf16[128,1152]{1,0:T(8,128)(2,1)S(1)} %get-tuple-element.32), channel_id=1, source_target_pairs={{0,26},{1,27},{2,24},{3,25},{4,30},{5,31},{6,28},{7,29},{8,18},{9,... | collective-permute-start | bytes 884744 | tf_op jit(solution)/shard_map/ppermute | solution.py:64
  80.4 8.3 %collective-permute-done.5.refs_5_ = bf16[128,1152]{1,0:T(8,128)(2,1)S(1)} collective-permute-done((bf16[128,1152]{1,0:T(8,128)(2,1)S(1)}, bf16[128,1152]{1,0:T(8,128)(2,1)S(1)}, u32[]{:S(2)}, u32[]{:S(2)}) %collective-permute-start.5) | collective-permute-done | bytes 294944 | tf_op jit(solution)/shard_map/ppermute | solution.py:64
  88.6 7.0 %collective-permute-done.6.refs_6_ = bf16[128,1152]{1,0:T(8,128)(2,1)S(1)} collective-permute-done((bf16[128,1152]{1,0:T(8,128)(2,1)S(1)}, bf16[128,1152]{1,0:T(8,128)(2,1)S(1)}, u32[]{:S(2)}, u32[]{:S(2)}) %collective-permute-start.6) | collective-permute-done | bytes 294944 | tf_op jit(solution)/shard_map/ppermute | solution.py:64
  96.0 2.1 %collective-permute-start.14 = (bf16[128,1152]{1,0:T(8,128)(2,1)S(1)}, bf16[128,1152]{1,0:T(8,128)(2,1)S(1)}, u32[]{:S(2)}, u32[]{:S(2)}) collective-permute-start(bf16[128,1152]{1,0:T(8,128)(2,1)S(1)} %add_strips.1.refs_0_), channel_id=1, source_target_pairs={{0,26},{1,27},{2,24},{3,25},{4,30},{5,31},{6,28},{7,29},{8,18},{9,... | collective-permute-start | bytes 884744 | tf_op jit(solution)/shard_map/ppermute | solution.py:64
  98.1 1.4 collective-permute-start.13
  101.9 1.5 collective-permute-start.10
  103.4 5.3 %collective-permute-done.14.refs_7_ = bf16[128,1152]{1,0:T(8,128)(2,1)S(1)} collective-permute-done((bf16[128,1152]{1,0:T(8,128)(2,1)S(1)}, bf16[128,1152]{1,0:T(8,128)(2,1)S(1)}, u32[]{:S(2)}, u32[]{:S(2)}) %collective-permute-start.14) | collective-permute-done | bytes 294944 | tf_op jit(solution)/shard_map/ppermute | solution.py:64
  109.9 14.1 %collective-permute-done.13.refs_6_ = bf16[128,1152]{1,0:T(8,128)(2,1)S(1)} collective-permute-done((bf16[128,1152]{1,0:T(8,128)(2,1)S(1)}, bf16[128,1152]{1,0:T(8,128)(2,1)S(1)}, u32[]{:S(2)}, u32[]{:S(2)}) %collective-permute-start.13) | collective-permute-done | bytes 294944 | tf_op jit(solution)/shard_map/ppermute | solution.py:64
  125.7 4.3 %collective-permute-done.9.refs_2_ = bf16[128,1152]{1,0:T(8,128)(2,1)S(1)} collective-permute-done((bf16[128,1152]{1,0:T(8,128)(2,1)S(1)}, bf16[128,1152]{1,0:T(8,128)(2,1)S(1)}, u32[]{:S(2)}, u32[]{:S(2)}) %collective-permute-start.9) | collective-permute-done | bytes 294944 | tf_op jit(solution)/shard_map/ppermute | solution.py:64
  130.0 2.9 %collective-permute-done.8.refs_1_ = bf16[128,1152]{1,0:T(8,128)(2,1)S(1)} collective-permute-done((bf16[128,1152]{1,0:T(8,128)(2,1)S(1)}, bf16[128,1152]{1,0:T(8,128)(2,1)S(1)}, u32[]{:S(2)}, u32[]{:S(2)}) %collective-permute-start.8) | collective-permute-done | bytes 294944 | tf_op jit(solution)/shard_map/ppermute | solution.py:64
  134.3 4.5 %collective-permute-done.15.b_ref = bf16[8,128,1152]{2,1,0:T(8,128)(2,1)S(1)} collective-permute-done((bf16[8,128,1152]{2,1,0:T(8,128)(2,1)S(1)}, bf16[8,128,1152]{2,1,0:T(8,128)(2,1)S(1)}, u32[]{:S(2)}, u32[]{:S(2)}) %collective-permute-start.15) | collective-permute-done | bytes 2359328 | tf_op jit(solution)/shard_map/ppermute | solution.py:64
  138.8 1.4 copy-done.5
  140.2 18.3 %poly_rows.1 = (bf16[8,2,32,896]{3,2,1,0:T(8,128)(2,1)}, bf16[8,2,32,896]{3,2,1,0:T(8,128)(2,1)S(1)}) custom-call(s32[4]{0:T(128)S(1)} %pad_add_fusion.p_ref.s_ref, bf16[8,128,1152]{2,1,0:T(8,128)(2,1)} %copy-done, bf16[8,128,1152]{2,1,0:T(8,128)(2,1)} %copy-done.5, bf16[1024,896]{1,0:T(8,128)(2,1)S(1)} %bitcast.11, ...), custom_call_target="tpu_custom_call" | custom-call | tf_op jit(solution)/shard_map/poly_rows/pallas_call | solution.py:215
  159.8 41.7 %collective-permute-done.16 = bf16[8,2,32,896]{3,2,1,0:T(8,128)(2,1)S(1)} collective-permute-done((bf16[8,2,32,896]{3,2,1,0:T(8,128)(2,1)}, bf16[8,2,32,896]{3,2,1,0:T(8,128)(2,1)S(1)}, u32[]{:S(2)}, u32[]{:S(2)}) %collective-permute-start.16) | collective-permute-done | bytes 917536 | tf_op jit(solution)/shard_map/ppermute | solution.py:64
  201.5 2.2 %conditional.1 = (bf16[1,512,896]{2,1,0:T(8,128)(2,1)S(1)}, bf16[1,512,896]{2,1,0:T(8,128)(2,1)S(1)}) conditional(s32[]{:T(128)} %convert_element_type.3, (bf16[1,512,896]{2,1,0:T(8,128)(2,1)S(1)}, bf16[1,512,896]{2,1,0:T(8,128)(2,1)S(1)}) %tuple.17, (bf16[1,512,896]{2,1,0:T(8,128)(2,1)S(1)}, bf16[1,512,896]{2,1,0:T(8,128)(2,1)S(1)}) %tuple.18), branch_computations={%region_0.1_spmd, %region_1.2_spmd} | conditional | bytes 11010120 | solution.py:249
  (33 shorter events, 15.7 us)
Async XLA Ops:
  0.0 1.5 copy-start.1
  52.2 3.9 %collective-permute-start = (bf16[1024,896]{1,0:T(8,128)(2,1)S(1)}, bf16[1024,896]{1,0:T(8,128)(2,1)}, u32[]{:S(2)}, u32[]{:S(2)}) collective-permute-start(bf16[1024,896]{1,0:T(8,128)(2,1)S(1)} %bitcast.9), channel_id=1, source_target_pairs={{0,1},{1,0},{2,3},{3,2},{4,5},{5,4},{6,7},{7,6},{8,9},{9,8},{10,11... | collective-permute-start | bytes 5505032 | tf_op jit(solution)/shard_map/ppermute | solution.py:64
  60.7 9.9 %collective-permute-start.1 = (bf16[128,1152]{1,0:T(8,128)(2,1)S(1)}, bf16[128,1152]{1,0:T(8,128)(2,1)S(1)}, u32[]{:S(2)}, u32[]{:S(2)}) collective-permute-start(bf16[128,1152]{1,0:T(8,128)(2,1)S(1)} %get-tuple-element.26), channel_id=1, source_target_pairs={{0,2},{1,3},{2,0},{3,1},{4,6},{5,7},{6,4},{7,5},{8,10},{9,11},{10,... | collective-permute-start | bytes 884744 | tf_op jit(solution)/shard_map/ppermute | solution.py:64
  62.1 14.4 %collective-permute-start.2 = (bf16[128,1152]{1,0:T(8,128)(2,1)S(1)}, bf16[128,1152]{1,0:T(8,128)(2,1)S(1)}, u32[]{:S(2)}, u32[]{:S(2)}) collective-permute-start(bf16[128,1152]{1,0:T(8,128)(2,1)S(1)} %get-tuple-element.27), channel_id=1, source_target_pairs={{0,8},{1,9},{2,10},{3,11},{4,12},{5,13},{6,14},{7,15},{8,0},{9,1},... | collective-permute-start | bytes 884744 | tf_op jit(solution)/shard_map/ppermute | solution.py:64
  62.9 17.5 %collective-permute-start.3 = (bf16[128,1152]{1,0:T(8,128)(2,1)S(1)}, bf16[128,1152]{1,0:T(8,128)(2,1)S(1)}, u32[]{:S(2)}, u32[]{:S(2)}) collective-permute-start(bf16[128,1152]{1,0:T(8,128)(2,1)S(1)} %get-tuple-element.28), channel_id=1, source_target_pairs={{0,10},{1,11},{2,8},{3,9},{4,14},{5,15},{6,12},{7,13},{8,2},{9,3},... | collective-permute-start | bytes 884744 | tf_op jit(solution)/shard_map/ppermute | solution.py:64
  64.2 16.1 %collective-permute-start.4 = (bf16[128,1152]{1,0:T(8,128)(2,1)S(1)}, bf16[128,1152]{1,0:T(8,128)(2,1)S(1)}, u32[]{:S(2)}, u32[]{:S(2)}) collective-permute-start(bf16[128,1152]{1,0:T(8,128)(2,1)S(1)} %get-tuple-element.29), channel_id=1, source_target_pairs={{0,16},{1,17},{2,18},{3,19},{4,20},{5,21},{6,22},{7,23},{8,24},{9,... | collective-permute-start | bytes 884744 | tf_op jit(solution)/shard_map/ppermute | solution.py:64
  65.7 22.9 %collective-permute-start.5 = (bf16[128,1152]{1,0:T(8,128)(2,1)S(1)}, bf16[128,1152]{1,0:T(8,128)(2,1)S(1)}, u32[]{:S(2)}, u32[]{:S(2)}) collective-permute-start(bf16[128,1152]{1,0:T(8,128)(2,1)S(1)} %get-tuple-element.30), channel_id=1, source_target_pairs={{0,18},{1,19},{2,16},{3,17},{4,22},{5,23},{6,20},{7,21},{8,26},{9,... | collective-permute-start | bytes 884744 | tf_op jit(solution)/shard_map/ppermute | solution.py:64
  70.6 25.0 %collective-permute-start.6 = (bf16[128,1152]{1,0:T(8,128)(2,1)S(1)}, bf16[128,1152]{1,0:T(8,128)(2,1)S(1)}, u32[]{:S(2)}, u32[]{:S(2)}) collective-permute-start(bf16[128,1152]{1,0:T(8,128)(2,1)S(1)} %get-tuple-element.31), channel_id=1, source_target_pairs={{0,24},{1,25},{2,26},{3,27},{4,28},{5,29},{6,30},{7,31},{8,16},{9,... | collective-permute-start | bytes 884744 | tf_op jit(solution)/shard_map/ppermute | solution.py:64
  76.5 19.2 %collective-permute-start.7 = (bf16[128,1152]{1,0:T(8,128)(2,1)S(1)}, bf16[128,1152]{1,0:T(8,128)(2,1)S(1)}, u32[]{:S(2)}, u32[]{:S(2)}) collective-permute-start(bf16[128,1152]{1,0:T(8,128)(2,1)S(1)} %get-tuple-element.32), channel_id=1, source_target_pairs={{0,26},{1,27},{2,24},{3,25},{4,30},{5,31},{6,28},{7,29},{8,18},{9,... | collective-permute-start | bytes 884744 | tf_op jit(solution)/shard_map/ppermute | solution.py:64
  96.0 12.8 %collective-permute-start.14 = (bf16[128,1152]{1,0:T(8,128)(2,1)S(1)}, bf16[128,1152]{1,0:T(8,128)(2,1)S(1)}, u32[]{:S(2)}, u32[]{:S(2)}) collective-permute-start(bf16[128,1152]{1,0:T(8,128)(2,1)S(1)} %add_strips.1.refs_0_), channel_id=1, source_target_pairs={{0,26},{1,27},{2,24},{3,25},{4,30},{5,31},{6,28},{7,29},{8,18},{9,... | collective-permute-start | bytes 884744 | tf_op jit(solution)/shard_map/ppermute | solution.py:64
  98.1 26.0 %collective-permute-start.13 = (bf16[128,1152]{1,0:T(8,128)(2,1)S(1)}, bf16[128,1152]{1,0:T(8,128)(2,1)S(1)}, u32[]{:S(2)}, u32[]{:S(2)}) collective-permute-start(bf16[128,1152]{1,0:T(8,128)(2,1)S(1)} %add_strips.1.refs_0_), channel_id=1, source_target_pairs={{0,24},{1,25},{2,26},{3,27},{4,28},{5,29},{6,30},{7,31},{8,16},{9,... | collective-permute-start | bytes 884744 | tf_op jit(solution)/shard_map/ppermute | solution.py:64
  99.5 25.5 %collective-permute-start.12 = (bf16[128,1152]{1,0:T(8,128)(2,1)S(1)}, bf16[128,1152]{1,0:T(8,128)(2,1)S(1)}, u32[]{:S(2)}, u32[]{:S(2)}) collective-permute-start(bf16[128,1152]{1,0:T(8,128)(2,1)S(1)} %add_strips.1.refs_0_), channel_id=1, source_target_pairs={{0,18},{1,19},{2,16},{3,17},{4,22},{5,23},{6,20},{7,21},{8,26},{9,... | collective-permute-start | bytes 884744 | tf_op jit(solution)/shard_map/ppermute | solution.py:64
  100.5 25.2 %collective-permute-start.11 = (bf16[128,1152]{1,0:T(8,128)(2,1)S(1)}, bf16[128,1152]{1,0:T(8,128)(2,1)S(1)}, u32[]{:S(2)}, u32[]{:S(2)}) collective-permute-start(bf16[128,1152]{1,0:T(8,128)(2,1)S(1)} %add_strips.1.refs_0_), channel_id=1, source_target_pairs={{0,16},{1,17},{2,18},{3,19},{4,20},{5,21},{6,22},{7,23},{8,24},{9,... | collective-permute-start | bytes 884744 | tf_op jit(solution)/shard_map/ppermute | solution.py:64
  101.9 23.8 %collective-permute-start.10 = (bf16[128,1152]{1,0:T(8,128)(2,1)S(1)}, bf16[128,1152]{1,0:T(8,128)(2,1)S(1)}, u32[]{:S(2)}, u32[]{:S(2)}) collective-permute-start(bf16[128,1152]{1,0:T(8,128)(2,1)S(1)} %add_strips.1.refs_0_), channel_id=1, source_target_pairs={{0,10},{1,11},{2,8},{3,9},{4,14},{5,15},{6,12},{7,13},{8,2},{9,3},... | collective-permute-start | bytes 884744 | tf_op jit(solution)/shard_map/ppermute | solution.py:64
  108.7 21.3 %collective-permute-start.9 = (bf16[128,1152]{1,0:T(8,128)(2,1)S(1)}, bf16[128,1152]{1,0:T(8,128)(2,1)S(1)}, u32[]{:S(2)}, u32[]{:S(2)}) collective-permute-start(bf16[128,1152]{1,0:T(8,128)(2,1)S(1)} %add_strips.1.refs_0_), channel_id=1, source_target_pairs={{0,8},{1,9},{2,10},{3,11},{4,12},{5,13},{6,14},{7,15},{8,0},{9,1},... | collective-permute-start | bytes 884744 | tf_op jit(solution)/shard_map/ppermute | solution.py:64
  124.0 8.8 %collective-permute-start.8 = (bf16[128,1152]{1,0:T(8,128)(2,1)S(1)}, bf16[128,1152]{1,0:T(8,128)(2,1)S(1)}, u32[]{:S(2)}, u32[]{:S(2)}) collective-permute-start(bf16[128,1152]{1,0:T(8,128)(2,1)S(1)} %add_strips.1.refs_0_), channel_id=1, source_target_pairs={{0,2},{1,3},{2,0},{3,1},{4,6},{5,7},{6,4},{7,5},{8,10},{9,11},{10,... | collective-permute-start | bytes 884744 | tf_op jit(solution)/shard_map/ppermute | solution.py:64
  134.2 4.6 %copy-start = (bf16[8,128,1152]{2,1,0:T(8,128)(2,1)}, bf16[8,128,1152]{2,1,0:T(8,128)(2,1)S(1)}, u32[]{:S(2)}) copy-start(bf16[8,128,1152]{2,1,0:T(8,128)(2,1)S(1)} %stack_strips.1.a_ref) | copy-start | bytes 7077892
  134.2 4.6 %collective-permute-start.15 = (bf16[8,128,1152]{2,1,0:T(8,128)(2,1)S(1)}, bf16[8,128,1152]{2,1,0:T(8,128)(2,1)S(1)}, u32[]{:S(2)}, u32[]{:S(2)}) collective-permute-start(bf16[8,128,1152]{2,1,0:T(8,128)(2,1)S(1)} %stack_strips.1.a_ref), channel_id=1, source_target_pairs={{0,1},{1,0},{2,3},{3,2},{4,5},{5,4},{6,7},{7,6},{8,9},{9,8},{10,11... | collective-permute-start | bytes 7077896 | tf_op jit(solution)/shard_map/ppermute | solution.py:64
  138.8 1.4 copy-start.5
  158.5 43.0 %collective-permute-start.16 = (bf16[8,2,32,896]{3,2,1,0:T(8,128)(2,1)}, bf16[8,2,32,896]{3,2,1,0:T(8,128)(2,1)S(1)}, u32[]{:S(2)}, u32[]{:S(2)}) collective-permute-start(bf16[8,2,32,896]{3,2,1,0:T(8,128)(2,1)} %get-tuple-element.33), channel_id=1, source_target_pairs={{0,4},{1,6},{2,5},{3,7},{4,0},{5,2},{6,1},{7,3},{8,12},{9,14},{10,... | collective-permute-start | bytes 2752520 | tf_op jit(solution)/shard_map/ppermute | solution.py:64
  159.1 42.4 %collective-permute-start.17 = (bf16[8,2,32,896]{3,2,1,0:T(8,128)(2,1)S(1)}, bf16[8,2,32,896]{3,2,1,0:T(8,128)(2,1)S(1)}, u32[]{:S(2)}, u32[]{:S(2)}) collective-permute-start(bf16[8,2,32,896]{3,2,1,0:T(8,128)(2,1)S(1)} %get-tuple-element.34), channel_id=1, source_target_pairs={{0,0},{1,2},{2,1},{3,3},{4,4},{5,6},{6,5},{7,7},{8,8},{9,10},{10,9... | collective-permute-start | bytes 2752520 | tf_op jit(solution)/shard_map/ppermute | solution.py:64
  201.5 0.9 copy-start.3
  202.4 1.2 copy-start.4

commit v2 on v1

v2 whole, which is shorter than its diff:
```python
import functools

import jax
import jax.numpy as jnp
from jax import lax
from jax.experimental import pallas as pl
from jax.experimental.pallas import tpu as pltpu
from jax.sharding import PartitionSpec as P

linear_coef = 3.4445
cubic_coef = -4.775
quintic_coef = 2.0315

AXES = ("mat", "gr", "gc")


def plain_body(iterate):
    regrouped = lax.all_to_all(iterate, ("mat", "gc"), split_axis=3, concat_axis=2, tiled=True)
    row_block = regrouped[:, 0]
    panel_rows = lax.all_gather(row_block, "gr", axis=1, tiled=True)
    total_rows = panel_rows.shape[1]
    groups = lax.axis_size(("mat", "gc"))
    gram_width = total_rows // groups
    inv_cols = 1.0 / iterate.shape[-1]
    partial_value = jnp.einsum(
        "irc,ijc->irj", row_block, panel_rows, preferred_element_type=jnp.float32
    )
    gram_rows = (lax.psum(partial_value, ("mat", "gc")) * inv_cols).astype(jnp.bfloat16)
    own_block = lax.dynamic_slice_in_dim(
        gram_rows, lax.axis_index(("mat", "gc")) * gram_width, gram_width, 2
    )
    square = jnp.einsum(
        "irk,ikj->irj",
        gram_rows,
        lax.all_gather(own_block, "gr", axis=1, tiled=True),
        preferred_element_type=jnp.float32,
    )
    poly_block = (cubic_coef * own_block.astype(jnp.float32) + quintic_coef * square).astype(
        jnp.bfloat16
    )
    mixed_sum = jnp.einsum(
        "irk,ikc->irc",
        lax.all_gather(poly_block, ("mat", "gc"), axis=2, tiled=True),
        panel_rows,
        preferred_element_type=jnp.float32,
    )
    result = linear_coef * row_block.astype(jnp.float32) + mixed_sum
    return result.astype(jnp.bfloat16)


CHIPS = 8
BLOCK = 128
STRIP = 9 * BLOCK
THIRD = STRIP // 3
ORDERS = ((2, 4, 1), (4, 1, 2), (1, 2, 4))
PARAMS = dict(vmem_limit_bytes=28 * 1024 * 1024)


def cost(flops, bytes_accessed):
    return pl.CostEstimate(flops=flops, bytes_accessed=bytes_accessed, transcendentals=0)


def offset(third, place):
    axes = ORDERS[third]
    return sum(axes[k] for k in range(3) if place >> (2 - k) & 1)


def send(value, move):
    perm = []
    for m in range(4):
        for r in range(4):
            for c in range(2):
                to = move(m, r, c)
                perm.append((m * 8 + r * 2 + c, to[0] * 8 + to[1] * 2 + to[2]))
    return lax.ppermute(value, AXES, perm)


def across(d):
    return lambda m, r, c: (m ^ (d >> 1), r ^ (d & 1), c)


def other_core(m, r, c):
    return m, r, 1 - c


def cut_kernel(x_ref, o_ref, sems):
    copies = []
    width = o_ref.shape[-1]
    for q in range(2):
        for k in range(CHIPS):
            copies.append(
                pltpu.make_async_copy(
                    x_ref.at[q, :, pl.ds(k * width, width)],
                    o_ref.at[q, k % 2, k // 2],
                    sems.at[q * CHIPS + k],
                )
            )
    for copy in copies:
        copy.start()
    for copy in copies:
        copy.wait()


def cut(x):
    _, rows, cols = x.shape
    return pl.pallas_call(
        cut_kernel,
        out_shape=jax.ShapeDtypeStruct((2, 2, 4, rows, cols // CHIPS), x.dtype),
        in_specs=[pl.BlockSpec(memory_space=pl.ANY)],
        out_specs=pl.BlockSpec(memory_space=pl.ANY),
        scratch_shapes=[pltpu.SemaphoreType.DMA((16,))],
        compiler_params=pltpu.CompilerParams(**PARAMS),
        name="cut_columns",
    )(x)


def gram_kernel(p_ref, own_ref, other_ref, *rest):
    keep, away, strips = rest[:3], rest[3:6], rest[6]
    dims = (((1,), (1,)), ((), ()))
    for t in range(4):
        lo = 256 * t
        rows = own_ref[lo : lo + 256, :]
        mine = lax.dot_general(rows, own_ref[lo:1024, :], dims, preferred_element_type=jnp.float32)
        theirs = lax.dot_general(
            rows, other_ref[0 : lo + 256, :], dims, preferred_element_type=jnp.float32
        )
        both = jnp.concatenate([mine, theirs], axis=1)
        strips[2 * t] = both[:128, :STRIP]
        strips[2 * t + 1] = both[128:, 128 : 128 + STRIP]
    p = p_ref[0]
    for i in range(3):
        cols = slice(THIRD * i, THIRD * (i + 1))
        for place in range(4):
            keep[i][place] = strips[p ^ offset(i, place), :, cols]
            away[i][place] = strips[p ^ offset(i, place + 4), :, cols].astype(jnp.bfloat16)


def gram_strips(p, own, other):
    shape = (4, BLOCK, THIRD)
    return pl.pallas_call(
        gram_kernel,
        out_shape=[jax.ShapeDtypeStruct(shape, jnp.float32)] * 3
        + [jax.ShapeDtypeStruct(shape, jnp.bfloat16)] * 3,
        in_specs=[pl.BlockSpec(memory_space=pltpu.SMEM)]
        + [pl.BlockSpec(memory_space=pltpu.VMEM)] * 2,
        out_specs=[pl.BlockSpec(memory_space=pltpu.VMEM)] * 6,
        scratch_shapes=[pltpu.VMEM((CHIPS, BLOCK, STRIP), jnp.float32)],
        compiler_params=pltpu.CompilerParams(**PARAMS),
        cost_estimate=cost(2 * 1024 * 1280 * own.shape[-1], 10**7),
        name="gram_strips",
    )(p, own, other)


def halves_kernel(*refs):
    held, came, keep, away = (refs[3 * k : 3 * k + 3] for k in range(4))
    for i in range(3):
        half = keep[i].shape[0]
        total = held[i][...] + came[i][...].astype(jnp.float32)
        keep[i][...] = total[:half]
        away[i][...] = total[half:].astype(jnp.bfloat16)


def pairs_kernel(*refs):
    held, came, keep, away = (refs[3 * k : 3 * k + 3] for k in range(4))
    for i in range(3):
        total = held[i][...] + came[i][...].astype(jnp.float32)
        keep[i][...] = total
        away[i][0] = total[1].astype(jnp.bfloat16)
        away[i][1] = total[0].astype(jnp.bfloat16)


def add_step(kernel, name, held, came, count):
    shape = (count, BLOCK, THIRD)
    made = pl.pallas_call(
        kernel,
        out_shape=[jax.ShapeDtypeStruct(shape, jnp.float32)] * 3
        + [jax.ShapeDtypeStruct(shape, jnp.bfloat16)] * 3,
        in_specs=[pl.BlockSpec(memory_space=pltpu.VMEM)] * 6,
        out_specs=[pl.BlockSpec(memory_space=pltpu.VMEM)] * 6,
        compiler_params=pltpu.CompilerParams(**PARAMS),
        name=name,
    )(*held, *came)
    return made[:3], made[3:]


def add_halves(held, came):
    return add_step(halves_kernel, "add_halves", held, came, 2)


def add_pairs(held, came):
    return add_step(pairs_kernel, "add_pairs", held, came, 2)


def last_kernel(scale, *refs):
    held, came, outs = refs[:3], refs[3:6], refs[6:]
    for i in range(3):
        total = held[i][...] + came[i][...].astype(jnp.float32)
        outs[i][...] = (total * scale).astype(jnp.bfloat16)


def add_last(held, came, scale):
    return pl.pallas_call(
        functools.partial(last_kernel, scale),
        out_shape=[jax.ShapeDtypeStruct(held[0].shape, jnp.bfloat16)] * 3,
        in_specs=[pl.BlockSpec(memory_space=pltpu.VMEM)] * 6,
        out_specs=[pl.BlockSpec(memory_space=pltpu.VMEM)] * 3,
        compiler_params=pltpu.CompilerParams(**PARAMS),
        name="add_last",
    )(*held, *came)


def sum_strips(keep, away, scale):
    came = [send(away[i], across(ORDERS[i][0])) for i in range(3)]
    keep, away = add_halves(keep, came)
    came = [send(away[i], across(ORDERS[i][1])) for i in range(3)]
    keep, away = add_pairs(keep, came)
    came = [send(away[i], across(ORDERS[i][2])) for i in range(3)]
    return add_last(keep, came, scale)


def gather_strips(parts):
    came = [send(parts[i], across(ORDERS[i][1])) for i in range(3)]
    parts = [jnp.concatenate([parts[i], came[i]], axis=0) for i in range(3)]
    late = [send(parts[i], across(ORDERS[i][0])) for i in range(3)]
    early_other = [send(part, other_core) for part in parts]
    late_other = [send(part, other_core) for part in late]
    return parts + late, early_other + late_other


def result_rows(gram, panels, poly, place, half):
    start = pl.multiple_of(place * 256, 256)
    rows = gram[pl.ds(1024 * half + start, 256), :]
    for n in range(0, 2048, 512):
        square = jnp.dot(rows, gram[:, n : n + 512], preferred_element_type=jnp.float32)
        poly[:, n : n + 512] = (
            cubic_coef * rows[:, n : n + 512].astype(jnp.float32) + quintic_coef * square
        ).astype(jnp.bfloat16)
    mixed = jnp.dot(poly[:, :1024], panels[0][...], preferred_element_type=jnp.float32)
    mixed += jnp.dot(poly[:, 1024:], panels[1][...], preferred_element_type=jnp.float32)
    return (linear_coef * panels[half][pl.ds(start, 256), :].astype(jnp.float32) + mixed).astype(
        jnp.bfloat16
    )


def first_kernel(s_ref, *refs):
    thirds, others, panels = refs[:6], refs[6:12], refs[12:14]
    gram, out, own, other, poly = refs[14:]
    p = s_ref[0]
    for i in range(3):
        cols = slice(THIRD * i, THIRD * (i + 1))
        for place in range(CHIPS):
            for strips, source in ((own, thirds), (other, others)):
                strips[p ^ offset(i, place), :, cols] = source[i + 3 * (place // 4)][place % 4]
    for i in range(CHIPS):
        lo = BLOCK * i
        gram[lo : lo + BLOCK, lo : lo + STRIP] = own[i]
        gram[lo + BLOCK : lo + 1024, lo : lo + BLOCK] = own[i][:, BLOCK:1024].T
        rows = slice(1024 + lo, 1024 + lo + BLOCK)
        left = 1024 - lo
        gram[rows, 1024 + lo : 2048] = other[i][:, :left]
        gram[rows, 0 : BLOCK + lo] = other[i][:, left:]
        if left > BLOCK:
            gram[1024 + lo + BLOCK : 2048, rows] = other[i][:, BLOCK:left].T
        if i:
            gram[0:lo, rows] = other[i][:, left:1024].T
    for half in range(2):
        out[256 * half : 256 * (half + 1)] = result_rows(gram, panels, poly, s_ref[1], half)


def first_rows(scalars, thirds, others, panels):
    cols = panels[0].shape[-1]
    return pl.pallas_call(
        first_kernel,
        out_shape=[
            jax.ShapeDtypeStruct((2048, 2048), jnp.bfloat16),
            jax.ShapeDtypeStruct((512, cols), jnp.bfloat16),
        ],
        in_specs=[pl.BlockSpec(memory_space=pltpu.SMEM)]
        + [pl.BlockSpec(memory_space=pltpu.VMEM)] * 14,
        out_specs=[pl.BlockSpec(memory_space=pltpu.VMEM)] * 2,
        scratch_shapes=[pltpu.VMEM((CHIPS, BLOCK, STRIP), jnp.bfloat16)] * 2
        + [pltpu.VMEM((256, 2048), jnp.bfloat16)],
        compiler_params=pltpu.CompilerParams(**PARAMS),
        cost_estimate=cost(2 * 512 * 2048 * (2048 + cols), 3 * 10**7),
        name="first_rows",
    )(scalars, *thirds, *others, *panels)


def near_kernel(s_ref, gram, own, other, out, poly):
    for half in range(2):
        out[256 * half : 256 * (half + 1)] = result_rows(
            gram, (own, other), poly, s_ref[2], half
        )


def near_rows(scalars, gram, panels):
    cols = panels[0].shape[-1]
    return pl.pallas_call(
        near_kernel,
        out_shape=jax.ShapeDtypeStruct((512, cols), jnp.bfloat16),
        in_specs=[pl.BlockSpec(memory_space=pltpu.SMEM)]
        + [pl.BlockSpec(memory_space=pltpu.VMEM)] * 3,
        out_specs=pl.BlockSpec(memory_space=pltpu.VMEM),
        scratch_shapes=[pltpu.VMEM((256, 2048), jnp.bfloat16)],
        cost_estimate=cost(2 * 512 * 2048 * (2048 + cols), 10**7),
        compiler_params=pltpu.CompilerParams(**PARAMS),
        name="near_rows",
    )(scalars, gram, *panels)


def place_kernel(far, s_ref, piece, *rest):
    out, sems = rest[-2:]
    matrix = 1 - s_ref[3] if far else s_ref[3]
    copies = [
        pltpu.make_async_copy(piece.at[0], out.at[matrix, :, s_ref[4]], sems.at[0]),
        pltpu.make_async_copy(piece.at[1], out.at[matrix, :, 1 - s_ref[4]], sems.at[1]),
    ]
    for copy in copies:
        copy.start()
    for copy in copies:
        copy.wait()


def place_rows(far, scalars, piece, *into):
    _, groups, rows, cols = piece.shape
    return pl.pallas_call(
        functools.partial(place_kernel, far),
        out_shape=jax.ShapeDtypeStruct((2, groups, 2, rows, cols), jnp.bfloat16),
        in_specs=[pl.BlockSpec(memory_space=pltpu.SMEM)]
        + [pl.BlockSpec(memory_space=pl.ANY)] * (1 + len(into)),
        out_specs=pl.BlockSpec(memory_space=pl.ANY),
        scratch_shapes=[pltpu.SemaphoreType.DMA((2,))],
        input_output_aliases={2: 0} if into else {},
        compiler_params=pltpu.CompilerParams(**PARAMS),
        name="place_rows",
    )(scalars, piece, *into)


def home_far(m, r, c):
    return m, (1 - r // 2) * 2 + c, r % 2


def home_near(m, r, c):
    return m, (r // 2) * 2 + c, r % 2


def fast_body(iterate):
    x = iterate[:, 0]
    mats, rows, cols = x.shape
    m, r, c = (lax.axis_index(axis) for axis in AXES)
    q, b = r // 2, r % 2
    scalars = jnp.stack([2 * m + b, 2 * (1 - q) + c, 2 * q + c, q, b]).astype(jnp.int32)
    pieces = cut(x).reshape(32, rows // 2, cols // CHIPS)
    own = lax.all_to_all(pieces, ("gr", "mat", "gc"), 0, 0, tiled=True)
    own = own.reshape(1024, cols // CHIPS)
    panels = (own, send(own, other_core))
    made = gram_strips(scalars, *panels)
    thirds, others = gather_strips(sum_strips(made[:3], made[3:], 1.0 / cols))
    gram, far = first_rows(scalars, thirds, others, panels)
    far_home = send(far, home_far)
    near_home = send(near_rows(scalars, gram, panels), home_near)
    shape = (2, 8, 32, cols // CHIPS)
    result = place_rows(True, scalars, far_home.reshape(shape))
    result = place_rows(False, scalars, near_home.reshape(shape), result)
    return result.reshape(mats, 512, cols // CHIPS)


def solution(mesh):
    fast = tuple(mesh.shape[axis] for axis in AXES) == (4, 4, 2)
    return jax.shard_map(
        fast_body if fast else plain_body,
        mesh=mesh,
        in_specs=(P(None, "gr", ("mat", "gc"), None),),
        out_specs=P(None, "gr", ("mat", "gc")),
        check_vma=False,
    )
```

time: 205 us -> 171 us (0.83)
  waiting for transfers between devices: 99.7 us -> 73.7 us
  starting transfers between devices: 23.5 us -> 17.3 us
  local copies, waits for them, and re-layouts: 5.12 us -> 1.74 us
  Pallas kernels: 25 us -> 27.4 us
    ppermute x18 -> x24, waiting for transfers between devices: 99.7 us -> 73.7 us  [send(): return lax.ppermute(value, AXES, perm)]
    ppermute x18 -> x24, starting transfers between devices: 23.5 us -> 17.3 us  [send(): return lax.ppermute(value, AXES, perm)]
    pallas_call x4 -> x8, Pallas kernels: 24.5 us -> 26.9 us  [the longest x1 10.2 us: first_rows(): pl.pallas_call(first_kernel, out_shape=[jax.ShapeDtypeStruct((2048, 2048)...]
    cond x6 -> x0, local copies, waits for them, and re-layouts: 2.17 us -> none
  transfers between devices with their start and end apart: 18 -> 24, of which waited for: 12 -> 18; matrix products, arithmetic and copies ran while one was open for 0% -> 0% of each run, Pallas kernels for 0% -> 6%
where the time goes in v2:
time: 171 us
  waiting for transfers between devices  73.7 us (43%)
  blocking collectives  50.2 us (29%)
  Pallas kernels  27.4 us (16%)
  starting transfers between devices  17.3 us (10%)
  local copies, waits for them, and re-layouts  1.74 us (1%)
    ppermute x24, waiting for transfers between devices, send(): return lax.ppermute(value, AXES, perm)  73.7 us
    all_to_all x1, blocking collectives, fast_body(): own = lax.all_to_all(pieces, ('gr', 'mat', 'gc'), 0, 0, tiled=True)  50.2 us
    ppermute x24, starting transfers between devices, send(): return lax.ppermute(value, AXES, perm)  17.3 us
    pallas_call x1, Pallas kernels, first_rows(): pl.pallas_call(first_kernel, out_shape=[jax.ShapeDtypeStruct((2048, 2048)...  10.2 us
    pallas_call x1, Pallas kernels, near_rows(): pl.pallas_call(near_kernel, out_shape=jax.ShapeDtypeStruct((512, cols), j...  8.54 us
    pallas_call x1, Pallas kernels, gram_strips(): pl.pallas_call(gram_kernel, out_shape=[jax.ShapeDtypeStruct(shape, jnp.fl...  4.69 us
  transfers between devices with their start and end apart: 24, of which 18 were waited for; matrix products, arithmetic and copies ran while one was open for 0% of the time, Pallas kernels for 6%

profile of v2, /device:TPU:0, one launch (start us, length us, event | category | flops | bytes accessed | tf_op | source)
XLA Modules:
  0.0 170.7 jit_solution(1980839601530127900)
XLA Ops:
  0.0 1.5 copy-done
  2.0 50.2 %all_to_all.5 = bf16[32,32,896]{2,1,0:T(8,128)(2,1)S(1)} all-to-all(bf16[32,32,896]{2,1,0:T(8,128)(2,1)S(1)} %bitcast.11), channel_id=1, replica_groups=mesh['mat'=4,'gr'=4,'gc'=2] {'gr','mat','gc'}, dimensions={0} | all-to-all | bytes 3670016 | tf_op jit(solution)/shard_map/all_to_all | solution.py:354
  52.3 3.8 %collective-permute-done.other_ref.refs_13_.other = bf16[1024,896]{1,0:T(8,128)(2,1)} collective-permute-done((bf16[1024,896]{1,0:T(8,128)(2,1)S(1)}, bf16[1024,896]{1,0:T(8,128)(2,1)}, u32[]{:S(2)}, u32[]{:S(2)}) %collective-permute-start) | collective-permute-done | bytes 1835040 | tf_op jit(solution)/shard_map/ppermute | solution.py:75
  56.1 4.7 %gram_strips.1 = (f32[4,128,384]{2,1,0:T(8,128)S(1)}, f32[4,128,384]{2,1,0:T(8,128)S(1)}, f32[4,128,384]{2,1,0:T(8,128)S(1)}, bf16[4,128,384]{2,1,0:T(8,128)(2,1...) custom-call(s32[5]{0:T(128)S(1)} %stack.23.p_ref.s_ref, bf16[1024,896]{1,0:T(8,128)(2,1)S(1)} %bitcast.14, ...), custom_call_target="tpu_custom_call" | custom-call | flops 2348810240 | bytes 10000000 | tf_op jit(solution)/shard_map/gram_strips/pallas_call | solution.py:140
  60.8 1.6 collective-permute-start.1
  62.4 1.4 collective-permute-start.2
  63.8 8.2 %collective-permute-done.1.refs_3_ = bf16[4,128,384]{2,1,0:T(8,128)(2,1)S(1)} collective-permute-done((bf16[4,128,384]{2,1,0:T(8,128)(2,1)S(1)}, bf16[4,128,384]{2,1,0:T(8,128)(2,1)S(1)}, u32[]{:S(2)}, u32[]{:S(2)}) %collective-permute-start.1) | collective-permute-done | bytes 393248 | tf_op jit(solution)/shard_map/ppermute | solution.py:75
  72.0 1.2 collective-permute-done.2.refs_4_
  77.1 3.2 %collective-permute-done.4.refs_3_ = bf16[2,128,384]{2,1,0:T(8,128)(2,1)S(1)} collective-permute-done((bf16[2,128,384]{2,1,0:T(8,128)(2,1)S(1)}, bf16[2,128,384]{2,1,0:T(8,128)(2,1)S(1)}, u32[]{:S(2)}, u32[]{:S(2)}) %collective-permute-start.4) | collective-permute-done | bytes 196640 | tf_op jit(solution)/shard_map/ppermute | solution.py:75
  82.0 1.2 collective-permute-start.7
  83.7 1.5 collective-permute-start.9
  85.2 2.5 %collective-permute-done.7.refs_3_ = bf16[2,128,384]{2,1,0:T(8,128)(2,1)S(1)} collective-permute-done((bf16[2,128,384]{2,1,0:T(8,128)(2,1)S(1)}, bf16[2,128,384]{2,1,0:T(8,128)(2,1)S(1)}, u32[]{:S(2)}, u32[]{:S(2)}) %collective-permute-start.7) | collective-permute-done | bytes 196640 | tf_op jit(solution)/shard_map/ppermute | solution.py:75
  87.7 1.2 collective-permute-done.8.refs_4_
  88.9 2.1 %collective-permute-done.9.refs_5_ = bf16[2,128,384]{2,1,0:T(8,128)(2,1)S(1)} collective-permute-done((bf16[2,128,384]{2,1,0:T(8,128)(2,1)S(1)}, bf16[2,128,384]{2,1,0:T(8,128)(2,1)S(1)}, u32[]{:S(2)}, u32[]{:S(2)}) %collective-permute-start.9) | collective-permute-done | bytes 196640 | tf_op jit(solution)/shard_map/ppermute | solution.py:75
  91.1 1.3 collective-permute-start.10
  92.5 1.3 collective-permute-start.11
  94.3 5.1 %collective-permute-done.12 = bf16[2,128,384]{2,1,0:T(8,128)(2,1)S(1)} collective-permute-done((bf16[2,128,384]{2,1,0:T(8,128)(2,1)S(1)}, bf16[2,128,384]{2,1,0:T(8,128)(2,1)S(1)}, u32[]{:S(2)}, u32[]{:S(2)}) %collective-permute-start.12) | collective-permute-done | bytes 196640 | tf_op jit(solution)/shard_map/ppermute | solution.py:75
  101.3 1.4 collective-permute-start.13
  103.2 7.9 %collective-permute-done.15.refs_5_ = bf16[4,128,384]{2,1,0:T(8,128)(2,1)S(1)} collective-permute-done((bf16[4,128,384]{2,1,0:T(8,128)(2,1)S(1)}, bf16[4,128,384]{2,1,0:T(8,128)(2,1)S(1)}, u32[]{:S(2)}, u32[]{:S(2)}) %collective-permute-start.15) | collective-permute-done | bytes 393248 | tf_op jit(solution)/shard_map/ppermute | solution.py:75
  114.0 10.2 %first_rows.1 = (bf16[2048,2048]{1,0:T(8,128)(2,1)S(1)}, bf16[512,896]{1,0:T(8,128)(2,1)S(1)}) custom-call(s32[5]{0:T(128)S(1)} %stack.23.p_ref.s_ref, bf16[4,128,384]{2,1,0:T(8,128)(2,1)S(1)} %constant_dynamic-update-slice_fusion.refs_0_, bf16[4,128,384]{2,1,0:T(8,128)(2,1)S(1)} %constant_dynamic-update-slice_fusion.2.refs_1_, ...), custom_call_target="tpu_custom_call" | custom-call | flops 6174015488 | bytes 30000000 | tf_op jit(solution)/shard_map/first_rows/pallas_call | solution.py:272
  125.4 8.5 %near_rows.1 = bf16[512,896]{1,0:T(8,128)(2,1)S(1)} custom-call(s32[5]{0:T(128)S(1)} %stack.23.p_ref.s_ref, bf16[2048,2048]{1,0:T(8,128)(2,1)S(1)} %get-tuple-element.49.gram, bf16[1024,896]{1,0:T(8,128)(2,1)S(1)} %bitcast.16, bf16[1024,896]{1,0:T(8,128)(2,1)} %collective-permute-done.other_ref.refs_13_.other), custom_call_target="tpu_custom_call" | custom-call | flops 6174015488 | bytes 10000000 | tf_op jit(solution)/shard_map/near_rows/pallas_call | solution.py:298
  134.6 32.9 %collective-permute-done.23 = bf16[512,896]{1,0:T(8,128)(2,1)S(1)} collective-permute-done((bf16[512,896]{1,0:T(8,128)(2,1)S(1)}, bf16[512,896]{1,0:T(8,128)(2,1)S(1)}, u32[]{:S(2)}, u32[]{:S(2)}) %collective-permute-start.23) | collective-permute-done | bytes 917536 | tf_op jit(solution)/shard_map/ppermute | solution.py:75
  167.5 1.5 place_rows.2.rest_0_
  169.0 1.5 place_rows.3
  (43 shorter events, 14.3 us)
Async XLA Ops:
  52.2 3.9 %collective-permute-start = (bf16[1024,896]{1,0:T(8,128)(2,1)S(1)}, bf16[1024,896]{1,0:T(8,128)(2,1)}, u32[]{:S(2)}, u32[]{:S(2)}) collective-permute-start(bf16[1024,896]{1,0:T(8,128)(2,1)S(1)} %bitcast.13), channel_id=1, source_target_pairs={{0,1},{1,0},{2,3},{3,2},{4,5},{5,4},{6,7},{7,6},{8,9},{9,8},{10,11... | collective-permute-start | bytes 5505032 | tf_op jit(solution)/shard_map/ppermute | solution.py:75
  60.8 11.2 %collective-permute-start.1 = (bf16[4,128,384]{2,1,0:T(8,128)(2,1)S(1)}, bf16[4,128,384]{2,1,0:T(8,128)(2,1)S(1)}, u32[]{:S(2)}, u32[]{:S(2)}) collective-permute-start(bf16[4,128,384]{2,1,0:T(8,128)(2,1)S(1)} %get-tuple-element.31), channel_id=1, source_target_pairs={{0,8},{1,9},{2,10},{3,11},{4,12},{5,13},{6,14},{7,15},{8,0},{9,1},... | collective-permute-start | bytes 1179656 | tf_op jit(solution)/shard_map/ppermute | solution.py:75
  62.4 10.9 %collective-permute-start.2 = (bf16[4,128,384]{2,1,0:T(8,128)(2,1)S(1)}, bf16[4,128,384]{2,1,0:T(8,128)(2,1)S(1)}, u32[]{:S(2)}, u32[]{:S(2)}) collective-permute-start(bf16[4,128,384]{2,1,0:T(8,128)(2,1)S(1)} %get-tuple-element.32), channel_id=1, source_target_pairs={{0,16},{1,17},{2,18},{3,19},{4,20},{5,21},{6,22},{7,23},{8,24},{9,... | collective-permute-start | bytes 1179656 | tf_op jit(solution)/shard_map/ppermute | solution.py:75
  63.8 10.6 %collective-permute-start.3 = (bf16[4,128,384]{2,1,0:T(8,128)(2,1)S(1)}, bf16[4,128,384]{2,1,0:T(8,128)(2,1)S(1)}, u32[]{:S(2)}, u32[]{:S(2)}) collective-permute-start(bf16[4,128,384]{2,1,0:T(8,128)(2,1)S(1)} %get-tuple-element.33), channel_id=1, source_target_pairs={{0,2},{1,3},{2,0},{3,1},{4,6},{5,7},{6,4},{7,5},{8,10},{9,11},{10,... | collective-permute-start | bytes 1179656 | tf_op jit(solution)/shard_map/ppermute | solution.py:75
  74.6 5.7 %collective-permute-start.4 = (bf16[2,128,384]{2,1,0:T(8,128)(2,1)S(1)}, bf16[2,128,384]{2,1,0:T(8,128)(2,1)S(1)}, u32[]{:S(2)}, u32[]{:S(2)}) collective-permute-start(bf16[2,128,384]{2,1,0:T(8,128)(2,1)S(1)} %get-tuple-element.37), channel_id=1, source_target_pairs={{0,16},{1,17},{2,18},{3,19},{4,20},{5,21},{6,22},{7,23},{8,24},{9,... | collective-permute-start | bytes 589832 | tf_op jit(solution)/shard_map/ppermute | solution.py:75
  75.3 5.7 %collective-permute-start.5 = (bf16[2,128,384]{2,1,0:T(8,128)(2,1)S(1)}, bf16[2,128,384]{2,1,0:T(8,128)(2,1)S(1)}, u32[]{:S(2)}, u32[]{:S(2)}) collective-permute-start(bf16[2,128,384]{2,1,0:T(8,128)(2,1)S(1)} %get-tuple-element.38), channel_id=1, source_target_pairs={{0,2},{1,3},{2,0},{3,1},{4,6},{5,7},{6,4},{7,5},{8,10},{9,11},{10,... | collective-permute-start | bytes 589832 | tf_op jit(solution)/shard_map/ppermute | solution.py:75
  76.1 5.7 %collective-permute-start.6 = (bf16[2,128,384]{2,1,0:T(8,128)(2,1)S(1)}, bf16[2,128,384]{2,1,0:T(8,128)(2,1)S(1)}, u32[]{:S(2)}, u32[]{:S(2)}) collective-permute-start(bf16[2,128,384]{2,1,0:T(8,128)(2,1)S(1)} %get-tuple-element.39), channel_id=1, source_target_pairs={{0,8},{1,9},{2,10},{3,11},{4,12},{5,13},{6,14},{7,15},{8,0},{9,1},... | collective-permute-start | bytes 589832 | tf_op jit(solution)/shard_map/ppermute | solution.py:75
  82.0 5.7 %collective-permute-start.7 = (bf16[2,128,384]{2,1,0:T(8,128)(2,1)S(1)}, bf16[2,128,384]{2,1,0:T(8,128)(2,1)S(1)}, u32[]{:S(2)}, u32[]{:S(2)}) collective-permute-start(bf16[2,128,384]{2,1,0:T(8,128)(2,1)S(1)} %get-tuple-element.43), channel_id=1, source_target_pairs={{0,2},{1,3},{2,0},{3,1},{4,6},{5,7},{6,4},{7,5},{8,10},{9,11},{10,... | collective-permute-start | bytes 589832 | tf_op jit(solution)/shard_map/ppermute | solution.py:75
  83.2 5.7 %collective-permute-start.8 = (bf16[2,128,384]{2,1,0:T(8,128)(2,1)S(1)}, bf16[2,128,384]{2,1,0:T(8,128)(2,1)S(1)}, u32[]{:S(2)}, u32[]{:S(2)}) collective-permute-start(bf16[2,128,384]{2,1,0:T(8,128)(2,1)S(1)} %get-tuple-element.44), channel_id=1, source_target_pairs={{0,8},{1,9},{2,10},{3,11},{4,12},{5,13},{6,14},{7,15},{8,0},{9,1},... | collective-permute-start | bytes 589832 | tf_op jit(solution)/shard_map/ppermute | solution.py:75
  83.7 7.3 %collective-permute-start.9 = (bf16[2,128,384]{2,1,0:T(8,128)(2,1)S(1)}, bf16[2,128,384]{2,1,0:T(8,128)(2,1)S(1)}, u32[]{:S(2)}, u32[]{:S(2)}) collective-permute-start(bf16[2,128,384]{2,1,0:T(8,128)(2,1)S(1)} %get-tuple-element.45), channel_id=1, source_target_pairs={{0,16},{1,17},{2,18},{3,19},{4,20},{5,21},{6,22},{7,23},{8,24},{9,... | collective-permute-start | bytes 589832 | tf_op jit(solution)/shard_map/ppermute | solution.py:75
  91.1 10.2 %collective-permute-start.10 = (bf16[2,128,384]{2,1,0:T(8,128)(2,1)S(1)}, bf16[2,128,384]{2,1,0:T(8,128)(2,1)S(1)}, u32[]{:S(2)}, u32[]{:S(2)}) collective-permute-start(bf16[2,128,384]{2,1,0:T(8,128)(2,1)S(1)} %get-tuple-element.46), channel_id=1, source_target_pairs={{0,16},{1,17},{2,18},{3,19},{4,20},{5,21},{6,22},{7,23},{8,24},{9,... | collective-permute-start | bytes 589832 | tf_op jit(solution)/shard_map/ppermute | solution.py:75
  92.5 7.9 %collective-permute-start.11 = (bf16[2,128,384]{2,1,0:T(8,128)(2,1)S(1)}, bf16[2,128,384]{2,1,0:T(8,128)(2,1)S(1)}, u32[]{:S(2)}, u32[]{:S(2)}) collective-permute-start(bf16[2,128,384]{2,1,0:T(8,128)(2,1)S(1)} %get-tuple-element.47), channel_id=1, source_target_pairs={{0,2},{1,3},{2,0},{3,1},{4,6},{5,7},{6,4},{7,5},{8,10},{9,11},{10,... | collective-permute-start | bytes 589832 | tf_op jit(solution)/shard_map/ppermute | solution.py:75
  93.8 5.7 %collective-permute-start.12 = (bf16[2,128,384]{2,1,0:T(8,128)(2,1)S(1)}, bf16[2,128,384]{2,1,0:T(8,128)(2,1)S(1)}, u32[]{:S(2)}, u32[]{:S(2)}) collective-permute-start(bf16[2,128,384]{2,1,0:T(8,128)(2,1)S(1)} %get-tuple-element.48), channel_id=1, source_target_pairs={{0,8},{1,9},{2,10},{3,11},{4,12},{5,13},{6,14},{7,15},{8,0},{9,1},... | collective-permute-start | bytes 589832 | tf_op jit(solution)/shard_map/ppermute | solution.py:75
  99.5 3.2 %collective-permute-start.18 = (bf16[4,128,384]{2,1,0:T(8,128)(2,1)S(1)}, bf16[4,128,384]{2,1,0:T(8,128)(2,1)S(1)}, u32[]{:S(2)}, u32[]{:S(2)}) collective-permute-start(bf16[4,128,384]{2,1,0:T(8,128)(2,1)S(1)} %constant_dynamic-update-slice_fusion.4.refs_2_), channel_id=1, source_target_pairs={{0,1},{1,0},{2,3},{3,2},{4,5},{5,4},{6,7},{7,6},{8,9},{9,8},{10,11... | collective-permute-start | bytes 1179656 | tf_op jit(solution)/shard_map/ppermute | solution.py:75
  99.6 11.5 %collective-permute-start.15 = (bf16[4,128,384]{2,1,0:T(8,128)(2,1)S(1)}, bf16[4,128,384]{2,1,0:T(8,128)(2,1)S(1)}, u32[]{:S(2)}, u32[]{:S(2)}) collective-permute-start(bf16[4,128,384]{2,1,0:T(8,128)(2,1)S(1)} %constant_dynamic-update-slice_fusion.4.refs_2_), channel_id=1, source_target_pairs={{0,2},{1,3},{2,0},{3,1},{4,6},{5,7},{6,4},{7,5},{8,10},{9,11},{10,... | collective-permute-start | bytes 1179656 | tf_op jit(solution)/shard_map/ppermute | solution.py:75
  100.5 11.3 %collective-permute-start.14 = (bf16[4,128,384]{2,1,0:T(8,128)(2,1)S(1)}, bf16[4,128,384]{2,1,0:T(8,128)(2,1)S(1)}, u32[]{:S(2)}, u32[]{:S(2)}) collective-permute-start(bf16[4,128,384]{2,1,0:T(8,128)(2,1)S(1)} %constant_dynamic-update-slice_fusion.2.refs_1_), channel_id=1, source_target_pairs={{0,16},{1,17},{2,18},{3,19},{4,20},{5,21},{6,22},{7,23},{8,24},{9,... | collective-permute-start | bytes 1179656 | tf_op jit(solution)/shard_map/ppermute | solution.py:75
  101.3 11.0 %collective-permute-start.13 = (bf16[4,128,384]{2,1,0:T(8,128)(2,1)S(1)}, bf16[4,128,384]{2,1,0:T(8,128)(2,1)S(1)}, u32[]{:S(2)}, u32[]{:S(2)}) collective-permute-start(bf16[4,128,384]{2,1,0:T(8,128)(2,1)S(1)} %constant_dynamic-update-slice_fusion.refs_0_), channel_id=1, source_target_pairs={{0,8},{1,9},{2,10},{3,11},{4,12},{5,13},{6,14},{7,15},{8,0},{9,1},... | collective-permute-start | bytes 1179656 | tf_op jit(solution)/shard_map/ppermute | solution.py:75
  102.7 9.6 %collective-permute-start.17 = (bf16[4,128,384]{2,1,0:T(8,128)(2,1)S(1)}, bf16[4,128,384]{2,1,0:T(8,128)(2,1)S(1)}, u32[]{:S(2)}, u32[]{:S(2)}) collective-permute-start(bf16[4,128,384]{2,1,0:T(8,128)(2,1)S(1)} %constant_dynamic-update-slice_fusion.2.refs_1_), channel_id=1, source_target_pairs={{0,1},{1,0},{2,3},{3,2},{4,5},{5,4},{6,7},{7,6},{8,9},{9,8},{10,11... | collective-permute-start | bytes 1179656 | tf_op jit(solution)/shard_map/ppermute | solution.py:75
  102.7 9.6 %collective-permute-start.16 = (bf16[4,128,384]{2,1,0:T(8,128)(2,1)S(1)}, bf16[4,128,384]{2,1,0:T(8,128)(2,1)S(1)}, u32[]{:S(2)}, u32[]{:S(2)}) collective-permute-start(bf16[4,128,384]{2,1,0:T(8,128)(2,1)S(1)} %constant_dynamic-update-slice_fusion.refs_0_), channel_id=1, source_target_pairs={{0,1},{1,0},{2,3},{3,2},{4,5},{5,4},{6,7},{7,6},{8,9},{9,8},{10,11... | collective-permute-start | bytes 1179656 | tf_op jit(solution)/shard_map/ppermute | solution.py:75
  111.1 1.7 %collective-permute-start.21 = (bf16[4,128,384]{2,1,0:T(8,128)(2,1)S(1)}, bf16[4,128,384]{2,1,0:T(8,128)(2,1)S(1)}, u32[]{:S(2)}, u32[]{:S(2)}) collective-permute-start(bf16[4,128,384]{2,1,0:T(8,128)(2,1)S(1)} %collective-permute-done.15.refs_5_), channel_id=1, source_target_pairs={{0,1},{1,0},{2,3},{3,2},{4,5},{5,4},{6,7},{7,6},{8,9},{9,8},{10,11... | collective-permute-start | bytes 1179656 | tf_op jit(solution)/shard_map/ppermute | solution.py:75
  111.7 1.7 %collective-permute-start.20 = (bf16[4,128,384]{2,1,0:T(8,128)(2,1)S(1)}, bf16[4,128,384]{2,1,0:T(8,128)(2,1)S(1)}, u32[]{:S(2)}, u32[]{:S(2)}) collective-permute-start(bf16[4,128,384]{2,1,0:T(8,128)(2,1)S(1)} %collective-permute-done.14.refs_4_), channel_id=1, source_target_pairs={{0,1},{1,0},{2,3},{3,2},{4,5},{5,4},{6,7},{7,6},{8,9},{9,8},{10,11... | collective-permute-start | bytes 1179656 | tf_op jit(solution)/shard_map/ppermute | solution.py:75
  112.3 1.7 %collective-permute-start.19 = (bf16[4,128,384]{2,1,0:T(8,128)(2,1)S(1)}, bf16[4,128,384]{2,1,0:T(8,128)(2,1)S(1)}, u32[]{:S(2)}, u32[]{:S(2)}) collective-permute-start(bf16[4,128,384]{2,1,0:T(8,128)(2,1)S(1)} %collective-permute-done.13.refs_3_), channel_id=1, source_target_pairs={{0,1},{1,0},{2,3},{3,2},{4,5},{5,4},{6,7},{7,6},{8,9},{9,8},{10,11... | collective-permute-start | bytes 1179656 | tf_op jit(solution)/shard_map/ppermute | solution.py:75
  124.2 43.3 %collective-permute-start.23 = (bf16[512,896]{1,0:T(8,128)(2,1)S(1)}, bf16[512,896]{1,0:T(8,128)(2,1)S(1)}, u32[]{:S(2)}, u32[]{:S(2)}) collective-permute-start(bf16[512,896]{1,0:T(8,128)(2,1)S(1)} %get-tuple-element.50), channel_id=1, source_target_pairs={{0,4},{1,6},{2,5},{3,7},{4,0},{5,2},{6,1},{7,3},{8,12},{9,14},{10,... | collective-permute-start | bytes 2752520 | tf_op jit(solution)/shard_map/ppermute | solution.py:75
  133.9 35.1 %collective-permute-start.22 = (bf16[512,896]{1,0:T(8,128)(2,1)S(1)}, bf16[512,896]{1,0:T(8,128)(2,1)S(1)}, u32[]{:S(2)}, u32[]{:S(2)}) collective-permute-start(bf16[512,896]{1,0:T(8,128)(2,1)S(1)} %near_rows.1), channel_id=1, source_target_pairs={{0,0},{1,2},{2,1},{3,3},{4,4},{5,6},{6,5},{7,7},{8,8},{9,10},{10,9... | collective-permute-start | bytes 2752520 | tf_op jit(solution)/shard_map/ppermute | solution.py:75
  (1 other events, 1.5 us)

commit v3 on v2

v3 whole, which is shorter than its diff:
```python
import functools

import jax
import jax.numpy as jnp
from jax import lax
from jax.experimental import pallas as pl
from jax.experimental.pallas import tpu as pltpu
from jax.sharding import PartitionSpec as P

linear_coef = 3.4445
cubic_coef = -4.775
quintic_coef = 2.0315

AXES = ("mat", "gr", "gc")


def plain_body(iterate):
    regrouped = lax.all_to_all(iterate, ("mat", "gc"), split_axis=3, concat_axis=2, tiled=True)
    row_block = regrouped[:, 0]
    panel_rows = lax.all_gather(row_block, "gr", axis=1, tiled=True)
    total_rows = panel_rows.shape[1]
    groups = lax.axis_size(("mat", "gc"))
    gram_width = total_rows // groups
    inv_cols = 1.0 / iterate.shape[-1]
    partial_value = jnp.einsum(
        "irc,ijc->irj", row_block, panel_rows, preferred_element_type=jnp.float32
    )
    gram_rows = (lax.psum(partial_value, ("mat", "gc")) * inv_cols).astype(jnp.bfloat16)
    own_block = lax.dynamic_slice_in_dim(
        gram_rows, lax.axis_index(("mat", "gc")) * gram_width, gram_width, 2
    )
    square = jnp.einsum(
        "irk,ikj->irj",
        gram_rows,
        lax.all_gather(own_block, "gr", axis=1, tiled=True),
        preferred_element_type=jnp.float32,
    )
    poly_block = (cubic_coef * own_block.astype(jnp.float32) + quintic_coef * square).astype(
        jnp.bfloat16
    )
    mixed_sum = jnp.einsum(
        "irk,ikc->irc",
        lax.all_gather(poly_block, ("mat", "gc"), axis=2, tiled=True),
        panel_rows,
        preferred_element_type=jnp.float32,
    )
    result = linear_coef * row_block.astype(jnp.float32) + mixed_sum
    return result.astype(jnp.bfloat16)


CHIPS = 8
BLOCK = 128
STRIP = 9 * BLOCK
THIRD = STRIP // 3
ORDERS = ((2, 4, 1), (4, 1, 2), (1, 2, 4))
PARAMS = dict(vmem_limit_bytes=28 * 1024 * 1024)


def cost(flops, bytes_accessed):
    return pl.CostEstimate(flops=flops, bytes_accessed=bytes_accessed, transcendentals=0)


def offset(third, place):
    axes = ORDERS[third]
    return sum(axes[k] for k in range(3) if place >> (2 - k) & 1)


def send(value, move):
    perm = []
    for m in range(4):
        for r in range(4):
            for c in range(2):
                to = move(m, r, c)
                perm.append((m * 8 + r * 2 + c, to[0] * 8 + to[1] * 2 + to[2]))
    return lax.ppermute(value, AXES, perm)


def across(d):
    return lambda m, r, c: (m ^ (d >> 1), r ^ (d & 1), c)


def other_core(m, r, c):
    return m, r, 1 - c


def cut_kernel(x_ref, o_ref, sems):
    copies = []
    width = o_ref.shape[-1]
    for q in range(2):
        for k in range(CHIPS):
            copies.append(
                pltpu.make_async_copy(
                    x_ref.at[q, :, pl.ds(k * width, width)],
                    o_ref.at[q, k % 2, k // 2],
                    sems.at[q * CHIPS + k],
                )
            )
    for copy in copies:
        copy.start()
    for copy in copies:
        copy.wait()


def cut(x):
    _, rows, cols = x.shape
    return pl.pallas_call(
        cut_kernel,
        out_shape=jax.ShapeDtypeStruct((2, 2, 4, rows, cols // CHIPS), x.dtype),
        in_specs=[pl.BlockSpec(memory_space=pl.ANY)],
        out_specs=pl.BlockSpec(memory_space=pl.ANY),
        scratch_shapes=[pltpu.SemaphoreType.DMA((16,))],
        compiler_params=pltpu.CompilerParams(**PARAMS),
        name="cut_columns",
    )(x)


GRAM_DIMS = (((1,), (1,)), ((), ()))


def own_kernel(own, strips, panel, sem):
    copy = pltpu.make_async_copy(own, panel.at[pl.ds(0, 1024)], sem)
    copy.start()
    for t in range(4):
        lo = 256 * t
        made = lax.dot_general(
            own[lo : lo + 256, :], own[lo:, :], GRAM_DIMS, preferred_element_type=jnp.float32
        )
        strips[2 * t, :, : 1024 - lo] = made[:BLOCK]
        strips[2 * t + 1, :, : 1024 - BLOCK - lo] = made[BLOCK:, BLOCK:]
    copy.wait()


def own_strips(own):
    rows, cols = own.shape
    return pl.pallas_call(
        own_kernel,
        out_shape=[
            jax.ShapeDtypeStruct((CHIPS, BLOCK, STRIP), jnp.float32),
            jax.ShapeDtypeStruct((2 * rows, cols), own.dtype),
        ],
        in_specs=[pl.BlockSpec(memory_space=pltpu.VMEM)],
        out_specs=[pl.BlockSpec(memory_space=pltpu.VMEM)] * 2,
        scratch_shapes=[pltpu.SemaphoreType.DMA],
        cost_estimate=cost(1024 * 1280 * cols, 10**7),
        compiler_params=pltpu.CompilerParams(**PARAMS),
        name="own_strips",
    )(own)


def gram_kernel(p_ref, strips_in, panel_in, own, other, *rest):
    del strips_in, panel_in
    keep, away, (strips, panel, sem) = rest[:3], rest[3:6], rest[6:]
    copy = pltpu.make_async_copy(other, panel.at[pl.ds(1024, 1024)], sem)
    copy.start()
    for t in range(4):
        lo = 256 * t
        made = lax.dot_general(
            own[lo : lo + 256, :],
            other[: lo + 256, :],
            GRAM_DIMS,
            preferred_element_type=jnp.float32,
        )
        strips[2 * t, :, 1024 - lo :] = made[:BLOCK, : BLOCK + lo]
        strips[2 * t + 1, :, 1024 - BLOCK - lo :] = made[BLOCK:]
    p = p_ref[0]
    for i in range(3):
        cols = slice(THIRD * i, THIRD * (i + 1))
        for place in range(4):
            keep[i][place] = strips[p ^ offset(i, place), :, cols]
            away[i][place] = strips[p ^ offset(i, place + 4), :, cols].astype(jnp.bfloat16)
    copy.wait()


def gram_strips(p, strips, panel, own, other):
    shape = (4, BLOCK, THIRD)
    made = pl.pallas_call(
        gram_kernel,
        out_shape=[jax.ShapeDtypeStruct(shape, jnp.float32)] * 3
        + [jax.ShapeDtypeStruct(shape, jnp.bfloat16)] * 3
        + [jax.ShapeDtypeStruct(v.shape, v.dtype) for v in (strips, panel)],
        in_specs=[pl.BlockSpec(memory_space=pltpu.SMEM)]
        + [pl.BlockSpec(memory_space=pltpu.VMEM)] * 4,
        out_specs=[pl.BlockSpec(memory_space=pltpu.VMEM)] * 8,
        scratch_shapes=[pltpu.SemaphoreType.DMA],
        input_output_aliases={1: 6, 2: 7},
        cost_estimate=cost(1024 * 1280 * own.shape[-1], 10**7),
        compiler_params=pltpu.CompilerParams(**PARAMS),
        name="gram_strips",
    )(p, strips, panel, own, other)
    return made[:3], made[3:6], made[7]


def halves_kernel(held, came, keep, away):
    half = keep.shape[0]
    total = held[...] + came[...].astype(jnp.float32)
    keep[...] = total[:half]
    away[...] = total[half:].astype(jnp.bfloat16)


def pairs_kernel(held, came, keep, away):
    total = held[...] + came[...].astype(jnp.float32)
    keep[...] = total
    away[0] = total[1].astype(jnp.bfloat16)
    away[1] = total[0].astype(jnp.bfloat16)


def last_kernel(scale, held, came, out):
    total = held[...] + came[...].astype(jnp.float32)
    out[...] = (total * scale).astype(jnp.bfloat16)


def add(kernel, name, types, held, came):
    shape = (2, BLOCK, THIRD)
    return pl.pallas_call(
        kernel,
        out_shape=[jax.ShapeDtypeStruct(shape, dtype) for dtype in types],
        in_specs=[pl.BlockSpec(memory_space=pltpu.VMEM)] * 2,
        out_specs=[pl.BlockSpec(memory_space=pltpu.VMEM)] * len(types),
        cost_estimate=cost(10**5, 10**6),
        compiler_params=pltpu.CompilerParams(**PARAMS),
        name=name,
    )(held, came)


def sum_third(third, keep, away, scale):
    first, second, last = (across(axis) for axis in ORDERS[third])
    both = (jnp.float32, jnp.bfloat16)
    keep, away = add(halves_kernel, "add_halves", both, keep, send(away, first))
    keep, away = add(pairs_kernel, "add_pairs", both, keep, send(away, second))
    (made,) = add(
        functools.partial(last_kernel, scale), "add_last", both[1:], keep, send(away, last)
    )
    return made


def sum_strips(keep, away, scale):
    return [sum_third(third, keep[third], away[third], scale) for third in range(3)]


def gather_strips(parts):
    came = [send(parts[i], across(ORDERS[i][1])) for i in range(3)]
    early = [jnp.concatenate([parts[i], came[i]], axis=0) for i in range(3)]
    late = [send(early[i], across(ORDERS[i][0])) for i in range(3)]
    early += [send(part, other_core) for part in early]
    late += [send(part, other_core) for part in late]
    return early + late


def fill(gram, p, thirds, first_place):
    for k, ref in enumerate(thirds):
        third, far_half = k % 3, 8 * (k // 3)
        for j in range(4):
            row = (p ^ offset(third, first_place + j)) + far_half
            row_at = pl.ds(pl.multiple_of(row * BLOCK, BLOCK), BLOCK)
            for d in range(3 * third, 3 * third + 3):
                col = (row + d) & 15
                col_at = pl.ds(pl.multiple_of(col * BLOCK, BLOCK), BLOCK)
                block = ref[j, :, BLOCK * (d - 3 * third) : BLOCK * (d - 3 * third + 1)]
                gram[row_at, col_at] = block
                if 1 <= d <= 7:
                    gram[col_at, row_at] = block.T


def result_rows(gram, panel, poly, place, half):
    start = pl.multiple_of(1024 * half + place * 256, 256)
    rows = gram[pl.ds(start, 256), :]
    for n in range(0, 2048, 512):
        square = jnp.dot(rows, gram[:, n : n + 512], preferred_element_type=jnp.float32)
        poly[:, n : n + 512] = (
            cubic_coef * rows[:, n : n + 512].astype(jnp.float32) + quintic_coef * square
        ).astype(jnp.bfloat16)
    mixed = jnp.dot(poly[...], panel[...], preferred_element_type=jnp.float32)
    return (linear_coef * panel[pl.ds(start, 256), :].astype(jnp.float32) + mixed).astype(
        jnp.bfloat16
    )


def first_kernel(s_ref, *refs):
    strips, panel, gram, out, poly = refs[:12], *refs[12:]
    fill(gram, s_ref[0], strips[:6], 0)
    fill(gram, s_ref[0], strips[6:], 4)
    for half in range(2):
        out[256 * half : 256 * (half + 1)] = result_rows(gram, panel, poly, s_ref[1], half)


def first_rows(scalars, strips, panel):
    cols = panel.shape[-1]
    return pl.pallas_call(
        first_kernel,
        out_shape=[
            jax.ShapeDtypeStruct((2048, 2048), jnp.bfloat16),
            jax.ShapeDtypeStruct((512, cols), jnp.bfloat16),
        ],
        in_specs=[pl.BlockSpec(memory_space=pltpu.SMEM)]
        + [pl.BlockSpec(memory_space=pltpu.VMEM)] * 13,
        out_specs=[pl.BlockSpec(memory_space=pltpu.VMEM)] * 2,
        scratch_shapes=[pltpu.VMEM((256, 2048), jnp.bfloat16)],
        cost_estimate=cost(2 * 512 * 2048 * (2048 + cols), 3 * 10**7),
        compiler_params=pltpu.CompilerParams(**PARAMS),
        name="first_rows",
    )(scalars, *strips, panel)


def near_kernel(s_ref, gram, panel, out, poly):
    for half in range(2):
        out[256 * half : 256 * (half + 1)] = result_rows(gram, panel, poly, s_ref[2], half)


def near_rows(scalars, gram, panel):
    cols = panel.shape[-1]
    return pl.pallas_call(
        near_kernel,
        out_shape=jax.ShapeDtypeStruct((512, cols), jnp.bfloat16),
        in_specs=[pl.BlockSpec(memory_space=pltpu.SMEM)]
        + [pl.BlockSpec(memory_space=pltpu.VMEM)] * 2,
        out_specs=pl.BlockSpec(memory_space=pltpu.VMEM),
        scratch_shapes=[pltpu.VMEM((256, 2048), jnp.bfloat16)],
        cost_estimate=cost(2 * 512 * 2048 * (2048 + cols), 10**7),
        compiler_params=pltpu.CompilerParams(**PARAMS),
        name="near_rows",
    )(scalars, gram, panel)


def hold_kernel(piece, out):
    del piece, out


def hold(piece):
    return pl.pallas_call(
        hold_kernel,
        out_shape=jax.ShapeDtypeStruct(piece.shape, piece.dtype),
        in_specs=[pl.BlockSpec(memory_space=pl.ANY)],
        out_specs=pl.BlockSpec(memory_space=pl.ANY),
        input_output_aliases={0: 0},
        cost_estimate=cost(2 * 10**10, 10**6),
        compiler_params=pltpu.CompilerParams(**PARAMS),
        name="hold",
    )(piece)


def place_kernel(s_ref, near, far, out, sems):
    matrix, core = s_ref[3], s_ref[4]
    copies = []
    for piece, i in ((near, matrix), (far, 1 - matrix)):
        for half, sub in enumerate((core, 1 - core)):
            sem = sems.at[len(copies)]
            copies.append(pltpu.make_async_copy(piece.at[half], out.at[i, :, sub], sem))
    for copy in copies:
        copy.start()
    for copy in copies:
        copy.wait()


def place_rows(scalars, near, far):
    _, groups, rows, cols = near.shape
    return pl.pallas_call(
        place_kernel,
        out_shape=jax.ShapeDtypeStruct((2, groups, 2, rows, cols), jnp.bfloat16),
        in_specs=[pl.BlockSpec(memory_space=pltpu.SMEM)]
        + [pl.BlockSpec(memory_space=pl.ANY)] * 2,
        out_specs=pl.BlockSpec(memory_space=pl.ANY),
        scratch_shapes=[pltpu.SemaphoreType.DMA((4,))],
        compiler_params=pltpu.CompilerParams(**PARAMS),
        name="place_rows",
    )(scalars, near, far)


def home_far(m, r, c):
    return m, (1 - r // 2) * 2 + c, r % 2


def home_near(m, r, c):
    return m, (r // 2) * 2 + c, r % 2


def fast_body(iterate):
    x = iterate[:, 0]
    mats, rows, cols = x.shape
    m, r, c = (lax.axis_index(axis) for axis in AXES)
    q, b = r // 2, r % 2
    scalars = jnp.stack([2 * m + b, 2 * (1 - q) + c, 2 * q + c, q, b]).astype(jnp.int32)
    pieces = cut(x).reshape(32, rows // 2, cols // CHIPS)
    own = lax.all_to_all(pieces, ("gr", "mat", "gc"), 0, 0, tiled=True)
    own = own.reshape(1024, cols // CHIPS)
    other = send(own, other_core)
    keep, away, panel = gram_strips(scalars, *own_strips(own), own, other)
    strips = gather_strips(sum_strips(keep, away, 1.0 / cols))
    gram, far = first_rows(scalars, strips, panel)
    far = hold(send(far, home_far))
    near = send(near_rows(scalars, gram, panel), home_near)
    shape = (2, 8, 32, cols // CHIPS)
    result = place_rows(scalars, near.reshape(shape), far.reshape(shape))
    return result.reshape(mats, 512, cols // CHIPS)


def solution(mesh):
    fast = tuple(mesh.shape[axis] for axis in AXES) == (4, 4, 2)
    return jax.shard_map(
        fast_body if fast else plain_body,
        mesh=mesh,
        in_specs=(P(None, "gr", ("mat", "gc"), None),),
        out_specs=P(None, "gr", ("mat", "gc")),
        check_vma=False,
    )
```

time: 171 us -> 160 us (0.936)
  waiting for transfers between devices: 73.7 us -> 62.7 us
  Pallas kernels: 27.4 us -> 25.3 us
  starting transfers between devices: 17.3 us -> 19.4 us
    ppermute x24, waiting for transfers between devices: 73.7 us -> 62.7 us  [send(): return lax.ppermute(value, AXES, perm)]
    ppermute x24, starting transfers between devices: 17.3 us -> 19.4 us  [send(): return lax.ppermute(value, AXES, perm)]
    pallas_call x5 -> x12, Pallas kernels: 3.47 us -> 4.09 us  [the longest x1 1.8 us: place_rows(): pl.pallas_call(place_kernel, out_shape=jax.ShapeDtypeStruct((2, groups, 2...]
  transfers between devices with their start and end apart: 24 -> 24, of which waited for: 18 -> 13; matrix products, arithmetic and copies ran while one was open for 0% -> 0% of each run, Pallas kernels for 6% -> 6%
where the time goes in v3:
time: 160 us
  waiting for transfers between devices  62.7 us (39%)
  blocking collectives  50.2 us (31%)
  Pallas kernels  25.3 us (16%)
  starting transfers between devices  19.4 us (12%)
    ppermute x24, waiting for transfers between devices, send(): return lax.ppermute(value, AXES, perm)  62.7 us
    all_to_all x1, blocking collectives, fast_body(): own = lax.all_to_all(pieces, ('gr', 'mat', 'gc'), 0, 0, tiled=True)  50.2 us
    ppermute x24, starting transfers between devices, send(): return lax.ppermute(value, AXES, perm)  19.4 us
    pallas_call x1, Pallas kernels, first_rows(): pl.pallas_call(first_kernel, out_shape=[jax.ShapeDtypeStruct((2048, 2048)...  9.62 us
    pallas_call x1, Pallas kernels, near_rows(): pl.pallas_call(near_kernel, out_shape=jax.ShapeDtypeStruct((512, cols), j...  7.62 us
    pallas_call x1, Pallas kernels, gram_strips(): pl.pallas_call(gram_kernel, out_shape=[jax.ShapeDtypeStruct(shape, jnp.fl...  3.48 us
  transfers between devices with their start and end apart: 24, of which 13 were waited for; matrix products, arithmetic and copies ran while one was open for 0% of the time, Pallas kernels for 6%

profile of v3, /device:TPU:0, one launch (start us, length us, event | category | flops | bytes accessed | tf_op | source)
XLA Modules:
  0.0 159.5 jit_solution(2570617207989944060)
XLA Ops:
  0.0 1.5 copy-done
  2.0 50.2 %all_to_all.5 = bf16[32,32,896]{2,1,0:T(8,128)(2,1)S(1)} all-to-all(bf16[32,32,896]{2,1,0:T(8,128)(2,1)S(1)} %bitcast.11), channel_id=1, replica_groups=mesh['mat'=4,'gr'=4,'gc'=2] {'gr','mat','gc'}, dimensions={0} | all-to-all | bytes 3670016 | tf_op jit(solution)/shard_map/all_to_all | solution.py:383
  52.3 1.7 %own_strips.1 = (f32[8,128,1152]{2,1,0:T(8,128)S(1)}, bf16[2048,896]{1,0:T(8,128)(2,1)S(1)}) custom-call(bf16[1024,896]{1,0:T(8,128)(2,1)S(1)} %bitcast.13), custom_call_target="tpu_custom_call" | custom-call | flops 1174405120 | bytes 10000000 | tf_op jit(solution)/shard_map/own_strips/pallas_call | solution.py:135
  54.0 2.1 %collective-permute-done.other = bf16[1024,896]{1,0:T(8,128)(2,1)} collective-permute-done((bf16[1024,896]{1,0:T(8,128)(2,1)S(1)}, bf16[1024,896]{1,0:T(8,128)(2,1)}, u32[]{:S(2)}, u32[]{:S(2)}) %collective-permute-start) | collective-permute-done | bytes 1835040 | tf_op jit(solution)/shard_map/ppermute | solution.py:75
  56.1 3.5 %gram_strips.1 = (f32[4,128,384]{2,1,0:T(8,128)S(1)}, f32[4,128,384]{2,1,0:T(8,128)S(1)}, f32[4,128,384]{2,1,0:T(8,128)S(1)}, bf16[4,128,384]{2,1,0:T(8,128)(2,1...) custom-call(s32[5]{0:T(128)S(1)} %stack.23.p_ref.s_ref, ...), custom_call_target="tpu_custom_call", output_to_operand_aliasing={{6}: (1, {}), {7}: (2, {})} | custom-call | flops 1174405120 | bytes 10000000 | tf_op jit(solution)/shard_map/gram_strips/pallas_call | solution.py:176
  59.6 1.6 collective-permute-start.1
  61.1 1.4 collective-permute-start.5
  62.6 8.2 %collective-permute-done.1.came = bf16[4,128,384]{2,1,0:T(8,128)(2,1)S(1)} collective-permute-done((bf16[4,128,384]{2,1,0:T(8,128)(2,1)S(1)}, bf16[4,128,384]{2,1,0:T(8,128)(2,1)S(1)}, u32[]{:S(2)}, u32[]{:S(2)}) %collective-permute-start.1) | collective-permute-done | bytes 393248 | tf_op jit(solution)/shard_map/ppermute | solution.py:75
  70.9 1.5 collective-permute-start.2
  74.2 2.8 %collective-permute-done.2.came = bf16[2,128,384]{2,1,0:T(8,128)(2,1)S(1)} collective-permute-done((bf16[2,128,384]{2,1,0:T(8,128)(2,1)S(1)}, bf16[2,128,384]{2,1,0:T(8,128)(2,1)S(1)}, u32[]{:S(2)}, u32[]{:S(2)}) %collective-permute-start.2) | collective-permute-done | bytes 196640 | tf_op jit(solution)/shard_map/ppermute | solution.py:75
  77.1 1.4 collective-permute-start.3
  78.6 1.5 collective-permute-start.7
  80.7 2.1 %collective-permute-done.3.came = bf16[2,128,384]{2,1,0:T(8,128)(2,1)S(1)} collective-permute-done((bf16[2,128,384]{2,1,0:T(8,128)(2,1)S(1)}, bf16[2,128,384]{2,1,0:T(8,128)(2,1)S(1)}, u32[]{:S(2)}, u32[]{:S(2)}) %collective-permute-start.3) | collective-permute-done | bytes 196640 | tf_op jit(solution)/shard_map/ppermute | solution.py:75
  82.9 1.5 collective-permute-start.4
  85.5 1.8 %collective-permute-done.11.came = bf16[2,128,384]{2,1,0:T(8,128)(2,1)S(1)} collective-permute-done((bf16[2,128,384]{2,1,0:T(8,128)(2,1)S(1)}, bf16[2,128,384]{2,1,0:T(8,128)(2,1)S(1)}, u32[]{:S(2)}, u32[]{:S(2)}) %collective-permute-start.11) | collective-permute-done | bytes 196640 | tf_op jit(solution)/shard_map/ppermute | solution.py:75
  87.3 1.4 collective-permute-start.12
  89.4 1.5 collective-permute-start.16
  92.0 3.2 %collective-permute-done.12 = bf16[2,128,384]{2,1,0:T(8,128)(2,1)S(1)} collective-permute-done((bf16[2,128,384]{2,1,0:T(8,128)(2,1)S(1)}, bf16[2,128,384]{2,1,0:T(8,128)(2,1)S(1)}, u32[]{:S(2)}, u32[]{:S(2)}) %collective-permute-start.12) | collective-permute-done | bytes 196640 | tf_op jit(solution)/shard_map/ppermute | solution.py:75
  96.4 3.9 %collective-permute-done.16.refs_6_ = bf16[4,128,384]{2,1,0:T(8,128)(2,1)S(1)} collective-permute-done((bf16[4,128,384]{2,1,0:T(8,128)(2,1)S(1)}, bf16[4,128,384]{2,1,0:T(8,128)(2,1)S(1)}, u32[]{:S(2)}, u32[]{:S(2)}) %collective-permute-start.16) | collective-permute-done | bytes 393248 | tf_op jit(solution)/shard_map/ppermute | solution.py:75
  100.9 1.7 %collective-permute-done.17.refs_7_ = bf16[4,128,384]{2,1,0:T(8,128)(2,1)S(1)} collective-permute-done((bf16[4,128,384]{2,1,0:T(8,128)(2,1)S(1)}, bf16[4,128,384]{2,1,0:T(8,128)(2,1)S(1)}, u32[]{:S(2)}, u32[]{:S(2)}) %collective-permute-start.17) | collective-permute-done | bytes 393248 | tf_op jit(solution)/shard_map/ppermute | solution.py:75
  105.1 9.6 %first_rows.1 = (bf16[2048,2048]{1,0:T(8,128)(2,1)S(1)}, bf16[512,896]{1,0:T(8,128)(2,1)S(1)}) custom-call(s32[5]{0:T(128)S(1)} %stack.23.p_ref.s_ref, bf16[4,128,384]{2,1,0:T(8,128)(2,1)S(1)} %pad_maximum_fusion.refs_0_, bf16[4,128,384]{2,1,0:T(8,128)(2,1)S(1)} %pad_maximum_fusion.1.refs_1_, bf16[4,128,384]{2,1,0:T(8,128)(2,1)S(1)} %pad_maximum_fusion.2.refs_2_, ...), custom_call_target="tpu_custom_call" | custom-call | flops 6174015488 | bytes 30000000 | tf_op jit(solution)/shard_map/first_rows/pallas_call | solution.py:288
  115.6 7.6 %near_rows.1 = bf16[512,896]{1,0:T(8,128)(2,1)S(1)} custom-call(s32[5]{0:T(128)S(1)} %stack.23.p_ref.s_ref, bf16[2048,2048]{1,0:T(8,128)(2,1)S(1)} %get-tuple-element.49.gram, bf16[2048,896]{1,0:T(8,128)(2,1)S(1)} %get-tuple-element.48.refs_12_.panel), custom_call_target="tpu_custom_call" | custom-call | flops 6174015488 | bytes 10000000 | tf_op jit(solution)/shard_map/near_rows/pallas_call | solution.py:311
  123.9 33.6 %collective-permute-done.23.piece = bf16[512,896]{1,0:T(8,128)(2,1)S(1)} collective-permute-done((bf16[512,896]{1,0:T(8,128)(2,1)S(1)}, bf16[512,896]{1,0:T(8,128)(2,1)S(1)}, u32[]{:S(2)}, u32[]{:S(2)}) %collective-permute-start.23) | collective-permute-done | bytes 917536 | tf_op jit(solution)/shard_map/ppermute | solution.py:75
  157.5 1.8 %place_rows.1 = bf16[2,8,2,32,896]{4,3,2,1,0:T(8,128)(2,1)} custom-call(s32[5]{0:T(128)S(1)} %stack.23.p_ref.s_ref, bf16[2,8,32,896]{3,2,1,0:T(8,128)(2,1)S(1)} %bitcast.17, bf16[2,8,32,896]{3,2,1,0:T(8,128)(2,1)S(1)} %bitcast.16), custom_call_target="tpu_custom_call" | custom-call | tf_op jit(solution)/shard_map/place_rows/pallas_call | solution.py:356
  (47 shorter events, 12.1 us)
Async XLA Ops:
  52.2 3.9 %collective-permute-start = (bf16[1024,896]{1,0:T(8,128)(2,1)S(1)}, bf16[1024,896]{1,0:T(8,128)(2,1)}, u32[]{:S(2)}, u32[]{:S(2)}) collective-permute-start(bf16[1024,896]{1,0:T(8,128)(2,1)S(1)} %bitcast.12), channel_id=1, source_target_pairs={{0,1},{1,0},{2,3},{3,2},{4,5},{5,4},{6,7},{7,6},{8,9},{9,8},{10,11... | collective-permute-start | bytes 5505032 | tf_op jit(solution)/shard_map/ppermute | solution.py:75
  59.6 11.2 %collective-permute-start.1 = (bf16[4,128,384]{2,1,0:T(8,128)(2,1)S(1)}, bf16[4,128,384]{2,1,0:T(8,128)(2,1)S(1)}, u32[]{:S(2)}, u32[]{:S(2)}) collective-permute-start(bf16[4,128,384]{2,1,0:T(8,128)(2,1)S(1)} %get-tuple-element.31), channel_id=1, source_target_pairs={{0,8},{1,9},{2,10},{3,11},{4,12},{5,13},{6,14},{7,15},{8,0},{9,1},... | collective-permute-start | bytes 1179656 | tf_op jit(solution)/shard_map/ppermute | solution.py:75
  61.1 11.3 %collective-permute-start.5 = (bf16[4,128,384]{2,1,0:T(8,128)(2,1)S(1)}, bf16[4,128,384]{2,1,0:T(8,128)(2,1)S(1)}, u32[]{:S(2)}, u32[]{:S(2)}) collective-permute-start(bf16[4,128,384]{2,1,0:T(8,128)(2,1)S(1)} %get-tuple-element.37), channel_id=1, source_target_pairs={{0,16},{1,17},{2,18},{3,19},{4,20},{5,21},{6,22},{7,23},{8,24},{9,... | collective-permute-start | bytes 1179656 | tf_op jit(solution)/shard_map/ppermute | solution.py:75
  62.6 10.9 %collective-permute-start.9 = (bf16[4,128,384]{2,1,0:T(8,128)(2,1)S(1)}, bf16[4,128,384]{2,1,0:T(8,128)(2,1)S(1)}, u32[]{:S(2)}, u32[]{:S(2)}) collective-permute-start(bf16[4,128,384]{2,1,0:T(8,128)(2,1)S(1)} %get-tuple-element.43), channel_id=1, source_target_pairs={{0,2},{1,3},{2,0},{3,1},{4,6},{5,7},{6,4},{7,5},{8,10},{9,11},{10,... | collective-permute-start | bytes 1179656 | tf_op jit(solution)/shard_map/ppermute | solution.py:75
  70.9 6.2 %collective-permute-start.2 = (bf16[2,128,384]{2,1,0:T(8,128)(2,1)S(1)}, bf16[2,128,384]{2,1,0:T(8,128)(2,1)S(1)}, u32[]{:S(2)}, u32[]{:S(2)}) collective-permute-start(bf16[2,128,384]{2,1,0:T(8,128)(2,1)S(1)} %get-tuple-element.33), channel_id=1, source_target_pairs={{0,16},{1,17},{2,18},{3,19},{4,20},{5,21},{6,22},{7,23},{8,24},{9,... | collective-permute-start | bytes 589832 | tf_op jit(solution)/shard_map/ppermute | solution.py:75
  72.5 6.1 %collective-permute-start.6 = (bf16[2,128,384]{2,1,0:T(8,128)(2,1)S(1)}, bf16[2,128,384]{2,1,0:T(8,128)(2,1)S(1)}, u32[]{:S(2)}, u32[]{:S(2)}) collective-permute-start(bf16[2,128,384]{2,1,0:T(8,128)(2,1)S(1)} %get-tuple-element.39), channel_id=1, source_target_pairs={{0,2},{1,3},{2,0},{3,1},{4,6},{5,7},{6,4},{7,5},{8,10},{9,11},{10,... | collective-permute-start | bytes 589832 | tf_op jit(solution)/shard_map/ppermute | solution.py:75
  73.6 6.6 %collective-permute-start.10 = (bf16[2,128,384]{2,1,0:T(8,128)(2,1)S(1)}, bf16[2,128,384]{2,1,0:T(8,128)(2,1)S(1)}, u32[]{:S(2)}, u32[]{:S(2)}) collective-permute-start(bf16[2,128,384]{2,1,0:T(8,128)(2,1)S(1)} %get-tuple-element.45), channel_id=1, source_target_pairs={{0,8},{1,9},{2,10},{3,11},{4,12},{5,13},{6,14},{7,15},{8,0},{9,1},... | collective-permute-start | bytes 589832 | tf_op jit(solution)/shard_map/ppermute | solution.py:75
  77.1 5.7 %collective-permute-start.3 = (bf16[2,128,384]{2,1,0:T(8,128)(2,1)S(1)}, bf16[2,128,384]{2,1,0:T(8,128)(2,1)S(1)}, u32[]{:S(2)}, u32[]{:S(2)}) collective-permute-start(bf16[2,128,384]{2,1,0:T(8,128)(2,1)S(1)} %get-tuple-element.35), channel_id=1, source_target_pairs={{0,2},{1,3},{2,0},{3,1},{4,6},{5,7},{6,4},{7,5},{8,10},{9,11},{10,... | collective-permute-start | bytes 589832 | tf_op jit(solution)/shard_map/ppermute | solution.py:75
  78.6 5.8 %collective-permute-start.7 = (bf16[2,128,384]{2,1,0:T(8,128)(2,1)S(1)}, bf16[2,128,384]{2,1,0:T(8,128)(2,1)S(1)}, u32[]{:S(2)}, u32[]{:S(2)}) collective-permute-start(bf16[2,128,384]{2,1,0:T(8,128)(2,1)S(1)} %get-tuple-element.41), channel_id=1, source_target_pairs={{0,8},{1,9},{2,10},{3,11},{4,12},{5,13},{6,14},{7,15},{8,0},{9,1},... | collective-permute-start | bytes 589832 | tf_op jit(solution)/shard_map/ppermute | solution.py:75
  80.2 7.0 %collective-permute-start.11 = (bf16[2,128,384]{2,1,0:T(8,128)(2,1)S(1)}, bf16[2,128,384]{2,1,0:T(8,128)(2,1)S(1)}, u32[]{:S(2)}, u32[]{:S(2)}) collective-permute-start(bf16[2,128,384]{2,1,0:T(8,128)(2,1)S(1)} %get-tuple-element.47), channel_id=1, source_target_pairs={{0,16},{1,17},{2,18},{3,19},{4,20},{5,21},{6,22},{7,23},{8,24},{9,... | collective-permute-start | bytes 589832 | tf_op jit(solution)/shard_map/ppermute | solution.py:75
  82.9 6.5 %collective-permute-start.4 = (bf16[2,128,384]{2,1,0:T(8,128)(2,1)S(1)}, bf16[2,128,384]{2,1,0:T(8,128)(2,1)S(1)}, u32[]{:S(2)}, u32[]{:S(2)}) collective-permute-start(bf16[2,128,384]{2,1,0:T(8,128)(2,1)S(1)} %add_last.3), channel_id=1, source_target_pairs={{0,16},{1,17},{2,18},{3,19},{4,20},{5,21},{6,22},{7,23},{8,24},{9,... | collective-permute-start | bytes 589832 | tf_op jit(solution)/shard_map/ppermute | solution.py:75
  84.5 6.4 %collective-permute-start.8 = (bf16[2,128,384]{2,1,0:T(8,128)(2,1)S(1)}, bf16[2,128,384]{2,1,0:T(8,128)(2,1)S(1)}, u32[]{:S(2)}, u32[]{:S(2)}) collective-permute-start(bf16[2,128,384]{2,1,0:T(8,128)(2,1)S(1)} %add_last.4), channel_id=1, source_target_pairs={{0,2},{1,3},{2,0},{3,1},{4,6},{5,7},{6,4},{7,5},{8,10},{9,11},{10,... | collective-permute-start | bytes 589832 | tf_op jit(solution)/shard_map/ppermute | solution.py:75
  87.3 7.9 %collective-permute-start.12 = (bf16[2,128,384]{2,1,0:T(8,128)(2,1)S(1)}, bf16[2,128,384]{2,1,0:T(8,128)(2,1)S(1)}, u32[]{:S(2)}, u32[]{:S(2)}) collective-permute-start(bf16[2,128,384]{2,1,0:T(8,128)(2,1)S(1)} %add_last.5), channel_id=1, source_target_pairs={{0,8},{1,9},{2,10},{3,11},{4,12},{5,13},{6,14},{7,15},{8,0},{9,1},... | collective-permute-start | bytes 589832 | tf_op jit(solution)/shard_map/ppermute | solution.py:75
  89.4 10.9 %collective-permute-start.16 = (bf16[4,128,384]{2,1,0:T(8,128)(2,1)S(1)}, bf16[4,128,384]{2,1,0:T(8,128)(2,1)S(1)}, u32[]{:S(2)}, u32[]{:S(2)}) collective-permute-start(bf16[4,128,384]{2,1,0:T(8,128)(2,1)S(1)} %pad_maximum_fusion.refs_0_), channel_id=1, source_target_pairs={{0,8},{1,9},{2,10},{3,11},{4,12},{5,13},{6,14},{7,15},{8,0},{9,1},... | collective-permute-start | bytes 1179656 | tf_op jit(solution)/shard_map/ppermute | solution.py:75
  90.9 9.5 %collective-permute-start.13 = (bf16[4,128,384]{2,1,0:T(8,128)(2,1)S(1)}, bf16[4,128,384]{2,1,0:T(8,128)(2,1)S(1)}, u32[]{:S(2)}, u32[]{:S(2)}) collective-permute-start(bf16[4,128,384]{2,1,0:T(8,128)(2,1)S(1)} %pad_maximum_fusion.refs_0_), channel_id=1, source_target_pairs={{0,1},{1,0},{2,3},{3,2},{4,5},{5,4},{6,7},{7,6},{8,9},{9,8},{10,11... | collective-permute-start | bytes 1179656 | tf_op jit(solution)/shard_map/ppermute | solution.py:75
  90.9 11.6 %collective-permute-start.17 = (bf16[4,128,384]{2,1,0:T(8,128)(2,1)S(1)}, bf16[4,128,384]{2,1,0:T(8,128)(2,1)S(1)}, u32[]{:S(2)}, u32[]{:S(2)}) collective-permute-start(bf16[4,128,384]{2,1,0:T(8,128)(2,1)S(1)} %pad_maximum_fusion.1.refs_1_), channel_id=1, source_target_pairs={{0,16},{1,17},{2,18},{3,19},{4,20},{5,21},{6,22},{7,23},{8,24},{9,... | collective-permute-start | bytes 1179656 | tf_op jit(solution)/shard_map/ppermute | solution.py:75
  95.2 8.1 %collective-permute-start.18 = (bf16[4,128,384]{2,1,0:T(8,128)(2,1)S(1)}, bf16[4,128,384]{2,1,0:T(8,128)(2,1)S(1)}, u32[]{:S(2)}, u32[]{:S(2)}) collective-permute-start(bf16[4,128,384]{2,1,0:T(8,128)(2,1)S(1)} %pad_maximum_fusion.2.refs_2_), channel_id=1, source_target_pairs={{0,2},{1,3},{2,0},{3,1},{4,6},{5,7},{6,4},{7,5},{8,10},{9,11},{10,... | collective-permute-start | bytes 1179656 | tf_op jit(solution)/shard_map/ppermute | solution.py:75
  96.4 7.0 %collective-permute-start.14 = (bf16[4,128,384]{2,1,0:T(8,128)(2,1)S(1)}, bf16[4,128,384]{2,1,0:T(8,128)(2,1)S(1)}, u32[]{:S(2)}, u32[]{:S(2)}) collective-permute-start(bf16[4,128,384]{2,1,0:T(8,128)(2,1)S(1)} %pad_maximum_fusion.1.refs_1_), channel_id=1, source_target_pairs={{0,1},{1,0},{2,3},{3,2},{4,5},{5,4},{6,7},{7,6},{8,9},{9,8},{10,11... | collective-permute-start | bytes 1179656 | tf_op jit(solution)/shard_map/ppermute | solution.py:75
  100.4 3.0 %collective-permute-start.15 = (bf16[4,128,384]{2,1,0:T(8,128)(2,1)S(1)}, bf16[4,128,384]{2,1,0:T(8,128)(2,1)S(1)}, u32[]{:S(2)}, u32[]{:S(2)}) collective-permute-start(bf16[4,128,384]{2,1,0:T(8,128)(2,1)S(1)} %pad_maximum_fusion.2.refs_2_), channel_id=1, source_target_pairs={{0,1},{1,0},{2,3},{3,2},{4,5},{5,4},{6,7},{7,6},{8,9},{9,8},{10,11... | collective-permute-start | bytes 1179656 | tf_op jit(solution)/shard_map/ppermute | solution.py:75
  100.4 3.0 %collective-permute-start.19 = (bf16[4,128,384]{2,1,0:T(8,128)(2,1)S(1)}, bf16[4,128,384]{2,1,0:T(8,128)(2,1)S(1)}, u32[]{:S(2)}, u32[]{:S(2)}) collective-permute-start(bf16[4,128,384]{2,1,0:T(8,128)(2,1)S(1)} %collective-permute-done.16.refs_6_), channel_id=1, source_target_pairs={{0,1},{1,0},{2,3},{3,2},{4,5},{5,4},{6,7},{7,6},{8,9},{9,8},{10,11... | collective-permute-start | bytes 1179656 | tf_op jit(solution)/shard_map/ppermute | solution.py:75
  102.5 1.7 %collective-permute-start.20 = (bf16[4,128,384]{2,1,0:T(8,128)(2,1)S(1)}, bf16[4,128,384]{2,1,0:T(8,128)(2,1)S(1)}, u32[]{:S(2)}, u32[]{:S(2)}) collective-permute-start(bf16[4,128,384]{2,1,0:T(8,128)(2,1)S(1)} %collective-permute-done.17.refs_7_), channel_id=1, source_target_pairs={{0,1},{1,0},{2,3},{3,2},{4,5},{5,4},{6,7},{7,6},{8,9},{9,8},{10,11... | collective-permute-start | bytes 1179656 | tf_op jit(solution)/shard_map/ppermute | solution.py:75
  103.3 1.7 %collective-permute-start.21 = (bf16[4,128,384]{2,1,0:T(8,128)(2,1)S(1)}, bf16[4,128,384]{2,1,0:T(8,128)(2,1)S(1)}, u32[]{:S(2)}, u32[]{:S(2)}) collective-permute-start(bf16[4,128,384]{2,1,0:T(8,128)(2,1)S(1)} %collective-permute-done.18.refs_8_), channel_id=1, source_target_pairs={{0,1},{1,0},{2,3},{3,2},{4,5},{5,4},{6,7},{7,6},{8,9},{9,8},{10,11... | collective-permute-start | bytes 1179656 | tf_op jit(solution)/shard_map/ppermute | solution.py:75
  114.7 42.8 %collective-permute-start.23 = (bf16[512,896]{1,0:T(8,128)(2,1)S(1)}, bf16[512,896]{1,0:T(8,128)(2,1)S(1)}, u32[]{:S(2)}, u32[]{:S(2)}) collective-permute-start(bf16[512,896]{1,0:T(8,128)(2,1)S(1)} %get-tuple-element.50), channel_id=1, source_target_pairs={{0,4},{1,6},{2,5},{3,7},{4,0},{5,2},{6,1},{7,3},{8,12},{9,14},{10,... | collective-permute-start | bytes 2752520 | tf_op jit(solution)/shard_map/ppermute | solution.py:75
  123.2 34.3 %collective-permute-start.22 = (bf16[512,896]{1,0:T(8,128)(2,1)S(1)}, bf16[512,896]{1,0:T(8,128)(2,1)S(1)}, u32[]{:S(2)}, u32[]{:S(2)}) collective-permute-start(bf16[512,896]{1,0:T(8,128)(2,1)S(1)} %near_rows.1), channel_id=1, source_target_pairs={{0,0},{1,2},{2,1},{3,3},{4,4},{5,6},{6,5},{7,7},{8,8},{9,10},{10,9... | collective-permute-start | bytes 2752520 | tf_op jit(solution)/shard_map/ppermute | solution.py:75
  (1 other events, 1.5 us)

commit v4 on v3

--- a/solution.py
+++ b/solution.py
@@ -261,16 +261,16 @@
                     gram[col_at, row_at] = block.T
 
 
-def result_rows(gram, panel, poly, place, half):
-    start = pl.multiple_of(1024 * half + place * 256, 256)
-    rows = gram[pl.ds(start, 256), :]
+def result_rows(gram, panel, poly, place, half, first, count):
+    start = pl.multiple_of(1024 * half + place * 256 + first, BLOCK)
+    rows = gram[pl.ds(start, count), :]
     for n in range(0, 2048, 512):
         square = jnp.dot(rows, gram[:, n : n + 512], preferred_element_type=jnp.float32)
-        poly[:, n : n + 512] = (
+        poly[:count, n : n + 512] = (
             cubic_coef * rows[:, n : n + 512].astype(jnp.float32) + quintic_coef * square
         ).astype(jnp.bfloat16)
-    mixed = jnp.dot(poly[...], panel[...], preferred_element_type=jnp.float32)
-    return (linear_coef * panel[pl.ds(start, 256), :].astype(jnp.float32) + mixed).astype(
+    mixed = jnp.dot(poly[:count], panel[...], preferred_element_type=jnp.float32)
+    return (linear_coef * panel[pl.ds(start, count), :].astype(jnp.float32) + mixed).astype(
         jnp.bfloat16
     )
 
@@ -279,8 +279,8 @@
     strips, panel, gram, out, poly = refs[:12], *refs[12:]
     fill(gram, s_ref[0], strips[:6], 0)
     fill(gram, s_ref[0], strips[6:], 4)
-    for half in range(2):
-        out[256 * half : 256 * (half + 1)] = result_rows(gram, panel, poly, s_ref[1], half)
+    out[:256] = result_rows(gram, panel, poly, s_ref[1], 0, 0, 256)
+    out[256:] = result_rows(gram, panel, poly, s_ref[1], 1, 0, 128)
 
 
 def first_rows(scalars, strips, panel):
@@ -289,80 +289,88 @@
         first_kernel,
         out_shape=[
             jax.ShapeDtypeStruct((2048, 2048), jnp.bfloat16),
-            jax.ShapeDtypeStruct((512, cols), jnp.bfloat16),
+            jax.ShapeDtypeStruct((384, cols), jnp.bfloat16),
         ],
         in_specs=[pl.BlockSpec(memory_space=pltpu.SMEM)]
         + [pl.BlockSpec(memory_space=pltpu.VMEM)] * 13,
         out_specs=[pl.BlockSpec(memory_space=pltpu.VMEM)] * 2,
         scratch_shapes=[pltpu.VMEM((256, 2048), jnp.bfloat16)],
-        cost_estimate=cost(2 * 512 * 2048 * (2048 + cols), 3 * 10**7),
+        cost_estimate=cost(2 * 384 * 2048 * (2048 + cols), 3 * 10**7),
         compiler_params=pltpu.CompilerParams(**PARAMS),
         name="first_rows",
     )(scalars, *strips, panel)
 
 
-def near_kernel(s_ref, gram, panel, out, poly):
-    for half in range(2):
-        out[256 * half : 256 * (half + 1)] = result_rows(gram, panel, poly, s_ref[2], half)
-
-
-def near_rows(scalars, gram, panel):
+def more_kernel(scalar, parts, s_ref, gram, panel, *rest):
+    outs, poly = rest[:-1], rest[-1]
+    for part, out in zip(parts, outs, strict=True):
+        out[...] = result_rows(gram, panel, poly, s_ref[scalar], *part)
+
+
+def more_rows(scalar, parts, scalars, gram, panel):
     cols = panel.shape[-1]
-    return pl.pallas_call(
-        near_kernel,
-        out_shape=jax.ShapeDtypeStruct((512, cols), jnp.bfloat16),
+    rows = sum(part[2] for part in parts)
+    return pl.pallas_call(
+        functools.partial(more_kernel, scalar, parts),
+        out_shape=[jax.ShapeDtypeStruct((part[2], cols), jnp.bfloat16) for part in parts],
         in_specs=[pl.BlockSpec(memory_space=pltpu.SMEM)]
         + [pl.BlockSpec(memory_space=pltpu.VMEM)] * 2,
-        out_specs=pl.BlockSpec(memory_space=pltpu.VMEM),
+        out_specs=[pl.BlockSpec(memory_space=pltpu.VMEM)] * len(parts),
         scratch_shapes=[pltpu.VMEM((256, 2048), jnp.bfloat16)],
-        cost_estimate=cost(2 * 512 * 2048 * (2048 + cols), 10**7),
-        compiler_params=pltpu.CompilerParams(**PARAMS),
-        name="near_rows",
+        cost_estimate=cost(2 * rows * 2048 * (2048 + cols), 10**7),
+        compiler_params=pltpu.CompilerParams(**PARAMS),
+        name="more_rows",
     )(scalars, gram, panel)
 
 
-def hold_kernel(piece, out):
-    del piece, out
-
-
-def hold(piece):
+def hold_kernel(*refs):
+    del refs
+
+
+def hold(bytes_moved, piece, *earlier):
     return pl.pallas_call(
         hold_kernel,
         out_shape=jax.ShapeDtypeStruct(piece.shape, piece.dtype),
-        in_specs=[pl.BlockSpec(memory_space=pl.ANY)],
+        in_specs=[pl.BlockSpec(memory_space=pl.ANY)] * (1 + len(earlier)),
         out_specs=pl.BlockSpec(memory_space=pl.ANY),
         input_output_aliases={0: 0},
-        cost_estimate=cost(2 * 10**10, 10**6),
+        cost_estimate=cost(10**6, bytes_moved),
         compiler_params=pltpu.CompilerParams(**PARAMS),
         name="hold",
-    )(piece)
-
-
-def place_kernel(s_ref, near, far, out, sems):
+    )(piece, *earlier)
+
+
+def place_kernel(s_ref, far_first, far_second, near_own, near_other, out, sems):
     matrix, core = s_ref[3], s_ref[4]
-    copies = []
-    for piece, i in ((near, matrix), (far, 1 - matrix)):
-        for half, sub in enumerate((core, 1 - core)):
-            sem = sems.at[len(copies)]
-            copies.append(pltpu.make_async_copy(piece.at[half], out.at[i, :, sub], sem))
+    moves = (
+        (far_first.at[0:8], out.at[1 - matrix, :, core]),
+        (far_first.at[8:12], out.at[1 - matrix, 0:4, 1 - core]),
+        (far_second, out.at[1 - matrix, 4:8, 1 - core]),
+        (near_own, out.at[matrix, :, core]),
+        (near_other, out.at[matrix, :, 1 - core]),
+    )
+    copies = [
+        pltpu.make_async_copy(source, target, sems.at[k])
+        for k, (source, target) in enumerate(moves)
+    ]
     for copy in copies:
         copy.start()
     for copy in copies:
         copy.wait()
 
 
-def place_rows(scalars, near, far):
-    _, groups, rows, cols = near.shape
+def place_rows(scalars, *pieces):
+    _, rows, cols = pieces[0].shape
     return pl.pallas_call(
         place_kernel,
-        out_shape=jax.ShapeDtypeStruct((2, groups, 2, rows, cols), jnp.bfloat16),
+        out_shape=jax.ShapeDtypeStruct((2, 8, 2, rows, cols), jnp.bfloat16),
         in_specs=[pl.BlockSpec(memory_space=pltpu.SMEM)]
-        + [pl.BlockSpec(memory_space=pl.ANY)] * 2,
+        + [pl.BlockSpec(memory_space=pl.ANY)] * len(pieces),
         out_specs=pl.BlockSpec(memory_space=pl.ANY),
-        scratch_shapes=[pltpu.SemaphoreType.DMA((4,))],
+        scratch_shapes=[pltpu.SemaphoreType.DMA((5,))],
         compiler_params=pltpu.CompilerParams(**PARAMS),
         name="place_rows",
-    )(scalars, near, far)
+    )(scalars, *pieces)
 
 
 def home_far(m, r, c):
@@ -385,12 +393,14 @@
     other = send(own, other_core)
     keep, away, panel = gram_strips(scalars, *own_strips(own), own, other)
     strips = gather_strips(sum_strips(keep, away, 1.0 / cols))
-    gram, far = first_rows(scalars, strips, panel)
-    far = hold(send(far, home_far))
-    near = send(near_rows(scalars, gram, panel), home_near)
-    shape = (2, 8, 32, cols // CHIPS)
-    result = place_rows(scalars, near.reshape(shape), far.reshape(shape))
-    return result.reshape(mats, 512, cols // CHIPS)
+    gram, far_first = first_rows(scalars, strips, panel)
+    far_first = hold(4 * 10**7, send(far_first, home_far))
+    (far_second,) = more_rows(1, ((1, 128, 128),), scalars, gram, panel)
+    far_second = hold(10**7, send(far_second, home_far))
+    near = more_rows(2, ((0, 0, 256), (1, 0, 256)), scalars, gram, panel)
+    near = [send(piece, home_near) for piece in near]
+    pieces = [v.reshape(-1, 32, cols // CHIPS) for v in (far_first, far_second, *near)]
+    return place_rows(scalars, *pieces).reshape(mats, 512, cols // CHIPS)
 
 
 def solution(mesh):

time: 160 us -> 158 us (0.988)
  waiting for transfers between devices: 62.7 us -> 57.3 us
  starting transfers between devices: 19.4 us -> 22.2 us
    ppermute x24 -> x26, waiting for transfers between devices: 62.7 us -> 57.3 us  [send(): return lax.ppermute(value, AXES, perm)]
    ppermute x24 -> x26, starting transfers between devices: 19.4 us -> 22.2 us  [send(): return lax.ppermute(value, AXES, perm)]
    pallas_call x2 -> x3, Pallas kernels: 9.42 us -> 11.9 us  [the longest x2 10.1 us: more_rows(): pl.pallas_call(functools.partial(more_kernel, scalar, parts), out_shape=[...]
    pallas_call x1, Pallas kernels: 9.62 us -> 7.97 us  [first_rows(): pl.pallas_call(first_kernel, out_shape=[jax.ShapeDtypeStruct((2048, 2048)...]
  transfers between devices with their start and end apart: 24 -> 26, of which waited for: 13 -> 13; matrix products, arithmetic and copies ran while one was open for 0% -> 0% of each run, Pallas kernels for 6% -> 8%
where the time goes in v4:
time: 158 us
  waiting for transfers between devices  57.3 us (36%)
  blocking collectives  50.2 us (32%)
  Pallas kernels  26.1 us (17%)
  starting transfers between devices  22.2 us (14%)
  local copies, waits for them, and re-layouts  1.58 us (1%)
    ppermute x26, waiting for transfers between devices, send(): return lax.ppermute(value, AXES, perm)  57.3 us
    all_to_all x1, blocking collectives, fast_body(): own = lax.all_to_all(pieces, ('gr', 'mat', 'gc'), 0, 0, tiled=True)  50.2 us
    ppermute x26, starting transfers between devices, send(): return lax.ppermute(value, AXES, perm)  22.2 us
    pallas_call x2, Pallas kernels, more_rows(): pl.pallas_call(functools.partial(more_kernel, scalar, parts), out_shape=[...  10.1 us
    pallas_call x1, Pallas kernels, first_rows(): pl.pallas_call(first_kernel, out_shape=[jax.ShapeDtypeStruct((2048, 2048)...  7.97 us
    pallas_call x1, Pallas kernels, gram_strips(): pl.pallas_call(gram_kernel, out_shape=[jax.ShapeDtypeStruct(shape, jnp.fl...  3.48 us
  transfers between devices with their start and end apart: 26, of which 13 were waited for; matrix products, arithmetic and copies ran while one was open for 0% of the time, Pallas kernels for 8%

profile of v4, /device:TPU:0, one launch (start us, length us, event | category | flops | bytes accessed | tf_op | source)
XLA Modules:
  0.0 157.8 jit_solution(13352728661391943841)
XLA Ops:
  0.0 1.5 copy-done
  2.0 50.2 %all_to_all.5 = bf16[32,32,896]{2,1,0:T(8,128)(2,1)S(1)} all-to-all(bf16[32,32,896]{2,1,0:T(8,128)(2,1)S(1)} %bitcast.13), channel_id=1, replica_groups=mesh['mat'=4,'gr'=4,'gc'=2] {'gr','mat','gc'}, dimensions={0} | all-to-all | bytes 3670016 | tf_op jit(solution)/shard_map/all_to_all | solution.py:391
  52.3 1.7 %own_strips.1 = (f32[8,128,1152]{2,1,0:T(8,128)S(1)}, bf16[2048,896]{1,0:T(8,128)(2,1)S(1)}) custom-call(bf16[1024,896]{1,0:T(8,128)(2,1)S(1)} %bitcast.15), custom_call_target="tpu_custom_call" | custom-call | flops 1174405120 | bytes 10000000 | tf_op jit(solution)/shard_map/own_strips/pallas_call | solution.py:135
  54.0 2.1 %collective-permute-done.other = bf16[1024,896]{1,0:T(8,128)(2,1)} collective-permute-done((bf16[1024,896]{1,0:T(8,128)(2,1)S(1)}, bf16[1024,896]{1,0:T(8,128)(2,1)}, u32[]{:S(2)}, u32[]{:S(2)}) %collective-permute-start) | collective-permute-done | bytes 1835040 | tf_op jit(solution)/shard_map/ppermute | solution.py:75
  56.1 3.5 %gram_strips.1 = (f32[4,128,384]{2,1,0:T(8,128)S(1)}, f32[4,128,384]{2,1,0:T(8,128)S(1)}, f32[4,128,384]{2,1,0:T(8,128)S(1)}, bf16[4,128,384]{2,1,0:T(8,128)(2,1...) custom-call(s32[5]{0:T(128)S(1)} %stack.23.p_ref.s_ref, ...), custom_call_target="tpu_custom_call", output_to_operand_aliasing={{6}: (1, {}), {7}: (2, {})} | custom-call | flops 1174405120 | bytes 10000000 | tf_op jit(solution)/shard_map/gram_strips/pallas_call | solution.py:176
  59.6 1.6 collective-permute-start.1
  61.1 1.4 collective-permute-start.5
  62.6 8.2 %collective-permute-done.1.came = bf16[4,128,384]{2,1,0:T(8,128)(2,1)S(1)} collective-permute-done((bf16[4,128,384]{2,1,0:T(8,128)(2,1)S(1)}, bf16[4,128,384]{2,1,0:T(8,128)(2,1)S(1)}, u32[]{:S(2)}, u32[]{:S(2)}) %collective-permute-start.1) | collective-permute-done | bytes 393248 | tf_op jit(solution)/shard_map/ppermute | solution.py:75
  70.9 1.5 collective-permute-start.2
  74.2 2.8 %collective-permute-done.2.came = bf16[2,128,384]{2,1,0:T(8,128)(2,1)S(1)} collective-permute-done((bf16[2,128,384]{2,1,0:T(8,128)(2,1)S(1)}, bf16[2,128,384]{2,1,0:T(8,128)(2,1)S(1)}, u32[]{:S(2)}, u32[]{:S(2)}) %collective-permute-start.2) | collective-permute-done | bytes 196640 | tf_op jit(solution)/shard_map/ppermute | solution.py:75
  78.6 1.5 collective-permute-start.7
  80.7 2.1 %collective-permute-done.3.came = bf16[2,128,384]{2,1,0:T(8,128)(2,1)S(1)} collective-permute-done((bf16[2,128,384]{2,1,0:T(8,128)(2,1)S(1)}, bf16[2,128,384]{2,1,0:T(8,128)(2,1)S(1)}, u32[]{:S(2)}, u32[]{:S(2)}) %collective-permute-start.3) | collective-permute-done | bytes 196640 | tf_op jit(solution)/shard_map/ppermute | solution.py:75
  82.9 1.5 collective-permute-start.4
  85.5 1.8 %collective-permute-done.11.came = bf16[2,128,384]{2,1,0:T(8,128)(2,1)S(1)} collective-permute-done((bf16[2,128,384]{2,1,0:T(8,128)(2,1)S(1)}, bf16[2,128,384]{2,1,0:T(8,128)(2,1)S(1)}, u32[]{:S(2)}, u32[]{:S(2)}) %collective-permute-start.11) | collective-permute-done | bytes 196640 | tf_op jit(solution)/shard_map/ppermute | solution.py:75
  89.4 1.5 collective-permute-start.16
  92.0 3.2 %collective-permute-done.12 = bf16[2,128,384]{2,1,0:T(8,128)(2,1)S(1)} collective-permute-done((bf16[2,128,384]{2,1,0:T(8,128)(2,1)S(1)}, bf16[2,128,384]{2,1,0:T(8,128)(2,1)S(1)}, u32[]{:S(2)}, u32[]{:S(2)}) %collective-permute-start.12) | collective-permute-done | bytes 196640 | tf_op jit(solution)/shard_map/ppermute | solution.py:75
  96.4 3.9 %collective-permute-done.16.refs_6_ = bf16[4,128,384]{2,1,0:T(8,128)(2,1)S(1)} collective-permute-done((bf16[4,128,384]{2,1,0:T(8,128)(2,1)S(1)}, bf16[4,128,384]{2,1,0:T(8,128)(2,1)S(1)}, u32[]{:S(2)}, u32[]{:S(2)}) %collective-permute-start.16) | collective-permute-done | bytes 393248 | tf_op jit(solution)/shard_map/ppermute | solution.py:75
  100.9 1.7 %collective-permute-done.17.refs_7_ = bf16[4,128,384]{2,1,0:T(8,128)(2,1)S(1)} collective-permute-done((bf16[4,128,384]{2,1,0:T(8,128)(2,1)S(1)}, bf16[4,128,384]{2,1,0:T(8,128)(2,1)S(1)}, u32[]{:S(2)}, u32[]{:S(2)}) %collective-permute-start.17) | collective-permute-done | bytes 393248 | tf_op jit(solution)/shard_map/ppermute | solution.py:75
  105.1 8.0 %first_rows.1 = (bf16[2048,2048]{1,0:T(8,128)(2,1)S(1)}, bf16[384,896]{1,0:T(8,128)(2,1)S(1)}) custom-call(s32[5]{0:T(128)S(1)} %stack.23.p_ref.s_ref, bf16[4,128,384]{2,1,0:T(8,128)(2,1)S(1)} %pad_maximum_fusion.refs_0_, bf16[4,128,384]{2,1,0:T(8,128)(2,1)S(1)} %pad_maximum_fusion.1.refs_1_, bf16[4,128,384]{2,1,0:T(8,128)(2,1)S(1)} %pad_maximum_fusion.2.refs_2_, ...), custom_call_target="tpu_custom_call" | custom-call | flops 4630511616 | bytes 30000000 | tf_op jit(solution)/shard_map/first_rows/pallas_call | solution.py:288
  113.9 7.6 %more_rows.3 = (bf16[256,896]{1,0:T(8,128)(2,1)S(1)}, bf16[256,896]{1,0:T(8,128)(2,1)S(1)}) custom-call(s32[5]{0:T(128)S(1)} %stack.23.p_ref.s_ref, bf16[2048,2048]{1,0:T(8,128)(2,1)S(1)} %get-tuple-element.52.gram, bf16[2048,896]{1,0:T(8,128)(2,1)S(1)} %get-tuple-element.50.refs_12_.panel), custom_call_target="tpu_custom_call" | custom-call | flops 6174015488 | bytes 10000000 | tf_op jit(solution)/shard_map/more_rows/pallas_call | solution.py:313
  123.0 2.4 %more_rows.2 = bf16[128,896]{1,0:T(8,128)(2,1)S(1)} custom-call(s32[5]{0:T(128)S(1)} %stack.23.p_ref.s_ref, bf16[2048,2048]{1,0:T(8,128)(2,1)S(1)} %get-tuple-element.52.gram, bf16[2048,896]{1,0:T(8,128)(2,1)S(1)} %get-tuple-element.50.refs_12_.panel), custom_call_target="tpu_custom_call" | custom-call | flops 1543503872 | bytes 10000000 | tf_op jit(solution)/shard_map/more_rows/pallas_call | solution.py:313
  125.4 2.2 %collective-permute-start.23 = (bf16[128,896]{1,0:T(8,128)(2,1)S(1)}, bf16[128,896]{1,0:T(8,128)(2,1)S(1)}, u32[]{:S(2)}, u32[]{:S(2)}) collective-permute-start(bf16[128,896]{1,0:T(8,128)(2,1)S(1)} %more_rows.2), channel_id=1, source_target_pairs={{0,4},{1,6},{2,5},{3,7},{4,0},{5,2},{6,1},{7,3},{8,12},{9,14},{10,... | collective-permute-start | bytes 688136 | tf_op jit(solution)/shard_map/ppermute | solution.py:75
  127.6 28.3 %collective-permute-done.23.refs_0_ = bf16[128,896]{1,0:T(8,128)(2,1)S(1)} collective-permute-done((bf16[128,896]{1,0:T(8,128)(2,1)S(1)}, bf16[128,896]{1,0:T(8,128)(2,1)S(1)}, u32[]{:S(2)}, u32[]{:S(2)}) %collective-permute-start.23) | collective-permute-done | bytes 229408 | tf_op jit(solution)/shard_map/ppermute | solution.py:75
  155.9 1.8 %place_rows.1 = bf16[2,8,2,32,896]{4,3,2,1,0:T(8,128)(2,1)} custom-call(s32[5]{0:T(128)S(1)} %stack.23.p_ref.s_ref, bf16[12,32,896]{2,1,0:T(8,128)(2,1)S(1)} %bitcast.17, bf16[4,32,896]{2,1,0:T(8,128)(2,1)S(1)} %bitcast.19, bf16[8,32,896]{2,1,0:T(8,128)(2,1)S(1)} %bitcast.20, bf16[8,32,896]{2,1,0:T(8,128)(2,1)S(1)} %bitcast.21), custom_call_target="tpu_custom_call" | custom-call | tf_op jit(solution)/shard_map/place_rows/pallas_call | solution.py:364
  (53 shorter events, 15.5 us)
Async XLA Ops:
  52.2 3.9 %collective-permute-start = (bf16[1024,896]{1,0:T(8,128)(2,1)S(1)}, bf16[1024,896]{1,0:T(8,128)(2,1)}, u32[]{:S(2)}, u32[]{:S(2)}) collective-permute-start(bf16[1024,896]{1,0:T(8,128)(2,1)S(1)} %bitcast.14), channel_id=1, source_target_pairs={{0,1},{1,0},{2,3},{3,2},{4,5},{5,4},{6,7},{7,6},{8,9},{9,8},{10,11... | collective-permute-start | bytes 5505032 | tf_op jit(solution)/shard_map/ppermute | solution.py:75
  59.6 11.2 %collective-permute-start.1 = (bf16[4,128,384]{2,1,0:T(8,128)(2,1)S(1)}, bf16[4,128,384]{2,1,0:T(8,128)(2,1)S(1)}, u32[]{:S(2)}, u32[]{:S(2)}) collective-permute-start(bf16[4,128,384]{2,1,0:T(8,128)(2,1)S(1)} %get-tuple-element.33), channel_id=1, source_target_pairs={{0,8},{1,9},{2,10},{3,11},{4,12},{5,13},{6,14},{7,15},{8,0},{9,1},... | collective-permute-start | bytes 1179656 | tf_op jit(solution)/shard_map/ppermute | solution.py:75
  61.1 11.3 %collective-permute-start.5 = (bf16[4,128,384]{2,1,0:T(8,128)(2,1)S(1)}, bf16[4,128,384]{2,1,0:T(8,128)(2,1)S(1)}, u32[]{:S(2)}, u32[]{:S(2)}) collective-permute-start(bf16[4,128,384]{2,1,0:T(8,128)(2,1)S(1)} %get-tuple-element.39), channel_id=1, source_target_pairs={{0,16},{1,17},{2,18},{3,19},{4,20},{5,21},{6,22},{7,23},{8,24},{9,... | collective-permute-start | bytes 1179656 | tf_op jit(solution)/shard_map/ppermute | solution.py:75
  62.6 10.9 %collective-permute-start.9 = (bf16[4,128,384]{2,1,0:T(8,128)(2,1)S(1)}, bf16[4,128,384]{2,1,0:T(8,128)(2,1)S(1)}, u32[]{:S(2)}, u32[]{:S(2)}) collective-permute-start(bf16[4,128,384]{2,1,0:T(8,128)(2,1)S(1)} %get-tuple-element.45), channel_id=1, source_target_pairs={{0,2},{1,3},{2,0},{3,1},{4,6},{5,7},{6,4},{7,5},{8,10},{9,11},{10,... | collective-permute-start | bytes 1179656 | tf_op jit(solution)/shard_map/ppermute | solution.py:75
  70.9 6.2 %collective-permute-start.2 = (bf16[2,128,384]{2,1,0:T(8,128)(2,1)S(1)}, bf16[2,128,384]{2,1,0:T(8,128)(2,1)S(1)}, u32[]{:S(2)}, u32[]{:S(2)}) collective-permute-start(bf16[2,128,384]{2,1,0:T(8,128)(2,1)S(1)} %get-tuple-element.35), channel_id=1, source_target_pairs={{0,16},{1,17},{2,18},{3,19},{4,20},{5,21},{6,22},{7,23},{8,24},{9,... | collective-permute-start | bytes 589832 | tf_op jit(solution)/shard_map/ppermute | solution.py:75
  72.5 6.1 %collective-permute-start.6 = (bf16[2,128,384]{2,1,0:T(8,128)(2,1)S(1)}, bf16[2,128,384]{2,1,0:T(8,128)(2,1)S(1)}, u32[]{:S(2)}, u32[]{:S(2)}) collective-permute-start(bf16[2,128,384]{2,1,0:T(8,128)(2,1)S(1)} %get-tuple-element.41), channel_id=1, source_target_pairs={{0,2},{1,3},{2,0},{3,1},{4,6},{5,7},{6,4},{7,5},{8,10},{9,11},{10,... | collective-permute-start | bytes 589832 | tf_op jit(solution)/shard_map/ppermute | solution.py:75
  73.6 6.6 %collective-permute-start.10 = (bf16[2,128,384]{2,1,0:T(8,128)(2,1)S(1)}, bf16[2,128,384]{2,1,0:T(8,128)(2,1)S(1)}, u32[]{:S(2)}, u32[]{:S(2)}) collective-permute-start(bf16[2,128,384]{2,1,0:T(8,128)(2,1)S(1)} %get-tuple-element.47), channel_id=1, source_target_pairs={{0,8},{1,9},{2,10},{3,11},{4,12},{5,13},{6,14},{7,15},{8,0},{9,1},... | collective-permute-start | bytes 589832 | tf_op jit(solution)/shard_map/ppermute | solution.py:75
  77.1 5.7 %collective-permute-start.3 = (bf16[2,128,384]{2,1,0:T(8,128)(2,1)S(1)}, bf16[2,128,384]{2,1,0:T(8,128)(2,1)S(1)}, u32[]{:S(2)}, u32[]{:S(2)}) collective-permute-start(bf16[2,128,384]{2,1,0:T(8,128)(2,1)S(1)} %get-tuple-element.37), channel_id=1, source_target_pairs={{0,2},{1,3},{2,0},{3,1},{4,6},{5,7},{6,4},{7,5},{8,10},{9,11},{10,... | collective-permute-start | bytes 589832 | tf_op jit(solution)/shard_map/ppermute | solution.py:75
  78.6 5.8 %collective-permute-start.7 = (bf16[2,128,384]{2,1,0:T(8,128)(2,1)S(1)}, bf16[2,128,384]{2,1,0:T(8,128)(2,1)S(1)}, u32[]{:S(2)}, u32[]{:S(2)}) collective-permute-start(bf16[2,128,384]{2,1,0:T(8,128)(2,1)S(1)} %get-tuple-element.43), channel_id=1, source_target_pairs={{0,8},{1,9},{2,10},{3,11},{4,12},{5,13},{6,14},{7,15},{8,0},{9,1},... | collective-permute-start | bytes 589832 | tf_op jit(solution)/shard_map/ppermute | solution.py:75
  80.2 7.0 %collective-permute-start.11 = (bf16[2,128,384]{2,1,0:T(8,128)(2,1)S(1)}, bf16[2,128,384]{2,1,0:T(8,128)(2,1)S(1)}, u32[]{:S(2)}, u32[]{:S(2)}) collective-permute-start(bf16[2,128,384]{2,1,0:T(8,128)(2,1)S(1)} %get-tuple-element.49), channel_id=1, source_target_pairs={{0,16},{1,17},{2,18},{3,19},{4,20},{5,21},{6,22},{7,23},{8,24},{9,... | collective-permute-start | bytes 589832 | tf_op jit(solution)/shard_map/ppermute | solution.py:75
  82.9 6.5 %collective-permute-start.4 = (bf16[2,128,384]{2,1,0:T(8,128)(2,1)S(1)}, bf16[2,128,384]{2,1,0:T(8,128)(2,1)S(1)}, u32[]{:S(2)}, u32[]{:S(2)}) collective-permute-start(bf16[2,128,384]{2,1,0:T(8,128)(2,1)S(1)} %add_last.3), channel_id=1, source_target_pairs={{0,16},{1,17},{2,18},{3,19},{4,20},{5,21},{6,22},{7,23},{8,24},{9,... | collective-permute-start | bytes 589832 | tf_op jit(solution)/shard_map/ppermute | solution.py:75
  84.5 6.4 %collective-permute-start.8 = (bf16[2,128,384]{2,1,0:T(8,128)(2,1)S(1)}, bf16[2,128,384]{2,1,0:T(8,128)(2,1)S(1)}, u32[]{:S(2)}, u32[]{:S(2)}) collective-permute-start(bf16[2,128,384]{2,1,0:T(8,128)(2,1)S(1)} %add_last.4), channel_id=1, source_target_pairs={{0,2},{1,3},{2,0},{3,1},{4,6},{5,7},{6,4},{7,5},{8,10},{9,11},{10,... | collective-permute-start | bytes 589832 | tf_op jit(solution)/shard_map/ppermute | solution.py:75
  87.3 7.9 %collective-permute-start.12 = (bf16[2,128,384]{2,1,0:T(8,128)(2,1)S(1)}, bf16[2,128,384]{2,1,0:T(8,128)(2,1)S(1)}, u32[]{:S(2)}, u32[]{:S(2)}) collective-permute-start(bf16[2,128,384]{2,1,0:T(8,128)(2,1)S(1)} %add_last.5), channel_id=1, source_target_pairs={{0,8},{1,9},{2,10},{3,11},{4,12},{5,13},{6,14},{7,15},{8,0},{9,1},... | collective-permute-start | bytes 589832 | tf_op jit(solution)/shard_map/ppermute | solution.py:75
  89.4 10.9 %collective-permute-start.16 = (bf16[4,128,384]{2,1,0:T(8,128)(2,1)S(1)}, bf16[4,128,384]{2,1,0:T(8,128)(2,1)S(1)}, u32[]{:S(2)}, u32[]{:S(2)}) collective-permute-start(bf16[4,128,384]{2,1,0:T(8,128)(2,1)S(1)} %pad_maximum_fusion.refs_0_), channel_id=1, source_target_pairs={{0,8},{1,9},{2,10},{3,11},{4,12},{5,13},{6,14},{7,15},{8,0},{9,1},... | collective-permute-start | bytes 1179656 | tf_op jit(solution)/shard_map/ppermute | solution.py:75
  90.9 9.5 %collective-permute-start.13 = (bf16[4,128,384]{2,1,0:T(8,128)(2,1)S(1)}, bf16[4,128,384]{2,1,0:T(8,128)(2,1)S(1)}, u32[]{:S(2)}, u32[]{:S(2)}) collective-permute-start(bf16[4,128,384]{2,1,0:T(8,128)(2,1)S(1)} %pad_maximum_fusion.refs_0_), channel_id=1, source_target_pairs={{0,1},{1,0},{2,3},{3,2},{4,5},{5,4},{6,7},{7,6},{8,9},{9,8},{10,11... | collective-permute-start | bytes 1179656 | tf_op jit(solution)/shard_map/ppermute | solution.py:75
  90.9 11.6 %collective-permute-start.17 = (bf16[4,128,384]{2,1,0:T(8,128)(2,1)S(1)}, bf16[4,128,384]{2,1,0:T(8,128)(2,1)S(1)}, u32[]{:S(2)}, u32[]{:S(2)}) collective-permute-start(bf16[4,128,384]{2,1,0:T(8,128)(2,1)S(1)} %pad_maximum_fusion.1.refs_1_), channel_id=1, source_target_pairs={{0,16},{1,17},{2,18},{3,19},{4,20},{5,21},{6,22},{7,23},{8,24},{9,... | collective-permute-start | bytes 1179656 | tf_op jit(solution)/shard_map/ppermute | solution.py:75
  95.2 8.1 %collective-permute-start.18 = (bf16[4,128,384]{2,1,0:T(8,128)(2,1)S(1)}, bf16[4,128,384]{2,1,0:T(8,128)(2,1)S(1)}, u32[]{:S(2)}, u32[]{:S(2)}) collective-permute-start(bf16[4,128,384]{2,1,0:T(8,128)(2,1)S(1)} %pad_maximum_fusion.2.refs_2_), channel_id=1, source_target_pairs={{0,2},{1,3},{2,0},{3,1},{4,6},{5,7},{6,4},{7,5},{8,10},{9,11},{10,... | collective-permute-start | bytes 1179656 | tf_op jit(solution)/shard_map/ppermute | solution.py:75
  96.4 7.0 %collective-permute-start.14 = (bf16[4,128,384]{2,1,0:T(8,128)(2,1)S(1)}, bf16[4,128,384]{2,1,0:T(8,128)(2,1)S(1)}, u32[]{:S(2)}, u32[]{:S(2)}) collective-permute-start(bf16[4,128,384]{2,1,0:T(8,128)(2,1)S(1)} %pad_maximum_fusion.1.refs_1_), channel_id=1, source_target_pairs={{0,1},{1,0},{2,3},{3,2},{4,5},{5,4},{6,7},{7,6},{8,9},{9,8},{10,11... | collective-permute-start | bytes 1179656 | tf_op jit(solution)/shard_map/ppermute | solution.py:75
  100.4 3.0 %collective-permute-start.15 = (bf16[4,128,384]{2,1,0:T(8,128)(2,1)S(1)}, bf16[4,128,384]{2,1,0:T(8,128)(2,1)S(1)}, u32[]{:S(2)}, u32[]{:S(2)}) collective-permute-start(bf16[4,128,384]{2,1,0:T(8,128)(2,1)S(1)} %pad_maximum_fusion.2.refs_2_), channel_id=1, source_target_pairs={{0,1},{1,0},{2,3},{3,2},{4,5},{5,4},{6,7},{7,6},{8,9},{9,8},{10,11... | collective-permute-start | bytes 1179656 | tf_op jit(solution)/shard_map/ppermute | solution.py:75
  100.4 3.0 %collective-permute-start.19 = (bf16[4,128,384]{2,1,0:T(8,128)(2,1)S(1)}, bf16[4,128,384]{2,1,0:T(8,128)(2,1)S(1)}, u32[]{:S(2)}, u32[]{:S(2)}) collective-permute-start(bf16[4,128,384]{2,1,0:T(8,128)(2,1)S(1)} %collective-permute-done.16.refs_6_), channel_id=1, source_target_pairs={{0,1},{1,0},{2,3},{3,2},{4,5},{5,4},{6,7},{7,6},{8,9},{9,8},{10,11... | collective-permute-start | bytes 1179656 | tf_op jit(solution)/shard_map/ppermute | solution.py:75
  113.0 42.8 %collective-permute-start.22 = (bf16[384,896]{1,0:T(8,128)(2,1)S(1)}, bf16[384,896]{1,0:T(8,128)(2,1)S(1)}, u32[]{:S(2)}, u32[]{:S(2)}) collective-permute-start(bf16[384,896]{1,0:T(8,128)(2,1)S(1)} %get-tuple-element.51), channel_id=1, source_target_pairs={{0,4},{1,6},{2,5},{3,7},{4,0},{5,2},{6,1},{7,3},{8,12},{9,14},{10,... | collective-permute-start | bytes 2064392 | tf_op jit(solution)/shard_map/ppermute | solution.py:75
  121.6 34.3 %collective-permute-start.24 = (bf16[256,896]{1,0:T(8,128)(2,1)S(1)}, bf16[256,896]{1,0:T(8,128)(2,1)S(1)}, u32[]{:S(2)}, u32[]{:S(2)}) collective-permute-start(bf16[256,896]{1,0:T(8,128)(2,1)S(1)} %get-tuple-element.53), channel_id=1, source_target_pairs={{0,0},{1,2},{2,1},{3,3},{4,4},{5,6},{6,5},{7,7},{8,8},{9,10},{10,9... | collective-permute-start | bytes 1376264 | tf_op jit(solution)/shard_map/ppermute | solution.py:75
  122.3 33.6 %collective-permute-start.25 = (bf16[256,896]{1,0:T(8,128)(2,1)S(1)}, bf16[256,896]{1,0:T(8,128)(2,1)S(1)}, u32[]{:S(2)}, u32[]{:S(2)}) collective-permute-start(bf16[256,896]{1,0:T(8,128)(2,1)S(1)} %get-tuple-element.54), channel_id=1, source_target_pairs={{0,0},{1,2},{2,1},{3,3},{4,4},{5,6},{6,5},{7,7},{8,8},{9,10},{10,9... | collective-permute-start | bytes 1376264 | tf_op jit(solution)/shard_map/ppermute | solution.py:75
  125.4 30.4 %collective-permute-start.23 = (bf16[128,896]{1,0:T(8,128)(2,1)S(1)}, bf16[128,896]{1,0:T(8,128)(2,1)S(1)}, u32[]{:S(2)}, u32[]{:S(2)}) collective-permute-start(bf16[128,896]{1,0:T(8,128)(2,1)S(1)} %more_rows.2), channel_id=1, source_target_pairs={{0,4},{1,6},{2,5},{3,7},{4,0},{5,2},{6,1},{7,3},{8,12},{9,14},{10,... | collective-permute-start | bytes 688136 | tf_op jit(solution)/shard_map/ppermute | solution.py:75
  (3 other events, 4.9 us)

commit v5 on v4

--- a/solution.py
+++ b/solution.py
@@ -237,13 +237,13 @@
     return [sum_third(third, keep[third], away[third], scale) for third in range(3)]
 
 
-def gather_strips(parts):
+def gather_strips(scalars, parts):
     came = [send(parts[i], across(ORDERS[i][1])) for i in range(3)]
     early = [jnp.concatenate([parts[i], came[i]], axis=0) for i in range(3)]
     late = [send(early[i], across(ORDERS[i][0])) for i in range(3)]
     early += [send(part, other_core) for part in early]
-    late += [send(part, other_core) for part in late]
-    return early + late
+    gram = early_gram(scalars, early, late[0])
+    return gram, late + [send(part, other_core) for part in late]
 
 
 def fill(gram, p, thirds, first_place):
@@ -261,6 +261,24 @@
                     gram[col_at, row_at] = block.T
 
 
+def early_kernel(s_ref, *refs):
+    fill(refs[7], s_ref[0], refs[:6], 0)
+
+
+def early_gram(scalars, early, first_late):
+    return pl.pallas_call(
+        early_kernel,
+        out_shape=jax.ShapeDtypeStruct((2048, 2048), jnp.bfloat16),
+        in_specs=[pl.BlockSpec(memory_space=pltpu.SMEM)]
+        + [pl.BlockSpec(memory_space=pltpu.VMEM)] * 6
+        + [pl.BlockSpec(memory_space=pl.ANY)],
+        out_specs=pl.BlockSpec(memory_space=pltpu.VMEM),
+        cost_estimate=cost(10**5, 3 * 10**7),
+        compiler_params=pltpu.CompilerParams(**PARAMS),
+        name="early_gram",
+    )(scalars, *early, first_late)
+
+
 def result_rows(gram, panel, poly, place, half, first, count):
     start = pl.multiple_of(1024 * half + place * 256 + first, BLOCK)
     rows = gram[pl.ds(start, count), :]
@@ -276,14 +294,14 @@
 
 
 def first_kernel(s_ref, *refs):
-    strips, panel, gram, out, poly = refs[:12], *refs[12:]
-    fill(gram, s_ref[0], strips[:6], 0)
-    fill(gram, s_ref[0], strips[6:], 4)
+    late, gram_in, panel, gram, out, poly = refs[:6], *refs[6:]
+    del gram_in
+    fill(gram, s_ref[0], late, 4)
     out[:256] = result_rows(gram, panel, poly, s_ref[1], 0, 0, 256)
     out[256:] = result_rows(gram, panel, poly, s_ref[1], 1, 0, 128)
 
 
-def first_rows(scalars, strips, panel):
+def first_rows(scalars, gram, late, panel):
     cols = panel.shape[-1]
     return pl.pallas_call(
         first_kernel,
@@ -292,13 +310,14 @@
             jax.ShapeDtypeStruct((384, cols), jnp.bfloat16),
         ],
         in_specs=[pl.BlockSpec(memory_space=pltpu.SMEM)]
-        + [pl.BlockSpec(memory_space=pltpu.VMEM)] * 13,
+        + [pl.BlockSpec(memory_space=pltpu.VMEM)] * 8,
         out_specs=[pl.BlockSpec(memory_space=pltpu.VMEM)] * 2,
         scratch_shapes=[pltpu.VMEM((256, 2048), jnp.bfloat16)],
+        input_output_aliases={7: 0},
         cost_estimate=cost(2 * 384 * 2048 * (2048 + cols), 3 * 10**7),
         compiler_params=pltpu.CompilerParams(**PARAMS),
         name="first_rows",
-    )(scalars, *strips, panel)
+    )(scalars, *late, gram, panel)
 
 
 def more_kernel(scalar, parts, s_ref, gram, panel, *rest):
@@ -392,8 +411,8 @@
     own = own.reshape(1024, cols // CHIPS)
     other = send(own, other_core)
     keep, away, panel = gram_strips(scalars, *own_strips(own), own, other)
-    strips = gather_strips(sum_strips(keep, away, 1.0 / cols))
-    gram, far_first = first_rows(scalars, strips, panel)
+    gram, late = gather_strips(scalars, sum_strips(keep, away, 1.0 / cols))
+    gram, far_first = first_rows(scalars, gram, late, panel)
     far_first = hold(4 * 10**7, send(far_first, home_far))
     (far_second,) = more_rows(1, ((1, 128, 128),), scalars, gram, panel)
     far_second = hold(10**7, send(far_second, home_far))

time: 158 us -> 157 us (level)
  waiting for transfers between devices: 57.3 us -> 55.4 us
    ppermute x26, waiting for transfers between devices: 57.3 us -> 55.4 us  [send(): return lax.ppermute(value, AXES, perm)]
    pallas_call x0 -> x1, Pallas kernels: none -> 1.66 us  [early_gram(): pl.pallas_call(early_kernel, out_shape=jax.ShapeDtypeStruct((2048, 2048),...]
  transfers between devices with their start and end apart: 26 -> 26, of which waited for: 13 -> 12; matrix products, arithmetic and copies ran while one was open for 0% -> 0% of each run, Pallas kernels for 8% -> 9%
where the time goes in v5:
time: 157 us; the launch traced here: 156 us
  waiting for transfers between devices  55.4 us (35%)
  blocking collectives  50.2 us (32%)
  Pallas kernels  26.6 us (17%)
  starting transfers between devices  22.2 us (14%)
  local copies, waits for them, and re-layouts  1.58 us (1%)
    ppermute x26, waiting for transfers between devices, send(): return lax.ppermute(value, AXES, perm)  55.4 us
    all_to_all x1, blocking collectives, fast_body(): own = lax.all_to_all(pieces, ('gr', 'mat', 'gc'), 0, 0, tiled=True)  50.2 us
    ppermute x26, starting transfers between devices, send(): return lax.ppermute(value, AXES, perm)  22.2 us
    pallas_call x2, Pallas kernels, more_rows(): pl.pallas_call(functools.partial(more_kernel, scalar, parts), out_shape=[...  10 us
    pallas_call x1, Pallas kernels, first_rows(): pl.pallas_call(first_kernel, out_shape=[jax.ShapeDtypeStruct((2048, 2048)...  6.86 us
    pallas_call x1, Pallas kernels, gram_strips(): pl.pallas_call(gram_kernel, out_shape=[jax.ShapeDtypeStruct(shape, jnp.fl...  3.48 us
  transfers between devices with their start and end apart: 26, of which 12 were waited for; matrix products, arithmetic and copies ran while one was open for 0% of the time, Pallas kernels for 9%

profile of v5, /device:TPU:0, one launch (start us, length us, event | category | flops | bytes accessed | tf_op | source)
XLA Modules:
  0.0 156.5 jit_solution(8174212647070034465)
XLA Ops:
  0.0 1.5 copy-done
  2.0 50.2 %all_to_all.5 = bf16[32,32,896]{2,1,0:T(8,128)(2,1)S(1)} all-to-all(bf16[32,32,896]{2,1,0:T(8,128)(2,1)S(1)} %bitcast.13), channel_id=1, replica_groups=mesh['mat'=4,'gr'=4,'gc'=2] {'gr','mat','gc'}, dimensions={0} | all-to-all | bytes 3670016 | tf_op jit(solution)/shard_map/all_to_all | solution.py:410
  52.3 1.7 %own_strips.1 = (f32[8,128,1152]{2,1,0:T(8,128)S(1)}, bf16[2048,896]{1,0:T(8,128)(2,1)S(1)}) custom-call(bf16[1024,896]{1,0:T(8,128)(2,1)S(1)} %bitcast.15), custom_call_target="tpu_custom_call" | custom-call | flops 1174405120 | bytes 10000000 | tf_op jit(solution)/shard_map/own_strips/pallas_call | solution.py:135
  54.0 2.1 %collective-permute-done.other = bf16[1024,896]{1,0:T(8,128)(2,1)} collective-permute-done((bf16[1024,896]{1,0:T(8,128)(2,1)S(1)}, bf16[1024,896]{1,0:T(8,128)(2,1)}, u32[]{:S(2)}, u32[]{:S(2)}) %collective-permute-start) | collective-permute-done | bytes 1835040 | tf_op jit(solution)/shard_map/ppermute | solution.py:75
  56.1 3.5 %gram_strips.1 = (f32[4,128,384]{2,1,0:T(8,128)S(1)}, f32[4,128,384]{2,1,0:T(8,128)S(1)}, f32[4,128,384]{2,1,0:T(8,128)S(1)}, bf16[4,128,384]{2,1,0:T(8,128)(2,1...) custom-call(s32[5]{0:T(128)S(1)} %stack.23.p_ref.s_ref, ...), custom_call_target="tpu_custom_call", output_to_operand_aliasing={{6}: (1, {}), {7}: (2, {})} | custom-call | flops 1174405120 | bytes 10000000 | tf_op jit(solution)/shard_map/gram_strips/pallas_call | solution.py:176
  59.6 1.6 %collective-permute-start.1 = (bf16[4,128,384]{2,1,0:T(8,128)(2,1)S(1)}, bf16[4,128,384]{2,1,0:T(8,128)(2,1)S(1)}, u32[]{:S(2)}, u32[]{:S(2)}) collective-permute-start(bf16[4,128,384]{2,1,0:T(8,128)(2,1)S(1)} %get-tuple-element.33), channel_id=1, source_target_pairs={{0,8},{1,9},{2,10},{3,11},{4,12},{5,13},{6,14},{7,15},{8,0},{9,1},... | collective-permute-start | bytes 1179656 | tf_op jit(solution)/shard_map/ppermute | solution.py:75
  61.1 1.4 collective-permute-start.6
  62.6 8.2 %collective-permute-done.1.came = bf16[4,128,384]{2,1,0:T(8,128)(2,1)S(1)} collective-permute-done((bf16[4,128,384]{2,1,0:T(8,128)(2,1)S(1)}, bf16[4,128,384]{2,1,0:T(8,128)(2,1)S(1)}, u32[]{:S(2)}, u32[]{:S(2)}) %collective-permute-start.1) | collective-permute-done | bytes 393248 | tf_op jit(solution)/shard_map/ppermute | solution.py:75
  70.9 1.5 collective-permute-start.2
  74.3 2.8 %collective-permute-done.2.came = bf16[2,128,384]{2,1,0:T(8,128)(2,1)S(1)} collective-permute-done((bf16[2,128,384]{2,1,0:T(8,128)(2,1)S(1)}, bf16[2,128,384]{2,1,0:T(8,128)(2,1)S(1)}, u32[]{:S(2)}, u32[]{:S(2)}) %collective-permute-start.2) | collective-permute-done | bytes 196640 | tf_op jit(solution)/shard_map/ppermute | solution.py:75
  77.1 1.4 collective-permute-start.3
  78.7 1.5 collective-permute-start.8
  80.7 2.1 %collective-permute-done.3.came = bf16[2,128,384]{2,1,0:T(8,128)(2,1)S(1)} collective-permute-done((bf16[2,128,384]{2,1,0:T(8,128)(2,1)S(1)}, bf16[2,128,384]{2,1,0:T(8,128)(2,1)S(1)}, u32[]{:S(2)}, u32[]{:S(2)}) %collective-permute-start.3) | collective-permute-done | bytes 196640 | tf_op jit(solution)/shard_map/ppermute | solution.py:75
  82.9 1.5 collective-permute-start.4
  85.5 1.8 %collective-permute-done.13.came = bf16[2,128,384]{2,1,0:T(8,128)(2,1)S(1)} collective-permute-done((bf16[2,128,384]{2,1,0:T(8,128)(2,1)S(1)}, bf16[2,128,384]{2,1,0:T(8,128)(2,1)S(1)}, u32[]{:S(2)}, u32[]{:S(2)}) %collective-permute-start.13) | collective-permute-done | bytes 196640 | tf_op jit(solution)/shard_map/ppermute | solution.py:75
  89.5 1.5 collective-permute-start.5
  95.2 6.3 %collective-permute-done.5.refs_6_.refs_0_ = bf16[4,128,384]{2,1,0:T(8,128)(2,1)S(1)} collective-permute-done((bf16[4,128,384]{2,1,0:T(8,128)(2,1)S(1)}, bf16[4,128,384]{2,1,0:T(8,128)(2,1)S(1)}, u32[]{:S(2)}, u32[]{:S(2)}) %collective-permute-start.5) | collective-permute-done | bytes 393248 | tf_op jit(solution)/shard_map/ppermute | solution.py:75
  103.1 1.7 %early_gram.1.refs_6_ = bf16[2048,2048]{1,0:T(8,128)(2,1)S(1)} custom-call(s32[5]{0:T(128)S(1)} %stack.23.p_ref.s_ref, bf16[4,128,384]{2,1,0:T(8,128)(2,1)S(1)} %pad_maximum_fusion.refs_0_, bf16[4,128,384]{2,1,0:T(8,128)(2,1)S(1)} %pad_maximum_fusion.1.refs_1_, bf16[4,128,384]{2,1,0:T(8,128)(2,1)S(1)} %pad_maximum_fusion.2.refs_2_, ...), custom_call_target="tpu_custom_call" | custom-call | flops 100000 | bytes 30000000 | tf_op jit(solution)/shard_map/early_gram/pallas_call | solution.py:269
  104.8 6.9 %first_rows.1 = (bf16[2048,2048]{1,0:T(8,128)(2,1)S(1)}, bf16[384,896]{1,0:T(8,128)(2,1)S(1)}) custom-call(s32[5]{0:T(128)S(1)} %stack.23.p_ref.s_ref, bf16[4,128,384]{2,1,0:T(8,128)(2,1)S(1)} %collective-permute-done.5.refs_6_.refs_0_, bf16[4,128,384]{2,1,0:T(8,128)(2,1)S(1)} %collective-permute-done.10.refs_1_, ...), custom_call_target="tpu_custom_call", output_to_operand_aliasing={{0}: (7, {})} | custom-call | flops 4630511616 | bytes 30000000 | tf_op jit(solution)/shard_map/first_rows/pallas_call | solution.py:306
  112.4 7.6 %more_rows.3 = (bf16[256,896]{1,0:T(8,128)(2,1)S(1)}, bf16[256,896]{1,0:T(8,128)(2,1)S(1)}) custom-call(s32[5]{0:T(128)S(1)} %stack.23.p_ref.s_ref, bf16[2048,2048]{1,0:T(8,128)(2,1)S(1)} %get-tuple-element.52.gram, bf16[2048,896]{1,0:T(8,128)(2,1)S(1)} %get-tuple-element.50.refs_7_.panel), custom_call_target="tpu_custom_call" | custom-call | flops 6174015488 | bytes 10000000 | tf_op jit(solution)/shard_map/more_rows/pallas_call | solution.py:332
  121.4 2.4 %more_rows.2 = bf16[128,896]{1,0:T(8,128)(2,1)S(1)} custom-call(s32[5]{0:T(128)S(1)} %stack.23.p_ref.s_ref, bf16[2048,2048]{1,0:T(8,128)(2,1)S(1)} %get-tuple-element.52.gram, bf16[2048,896]{1,0:T(8,128)(2,1)S(1)} %get-tuple-element.50.refs_7_.panel), custom_call_target="tpu_custom_call" | custom-call | flops 1543503872 | bytes 10000000 | tf_op jit(solution)/shard_map/more_rows/pallas_call | solution.py:332
  123.8 2.4 %collective-permute-start.23 = (bf16[128,896]{1,0:T(8,128)(2,1)S(1)}, bf16[128,896]{1,0:T(8,128)(2,1)S(1)}, u32[]{:S(2)}, u32[]{:S(2)}) collective-permute-start(bf16[128,896]{1,0:T(8,128)(2,1)S(1)} %more_rows.2), channel_id=1, source_target_pairs={{0,4},{1,6},{2,5},{3,7},{4,0},{5,2},{6,1},{7,3},{8,12},{9,14},{10,... | collective-permute-start | bytes 688136 | tf_op jit(solution)/shard_map/ppermute | solution.py:75
  126.2 28.3 %collective-permute-done.23.refs_0_ = bf16[128,896]{1,0:T(8,128)(2,1)S(1)} collective-permute-done((bf16[128,896]{1,0:T(8,128)(2,1)S(1)}, bf16[128,896]{1,0:T(8,128)(2,1)S(1)}, u32[]{:S(2)}, u32[]{:S(2)}) %collective-permute-start.23) | collective-permute-done | bytes 229408 | tf_op jit(solution)/shard_map/ppermute | solution.py:75
  154.5 1.8 %place_rows.1 = bf16[2,8,2,32,896]{4,3,2,1,0:T(8,128)(2,1)} custom-call(s32[5]{0:T(128)S(1)} %stack.23.p_ref.s_ref, bf16[12,32,896]{2,1,0:T(8,128)(2,1)S(1)} %bitcast.17, bf16[4,32,896]{2,1,0:T(8,128)(2,1)S(1)} %bitcast.19, bf16[8,32,896]{2,1,0:T(8,128)(2,1)S(1)} %bitcast.20, bf16[8,32,896]{2,1,0:T(8,128)(2,1)S(1)} %bitcast.21), custom_call_target="tpu_custom_call" | custom-call | tf_op jit(solution)/shard_map/place_rows/pallas_call | solution.py:383
  (54 shorter events, 14.4 us)
Async XLA Ops:
  52.2 3.9 %collective-permute-start = (bf16[1024,896]{1,0:T(8,128)(2,1)S(1)}, bf16[1024,896]{1,0:T(8,128)(2,1)}, u32[]{:S(2)}, u32[]{:S(2)}) collective-permute-start(bf16[1024,896]{1,0:T(8,128)(2,1)S(1)} %bitcast.14), channel_id=1, source_target_pairs={{0,1},{1,0},{2,3},{3,2},{4,5},{5,4},{6,7},{7,6},{8,9},{9,8},{10,11... | collective-permute-start | bytes 5505032 | tf_op jit(solution)/shard_map/ppermute | solution.py:75
  59.6 11.2 %collective-permute-start.1 = (bf16[4,128,384]{2,1,0:T(8,128)(2,1)S(1)}, bf16[4,128,384]{2,1,0:T(8,128)(2,1)S(1)}, u32[]{:S(2)}, u32[]{:S(2)}) collective-permute-start(bf16[4,128,384]{2,1,0:T(8,128)(2,1)S(1)} %get-tuple-element.33), channel_id=1, source_target_pairs={{0,8},{1,9},{2,10},{3,11},{4,12},{5,13},{6,14},{7,15},{8,0},{9,1},... | collective-permute-start | bytes 1179656 | tf_op jit(solution)/shard_map/ppermute | solution.py:75
  61.1 11.3 %collective-permute-start.6 = (bf16[4,128,384]{2,1,0:T(8,128)(2,1)S(1)}, bf16[4,128,384]{2,1,0:T(8,128)(2,1)S(1)}, u32[]{:S(2)}, u32[]{:S(2)}) collective-permute-start(bf16[4,128,384]{2,1,0:T(8,128)(2,1)S(1)} %get-tuple-element.39), channel_id=1, source_target_pairs={{0,16},{1,17},{2,18},{3,19},{4,20},{5,21},{6,22},{7,23},{8,24},{9,... | collective-permute-start | bytes 1179656 | tf_op jit(solution)/shard_map/ppermute | solution.py:75
  62.6 10.9 %collective-permute-start.11 = (bf16[4,128,384]{2,1,0:T(8,128)(2,1)S(1)}, bf16[4,128,384]{2,1,0:T(8,128)(2,1)S(1)}, u32[]{:S(2)}, u32[]{:S(2)}) collective-permute-start(bf16[4,128,384]{2,1,0:T(8,128)(2,1)S(1)} %get-tuple-element.45), channel_id=1, source_target_pairs={{0,2},{1,3},{2,0},{3,1},{4,6},{5,7},{6,4},{7,5},{8,10},{9,11},{10,... | collective-permute-start | bytes 1179656 | tf_op jit(solution)/shard_map/ppermute | solution.py:75
  70.9 6.2 %collective-permute-start.2 = (bf16[2,128,384]{2,1,0:T(8,128)(2,1)S(1)}, bf16[2,128,384]{2,1,0:T(8,128)(2,1)S(1)}, u32[]{:S(2)}, u32[]{:S(2)}) collective-permute-start(bf16[2,128,384]{2,1,0:T(8,128)(2,1)S(1)} %get-tuple-element.35), channel_id=1, source_target_pairs={{0,16},{1,17},{2,18},{3,19},{4,20},{5,21},{6,22},{7,23},{8,24},{9,... | collective-permute-start | bytes 589832 | tf_op jit(solution)/shard_map/ppermute | solution.py:75
  72.5 6.1 %collective-permute-start.7 = (bf16[2,128,384]{2,1,0:T(8,128)(2,1)S(1)}, bf16[2,128,384]{2,1,0:T(8,128)(2,1)S(1)}, u32[]{:S(2)}, u32[]{:S(2)}) collective-permute-start(bf16[2,128,384]{2,1,0:T(8,128)(2,1)S(1)} %get-tuple-element.41), channel_id=1, source_target_pairs={{0,2},{1,3},{2,0},{3,1},{4,6},{5,7},{6,4},{7,5},{8,10},{9,11},{10,... | collective-permute-start | bytes 589832 | tf_op jit(solution)/shard_map/ppermute | solution.py:75
  73.6 6.6 %collective-permute-start.12 = (bf16[2,128,384]{2,1,0:T(8,128)(2,1)S(1)}, bf16[2,128,384]{2,1,0:T(8,128)(2,1)S(1)}, u32[]{:S(2)}, u32[]{:S(2)}) collective-permute-start(bf16[2,128,384]{2,1,0:T(8,128)(2,1)S(1)} %get-tuple-element.47), channel_id=1, source_target_pairs={{0,8},{1,9},{2,10},{3,11},{4,12},{5,13},{6,14},{7,15},{8,0},{9,1},... | collective-permute-start | bytes 589832 | tf_op jit(solution)/shard_map/ppermute | solution.py:75
  77.1 5.7 %collective-permute-start.3 = (bf16[2,128,384]{2,1,0:T(8,128)(2,1)S(1)}, bf16[2,128,384]{2,1,0:T(8,128)(2,1)S(1)}, u32[]{:S(2)}, u32[]{:S(2)}) collective-permute-start(bf16[2,128,384]{2,1,0:T(8,128)(2,1)S(1)} %get-tuple-element.37), channel_id=1, source_target_pairs={{0,2},{1,3},{2,0},{3,1},{4,6},{5,7},{6,4},{7,5},{8,10},{9,11},{10,... | collective-permute-start | bytes 589832 | tf_op jit(solution)/shard_map/ppermute | solution.py:75
  78.7 5.8 %collective-permute-start.8 = (bf16[2,128,384]{2,1,0:T(8,128)(2,1)S(1)}, bf16[2,128,384]{2,1,0:T(8,128)(2,1)S(1)}, u32[]{:S(2)}, u32[]{:S(2)}) collective-permute-start(bf16[2,128,384]{2,1,0:T(8,128)(2,1)S(1)} %get-tuple-element.43), channel_id=1, source_target_pairs={{0,8},{1,9},{2,10},{3,11},{4,12},{5,13},{6,14},{7,15},{8,0},{9,1},... | collective-permute-start | bytes 589832 | tf_op jit(solution)/shard_map/ppermute | solution.py:75
  80.3 7.0 %collective-permute-start.13 = (bf16[2,128,384]{2,1,0:T(8,128)(2,1)S(1)}, bf16[2,128,384]{2,1,0:T(8,128)(2,1)S(1)}, u32[]{:S(2)}, u32[]{:S(2)}) collective-permute-start(bf16[2,128,384]{2,1,0:T(8,128)(2,1)S(1)} %get-tuple-element.49), channel_id=1, source_target_pairs={{0,16},{1,17},{2,18},{3,19},{4,20},{5,21},{6,22},{7,23},{8,24},{9,... | collective-permute-start | bytes 589832 | tf_op jit(solution)/shard_map/ppermute | solution.py:75
  82.9 6.5 %collective-permute-start.4 = (bf16[2,128,384]{2,1,0:T(8,128)(2,1)S(1)}, bf16[2,128,384]{2,1,0:T(8,128)(2,1)S(1)}, u32[]{:S(2)}, u32[]{:S(2)}) collective-permute-start(bf16[2,128,384]{2,1,0:T(8,128)(2,1)S(1)} %add_last.3), channel_id=1, source_target_pairs={{0,16},{1,17},{2,18},{3,19},{4,20},{5,21},{6,22},{7,23},{8,24},{9,... | collective-permute-start | bytes 589832 | tf_op jit(solution)/shard_map/ppermute | solution.py:75
  84.5 6.5 %collective-permute-start.9 = (bf16[2,128,384]{2,1,0:T(8,128)(2,1)S(1)}, bf16[2,128,384]{2,1,0:T(8,128)(2,1)S(1)}, u32[]{:S(2)}, u32[]{:S(2)}) collective-permute-start(bf16[2,128,384]{2,1,0:T(8,128)(2,1)S(1)} %add_last.4), channel_id=1, source_target_pairs={{0,2},{1,3},{2,0},{3,1},{4,6},{5,7},{6,4},{7,5},{8,10},{9,11},{10,... | collective-permute-start | bytes 589832 | tf_op jit(solution)/shard_map/ppermute | solution.py:75
  87.3 6.1 %collective-permute-start.14 = (bf16[2,128,384]{2,1,0:T(8,128)(2,1)S(1)}, bf16[2,128,384]{2,1,0:T(8,128)(2,1)S(1)}, u32[]{:S(2)}, u32[]{:S(2)}) collective-permute-start(bf16[2,128,384]{2,1,0:T(8,128)(2,1)S(1)} %add_last.5), channel_id=1, source_target_pairs={{0,8},{1,9},{2,10},{3,11},{4,12},{5,13},{6,14},{7,15},{8,0},{9,1},... | collective-permute-start | bytes 589832 | tf_op jit(solution)/shard_map/ppermute | solution.py:75
  89.4 5.2 %collective-permute-start.19 = (bf16[4,128,384]{2,1,0:T(8,128)(2,1)S(1)}, bf16[4,128,384]{2,1,0:T(8,128)(2,1)S(1)}, u32[]{:S(2)}, u32[]{:S(2)}) collective-permute-start(bf16[4,128,384]{2,1,0:T(8,128)(2,1)S(1)} %pad_maximum_fusion.refs_0_), channel_id=1, source_target_pairs={{0,1},{1,0},{2,3},{3,2},{4,5},{5,4},{6,7},{7,6},{8,9},{9,8},{10,11... | collective-permute-start | bytes 1179656 | tf_op jit(solution)/shard_map/ppermute | solution.py:75
  89.5 12.0 %collective-permute-start.5 = (bf16[4,128,384]{2,1,0:T(8,128)(2,1)S(1)}, bf16[4,128,384]{2,1,0:T(8,128)(2,1)S(1)}, u32[]{:S(2)}, u32[]{:S(2)}) collective-permute-start(bf16[4,128,384]{2,1,0:T(8,128)(2,1)S(1)} %pad_maximum_fusion.refs_0_), channel_id=1, source_target_pairs={{0,8},{1,9},{2,10},{3,11},{4,12},{5,13},{6,14},{7,15},{8,0},{9,1},... | collective-permute-start | bytes 1179656 | tf_op jit(solution)/shard_map/ppermute | solution.py:75
  91.0 11.3 %collective-permute-start.10 = (bf16[4,128,384]{2,1,0:T(8,128)(2,1)S(1)}, bf16[4,128,384]{2,1,0:T(8,128)(2,1)S(1)}, u32[]{:S(2)}, u32[]{:S(2)}) collective-permute-start(bf16[4,128,384]{2,1,0:T(8,128)(2,1)S(1)} %pad_maximum_fusion.1.refs_1_), channel_id=1, source_target_pairs={{0,16},{1,17},{2,18},{3,19},{4,20},{5,21},{6,22},{7,23},{8,24},{9,... | collective-permute-start | bytes 1179656 | tf_op jit(solution)/shard_map/ppermute | solution.py:75
  93.5 9.6 %collective-permute-start.15 = (bf16[4,128,384]{2,1,0:T(8,128)(2,1)S(1)}, bf16[4,128,384]{2,1,0:T(8,128)(2,1)S(1)}, u32[]{:S(2)}, u32[]{:S(2)}) collective-permute-start(bf16[4,128,384]{2,1,0:T(8,128)(2,1)S(1)} %pad_maximum_fusion.2.refs_2_), channel_id=1, source_target_pairs={{0,2},{1,3},{2,0},{3,1},{4,6},{5,7},{6,4},{7,5},{8,10},{9,11},{10,... | collective-permute-start | bytes 1179656 | tf_op jit(solution)/shard_map/ppermute | solution.py:75
  94.7 8.4 %collective-permute-start.20 = (bf16[4,128,384]{2,1,0:T(8,128)(2,1)S(1)}, bf16[4,128,384]{2,1,0:T(8,128)(2,1)S(1)}, u32[]{:S(2)}, u32[]{:S(2)}) collective-permute-start(bf16[4,128,384]{2,1,0:T(8,128)(2,1)S(1)} %pad_maximum_fusion.1.refs_1_), channel_id=1, source_target_pairs={{0,1},{1,0},{2,3},{3,2},{4,5},{5,4},{6,7},{7,6},{8,9},{9,8},{10,11... | collective-permute-start | bytes 1179656 | tf_op jit(solution)/shard_map/ppermute | solution.py:75
  94.7 8.4 %collective-permute-start.21 = (bf16[4,128,384]{2,1,0:T(8,128)(2,1)S(1)}, bf16[4,128,384]{2,1,0:T(8,128)(2,1)S(1)}, u32[]{:S(2)}, u32[]{:S(2)}) collective-permute-start(bf16[4,128,384]{2,1,0:T(8,128)(2,1)S(1)} %pad_maximum_fusion.2.refs_2_), channel_id=1, source_target_pairs={{0,1},{1,0},{2,3},{3,2},{4,5},{5,4},{6,7},{7,6},{8,9},{9,8},{10,11... | collective-permute-start | bytes 1179656 | tf_op jit(solution)/shard_map/ppermute | solution.py:75
  101.5 3.3 %collective-permute-start.16 = (bf16[4,128,384]{2,1,0:T(8,128)(2,1)S(1)}, bf16[4,128,384]{2,1,0:T(8,128)(2,1)S(1)}, u32[]{:S(2)}, u32[]{:S(2)}) collective-permute-start(bf16[4,128,384]{2,1,0:T(8,128)(2,1)S(1)} %collective-permute-done.5.refs_6_.refs_0_), channel_id=1, source_target_pairs={{0,1},{1,0},{2,3},{3,2},{4,5},{5,4},{6,7},{7,6},{8,9},{9,8},{10,11... | collective-permute-start | bytes 1179656 | tf_op jit(solution)/shard_map/ppermute | solution.py:75
  111.7 42.8 %collective-permute-start.22 = (bf16[384,896]{1,0:T(8,128)(2,1)S(1)}, bf16[384,896]{1,0:T(8,128)(2,1)S(1)}, u32[]{:S(2)}, u32[]{:S(2)}) collective-permute-start(bf16[384,896]{1,0:T(8,128)(2,1)S(1)} %get-tuple-element.51), channel_id=1, source_target_pairs={{0,4},{1,6},{2,5},{3,7},{4,0},{5,2},{6,1},{7,3},{8,12},{9,14},{10,... | collective-permute-start | bytes 2064392 | tf_op jit(solution)/shard_map/ppermute | solution.py:75
  120.0 34.5 %collective-permute-start.24 = (bf16[256,896]{1,0:T(8,128)(2,1)S(1)}, bf16[256,896]{1,0:T(8,128)(2,1)S(1)}, u32[]{:S(2)}, u32[]{:S(2)}) collective-permute-start(bf16[256,896]{1,0:T(8,128)(2,1)S(1)} %get-tuple-element.53), channel_id=1, source_target_pairs={{0,0},{1,2},{2,1},{3,3},{4,4},{5,6},{6,5},{7,7},{8,8},{9,10},{10,9... | collective-permute-start | bytes 1376264 | tf_op jit(solution)/shard_map/ppermute | solution.py:75
  120.7 33.8 %collective-permute-start.25 = (bf16[256,896]{1,0:T(8,128)(2,1)S(1)}, bf16[256,896]{1,0:T(8,128)(2,1)S(1)}, u32[]{:S(2)}, u32[]{:S(2)}) collective-permute-start(bf16[256,896]{1,0:T(8,128)(2,1)S(1)} %get-tuple-element.54), channel_id=1, source_target_pairs={{0,0},{1,2},{2,1},{3,3},{4,4},{5,6},{6,5},{7,7},{8,8},{9,10},{10,9... | collective-permute-start | bytes 1376264 | tf_op jit(solution)/shard_map/ppermute | solution.py:75
  123.8 30.7 %collective-permute-start.23 = (bf16[128,896]{1,0:T(8,128)(2,1)S(1)}, bf16[128,896]{1,0:T(8,128)(2,1)S(1)}, u32[]{:S(2)}, u32[]{:S(2)}) collective-permute-start(bf16[128,896]{1,0:T(8,128)(2,1)S(1)} %more_rows.2), channel_id=1, source_target_pairs={{0,4},{1,6},{2,5},{3,7},{4,0},{5,2},{6,1},{7,3},{8,12},{9,14},{10,... | collective-permute-start | bytes 688136 | tf_op jit(solution)/shard_map/ppermute | solution.py:75
  (3 other events, 5.7 us)

commit v6 on v5

--- a/solution.py
+++ b/solution.py
@@ -368,10 +368,12 @@
         (near_own, out.at[matrix, :, core]),
         (near_other, out.at[matrix, :, 1 - core]),
     )
-    copies = [
-        pltpu.make_async_copy(source, target, sems.at[k])
-        for k, (source, target) in enumerate(moves)
-    ]
+    copies = []
+    for source, target in moves:
+        for k in range(0, source.shape[0], 2):
+            pair = pl.ds(k, 2)
+            sem = sems.at[len(copies)]
+            copies.append(pltpu.make_async_copy(source.at[pair], target.at[pair], sem))
     for copy in copies:
         copy.start()
     for copy in copies:
@@ -386,7 +388,7 @@
         in_specs=[pl.BlockSpec(memory_space=pltpu.SMEM)]
         + [pl.BlockSpec(memory_space=pl.ANY)] * len(pieces),
         out_specs=pl.BlockSpec(memory_space=pl.ANY),
-        scratch_shapes=[pltpu.SemaphoreType.DMA((5,))],
+        scratch_shapes=[pltpu.SemaphoreType.DMA((16,))],
         compiler_params=pltpu.CompilerParams(**PARAMS),
         name="place_rows",
     )(scalars, *pieces)

time: 157 us -> 157 us (level)
  no operation moved by 1% of the time
where the time goes in v6:
time: 157 us
  waiting for transfers between devices  55.4 us (35%)
  blocking collectives  50.2 us (32%)
  Pallas kernels  26.7 us (17%)
  starting transfers between devices  22.2 us (14%)
  local copies, waits for them, and re-layouts  1.58 us (1%)
    ppermute x26, waiting for transfers between devices, send(): return lax.ppermute(value, AXES, perm)  55.4 us
    all_to_all x1, blocking collectives, fast_body(): own = lax.all_to_all(pieces, ('gr', 'mat', 'gc'), 0, 0, tiled=True)  50.2 us
    ppermute x26, starting transfers between devices, send(): return lax.ppermute(value, AXES, perm)  22.2 us
    pallas_call x2, Pallas kernels, more_rows(): pl.pallas_call(functools.partial(more_kernel, scalar, parts), out_shape=[...  10 us
    pallas_call x1, Pallas kernels, first_rows(): pl.pallas_call(first_kernel, out_shape=[jax.ShapeDtypeStruct((2048, 2048)...  6.86 us
    pallas_call x1, Pallas kernels, gram_strips(): pl.pallas_call(gram_kernel, out_shape=[jax.ShapeDtypeStruct(shape, jnp.fl...  3.48 us
  transfers between devices with their start and end apart: 26, of which 12 were waited for; matrix products, arithmetic and copies ran while one was open for 0% of the time, Pallas kernels for 9%

profile of v6, /device:TPU:0, one launch (start us, length us, event | category | flops | bytes accessed | tf_op | source)
XLA Modules:
  0.0 156.6 jit_solution(11589566943607218746)
XLA Ops:
  0.0 1.5 copy-done
  2.0 50.2 %all_to_all.5 = bf16[32,32,896]{2,1,0:T(8,128)(2,1)S(1)} all-to-all(bf16[32,32,896]{2,1,0:T(8,128)(2,1)S(1)} %bitcast.13), channel_id=1, replica_groups=mesh['mat'=4,'gr'=4,'gc'=2] {'gr','mat','gc'}, dimensions={0} | all-to-all | bytes 3670016 | tf_op jit(solution)/shard_map/all_to_all | solution.py:412
  52.3 1.7 %own_strips.1 = (f32[8,128,1152]{2,1,0:T(8,128)S(1)}, bf16[2048,896]{1,0:T(8,128)(2,1)S(1)}) custom-call(bf16[1024,896]{1,0:T(8,128)(2,1)S(1)} %bitcast.15), custom_call_target="tpu_custom_call" | custom-call | flops 1174405120 | bytes 10000000 | tf_op jit(solution)/shard_map/own_strips/pallas_call | solution.py:135
  54.0 2.1 %collective-permute-done.other = bf16[1024,896]{1,0:T(8,128)(2,1)} collective-permute-done((bf16[1024,896]{1,0:T(8,128)(2,1)S(1)}, bf16[1024,896]{1,0:T(8,128)(2,1)}, u32[]{:S(2)}, u32[]{:S(2)}) %collective-permute-start) | collective-permute-done | bytes 1835040 | tf_op jit(solution)/shard_map/ppermute | solution.py:75
  56.1 3.5 %gram_strips.1 = (f32[4,128,384]{2,1,0:T(8,128)S(1)}, f32[4,128,384]{2,1,0:T(8,128)S(1)}, f32[4,128,384]{2,1,0:T(8,128)S(1)}, bf16[4,128,384]{2,1,0:T(8,128)(2,1...) custom-call(s32[5]{0:T(128)S(1)} %stack.23.p_ref.s_ref, ...), custom_call_target="tpu_custom_call", output_to_operand_aliasing={{6}: (1, {}), {7}: (2, {})} | custom-call | flops 1174405120 | bytes 10000000 | tf_op jit(solution)/shard_map/gram_strips/pallas_call | solution.py:176
  59.6 1.6 %collective-permute-start.1 = (bf16[4,128,384]{2,1,0:T(8,128)(2,1)S(1)}, bf16[4,128,384]{2,1,0:T(8,128)(2,1)S(1)}, u32[]{:S(2)}, u32[]{:S(2)}) collective-permute-start(bf16[4,128,384]{2,1,0:T(8,128)(2,1)S(1)} %get-tuple-element.33), channel_id=1, source_target_pairs={{0,8},{1,9},{2,10},{3,11},{4,12},{5,13},{6,14},{7,15},{8,0},{9,1},... | collective-permute-start | bytes 1179656 | tf_op jit(solution)/shard_map/ppermute | solution.py:75
  61.1 1.4 collective-permute-start.6
  62.6 8.2 %collective-permute-done.1.came = bf16[4,128,384]{2,1,0:T(8,128)(2,1)S(1)} collective-permute-done((bf16[4,128,384]{2,1,0:T(8,128)(2,1)S(1)}, bf16[4,128,384]{2,1,0:T(8,128)(2,1)S(1)}, u32[]{:S(2)}, u32[]{:S(2)}) %collective-permute-start.1) | collective-permute-done | bytes 393248 | tf_op jit(solution)/shard_map/ppermute | solution.py:75
  70.9 1.5 collective-permute-start.2
  74.3 2.8 %collective-permute-done.2.came = bf16[2,128,384]{2,1,0:T(8,128)(2,1)S(1)} collective-permute-done((bf16[2,128,384]{2,1,0:T(8,128)(2,1)S(1)}, bf16[2,128,384]{2,1,0:T(8,128)(2,1)S(1)}, u32[]{:S(2)}, u32[]{:S(2)}) %collective-permute-start.2) | collective-permute-done | bytes 196640 | tf_op jit(solution)/shard_map/ppermute | solution.py:75
  77.1 1.4 collective-permute-start.3
  78.7 1.5 collective-permute-start.8
  80.7 2.1 %collective-permute-done.3.came = bf16[2,128,384]{2,1,0:T(8,128)(2,1)S(1)} collective-permute-done((bf16[2,128,384]{2,1,0:T(8,128)(2,1)S(1)}, bf16[2,128,384]{2,1,0:T(8,128)(2,1)S(1)}, u32[]{:S(2)}, u32[]{:S(2)}) %collective-permute-start.3) | collective-permute-done | bytes 196640 | tf_op jit(solution)/shard_map/ppermute | solution.py:75
  82.9 1.5 collective-permute-start.4
  85.5 1.8 %collective-permute-done.13.came = bf16[2,128,384]{2,1,0:T(8,128)(2,1)S(1)} collective-permute-done((bf16[2,128,384]{2,1,0:T(8,128)(2,1)S(1)}, bf16[2,128,384]{2,1,0:T(8,128)(2,1)S(1)}, u32[]{:S(2)}, u32[]{:S(2)}) %collective-permute-start.13) | collective-permute-done | bytes 196640 | tf_op jit(solution)/shard_map/ppermute | solution.py:75
  89.5 1.5 collective-permute-start.5
  95.2 6.3 %collective-permute-done.5.refs_6_.refs_0_ = bf16[4,128,384]{2,1,0:T(8,128)(2,1)S(1)} collective-permute-done((bf16[4,128,384]{2,1,0:T(8,128)(2,1)S(1)}, bf16[4,128,384]{2,1,0:T(8,128)(2,1)S(1)}, u32[]{:S(2)}, u32[]{:S(2)}) %collective-permute-start.5) | collective-permute-done | bytes 393248 | tf_op jit(solution)/shard_map/ppermute | solution.py:75
  103.1 1.7 %early_gram.1.refs_6_ = bf16[2048,2048]{1,0:T(8,128)(2,1)S(1)} custom-call(s32[5]{0:T(128)S(1)} %stack.23.p_ref.s_ref, bf16[4,128,384]{2,1,0:T(8,128)(2,1)S(1)} %pad_maximum_fusion.refs_0_, bf16[4,128,384]{2,1,0:T(8,128)(2,1)S(1)} %pad_maximum_fusion.1.refs_1_, bf16[4,128,384]{2,1,0:T(8,128)(2,1)S(1)} %pad_maximum_fusion.2.refs_2_, ...), custom_call_target="tpu_custom_call" | custom-call | flops 100000 | bytes 30000000 | tf_op jit(solution)/shard_map/early_gram/pallas_call | solution.py:269
  104.8 6.9 %first_rows.1 = (bf16[2048,2048]{1,0:T(8,128)(2,1)S(1)}, bf16[384,896]{1,0:T(8,128)(2,1)S(1)}) custom-call(s32[5]{0:T(128)S(1)} %stack.23.p_ref.s_ref, bf16[4,128,384]{2,1,0:T(8,128)(2,1)S(1)} %collective-permute-done.5.refs_6_.refs_0_, bf16[4,128,384]{2,1,0:T(8,128)(2,1)S(1)} %collective-permute-done.10.refs_1_, ...), custom_call_target="tpu_custom_call", output_to_operand_aliasing={{0}: (7, {})} | custom-call | flops 4630511616 | bytes 30000000 | tf_op jit(solution)/shard_map/first_rows/pallas_call | solution.py:306
  112.4 7.6 %more_rows.3 = (bf16[256,896]{1,0:T(8,128)(2,1)S(1)}, bf16[256,896]{1,0:T(8,128)(2,1)S(1)}) custom-call(s32[5]{0:T(128)S(1)} %stack.23.p_ref.s_ref, bf16[2048,2048]{1,0:T(8,128)(2,1)S(1)} %get-tuple-element.52.gram, bf16[2048,896]{1,0:T(8,128)(2,1)S(1)} %get-tuple-element.50.refs_7_.panel), custom_call_target="tpu_custom_call" | custom-call | flops 6174015488 | bytes 10000000 | tf_op jit(solution)/shard_map/more_rows/pallas_call | solution.py:332
  121.4 2.4 %more_rows.2 = bf16[128,896]{1,0:T(8,128)(2,1)S(1)} custom-call(s32[5]{0:T(128)S(1)} %stack.23.p_ref.s_ref, bf16[2048,2048]{1,0:T(8,128)(2,1)S(1)} %get-tuple-element.52.gram, bf16[2048,896]{1,0:T(8,128)(2,1)S(1)} %get-tuple-element.50.refs_7_.panel), custom_call_target="tpu_custom_call" | custom-call | flops 1543503872 | bytes 10000000 | tf_op jit(solution)/shard_map/more_rows/pallas_call | solution.py:332
  123.8 2.4 %collective-permute-start.23 = (bf16[128,896]{1,0:T(8,128)(2,1)S(1)}, bf16[128,896]{1,0:T(8,128)(2,1)S(1)}, u32[]{:S(2)}, u32[]{:S(2)}) collective-permute-start(bf16[128,896]{1,0:T(8,128)(2,1)S(1)} %more_rows.2), channel_id=1, source_target_pairs={{0,4},{1,6},{2,5},{3,7},{4,0},{5,2},{6,1},{7,3},{8,12},{9,14},{10,... | collective-permute-start | bytes 688136 | tf_op jit(solution)/shard_map/ppermute | solution.py:75
  126.2 28.3 %collective-permute-done.23.refs_0_ = bf16[128,896]{1,0:T(8,128)(2,1)S(1)} collective-permute-done((bf16[128,896]{1,0:T(8,128)(2,1)S(1)}, bf16[128,896]{1,0:T(8,128)(2,1)S(1)}, u32[]{:S(2)}, u32[]{:S(2)}) %collective-permute-start.23) | collective-permute-done | bytes 229408 | tf_op jit(solution)/shard_map/ppermute | solution.py:75
  154.5 1.9 %place_rows.1 = bf16[2,8,2,32,896]{4,3,2,1,0:T(8,128)(2,1)} custom-call(s32[5]{0:T(128)S(1)} %stack.23.p_ref.s_ref, bf16[12,32,896]{2,1,0:T(8,128)(2,1)S(1)} %bitcast.17, bf16[4,32,896]{2,1,0:T(8,128)(2,1)S(1)} %bitcast.19, bf16[8,32,896]{2,1,0:T(8,128)(2,1)S(1)} %bitcast.20, bf16[8,32,896]{2,1,0:T(8,128)(2,1)S(1)} %bitcast.21), custom_call_target="tpu_custom_call" | custom-call | tf_op jit(solution)/shard_map/place_rows/pallas_call | solution.py:385
  (54 shorter events, 14.4 us)
Async XLA Ops:
  52.2 3.9 %collective-permute-start = (bf16[1024,896]{1,0:T(8,128)(2,1)S(1)}, bf16[1024,896]{1,0:T(8,128)(2,1)}, u32[]{:S(2)}, u32[]{:S(2)}) collective-permute-start(bf16[1024,896]{1,0:T(8,128)(2,1)S(1)} %bitcast.14), channel_id=1, source_target_pairs={{0,1},{1,0},{2,3},{3,2},{4,5},{5,4},{6,7},{7,6},{8,9},{9,8},{10,11... | collective-permute-start | bytes 5505032 | tf_op jit(solution)/shard_map/ppermute | solution.py:75
  59.6 11.2 %collective-permute-start.1 = (bf16[4,128,384]{2,1,0:T(8,128)(2,1)S(1)}, bf16[4,128,384]{2,1,0:T(8,128)(2,1)S(1)}, u32[]{:S(2)}, u32[]{:S(2)}) collective-permute-start(bf16[4,128,384]{2,1,0:T(8,128)(2,1)S(1)} %get-tuple-element.33), channel_id=1, source_target_pairs={{0,8},{1,9},{2,10},{3,11},{4,12},{5,13},{6,14},{7,15},{8,0},{9,1},... | collective-permute-start | bytes 1179656 | tf_op jit(solution)/shard_map/ppermute | solution.py:75
  61.1 11.3 %collective-permute-start.6 = (bf16[4,128,384]{2,1,0:T(8,128)(2,1)S(1)}, bf16[4,128,384]{2,1,0:T(8,128)(2,1)S(1)}, u32[]{:S(2)}, u32[]{:S(2)}) collective-permute-start(bf16[4,128,384]{2,1,0:T(8,128)(2,1)S(1)} %get-tuple-element.39), channel_id=1, source_target_pairs={{0,16},{1,17},{2,18},{3,19},{4,20},{5,21},{6,22},{7,23},{8,24},{9,... | collective-permute-start | bytes 1179656 | tf_op jit(solution)/shard_map/ppermute | solution.py:75
  62.6 10.9 %collective-permute-start.11 = (bf16[4,128,384]{2,1,0:T(8,128)(2,1)S(1)}, bf16[4,128,384]{2,1,0:T(8,128)(2,1)S(1)}, u32[]{:S(2)}, u32[]{:S(2)}) collective-permute-start(bf16[4,128,384]{2,1,0:T(8,128)(2,1)S(1)} %get-tuple-element.45), channel_id=1, source_target_pairs={{0,2},{1,3},{2,0},{3,1},{4,6},{5,7},{6,4},{7,5},{8,10},{9,11},{10,... | collective-permute-start | bytes 1179656 | tf_op jit(solution)/shard_map/ppermute | solution.py:75
  70.9 6.2 %collective-permute-start.2 = (bf16[2,128,384]{2,1,0:T(8,128)(2,1)S(1)}, bf16[2,128,384]{2,1,0:T(8,128)(2,1)S(1)}, u32[]{:S(2)}, u32[]{:S(2)}) collective-permute-start(bf16[2,128,384]{2,1,0:T(8,128)(2,1)S(1)} %get-tuple-element.35), channel_id=1, source_target_pairs={{0,16},{1,17},{2,18},{3,19},{4,20},{5,21},{6,22},{7,23},{8,24},{9,... | collective-permute-start | bytes 589832 | tf_op jit(solution)/shard_map/ppermute | solution.py:75
  72.5 6.1 %collective-permute-start.7 = (bf16[2,128,384]{2,1,0:T(8,128)(2,1)S(1)}, bf16[2,128,384]{2,1,0:T(8,128)(2,1)S(1)}, u32[]{:S(2)}, u32[]{:S(2)}) collective-permute-start(bf16[2,128,384]{2,1,0:T(8,128)(2,1)S(1)} %get-tuple-element.41), channel_id=1, source_target_pairs={{0,2},{1,3},{2,0},{3,1},{4,6},{5,7},{6,4},{7,5},{8,10},{9,11},{10,... | collective-permute-start | bytes 589832 | tf_op jit(solution)/shard_map/ppermute | solution.py:75
  73.6 6.6 %collective-permute-start.12 = (bf16[2,128,384]{2,1,0:T(8,128)(2,1)S(1)}, bf16[2,128,384]{2,1,0:T(8,128)(2,1)S(1)}, u32[]{:S(2)}, u32[]{:S(2)}) collective-permute-start(bf16[2,128,384]{2,1,0:T(8,128)(2,1)S(1)} %get-tuple-element.47), channel_id=1, source_target_pairs={{0,8},{1,9},{2,10},{3,11},{4,12},{5,13},{6,14},{7,15},{8,0},{9,1},... | collective-permute-start | bytes 589832 | tf_op jit(solution)/shard_map/ppermute | solution.py:75
  77.1 5.7 %collective-permute-start.3 = (bf16[2,128,384]{2,1,0:T(8,128)(2,1)S(1)}, bf16[2,128,384]{2,1,0:T(8,128)(2,1)S(1)}, u32[]{:S(2)}, u32[]{:S(2)}) collective-permute-start(bf16[2,128,384]{2,1,0:T(8,128)(2,1)S(1)} %get-tuple-element.37), channel_id=1, source_target_pairs={{0,2},{1,3},{2,0},{3,1},{4,6},{5,7},{6,4},{7,5},{8,10},{9,11},{10,... | collective-permute-start | bytes 589832 | tf_op jit(solution)/shard_map/ppermute | solution.py:75
  78.7 5.8 %collective-permute-start.8 = (bf16[2,128,384]{2,1,0:T(8,128)(2,1)S(1)}, bf16[2,128,384]{2,1,0:T(8,128)(2,1)S(1)}, u32[]{:S(2)}, u32[]{:S(2)}) collective-permute-start(bf16[2,128,384]{2,1,0:T(8,128)(2,1)S(1)} %get-tuple-element.43), channel_id=1, source_target_pairs={{0,8},{1,9},{2,10},{3,11},{4,12},{5,13},{6,14},{7,15},{8,0},{9,1},... | collective-permute-start | bytes 589832 | tf_op jit(solution)/shard_map/ppermute | solution.py:75
  80.3 7.0 %collective-permute-start.13 = (bf16[2,128,384]{2,1,0:T(8,128)(2,1)S(1)}, bf16[2,128,384]{2,1,0:T(8,128)(2,1)S(1)}, u32[]{:S(2)}, u32[]{:S(2)}) collective-permute-start(bf16[2,128,384]{2,1,0:T(8,128)(2,1)S(1)} %get-tuple-element.49), channel_id=1, source_target_pairs={{0,16},{1,17},{2,18},{3,19},{4,20},{5,21},{6,22},{7,23},{8,24},{9,... | collective-permute-start | bytes 589832 | tf_op jit(solution)/shard_map/ppermute | solution.py:75
  82.9 6.5 %collective-permute-start.4 = (bf16[2,128,384]{2,1,0:T(8,128)(2,1)S(1)}, bf16[2,128,384]{2,1,0:T(8,128)(2,1)S(1)}, u32[]{:S(2)}, u32[]{:S(2)}) collective-permute-start(bf16[2,128,384]{2,1,0:T(8,128)(2,1)S(1)} %add_last.3), channel_id=1, source_target_pairs={{0,16},{1,17},{2,18},{3,19},{4,20},{5,21},{6,22},{7,23},{8,24},{9,... | collective-permute-start | bytes 589832 | tf_op jit(solution)/shard_map/ppermute | solution.py:75
  84.5 6.5 %collective-permute-start.9 = (bf16[2,128,384]{2,1,0:T(8,128)(2,1)S(1)}, bf16[2,128,384]{2,1,0:T(8,128)(2,1)S(1)}, u32[]{:S(2)}, u32[]{:S(2)}) collective-permute-start(bf16[2,128,384]{2,1,0:T(8,128)(2,1)S(1)} %add_last.4), channel_id=1, source_target_pairs={{0,2},{1,3},{2,0},{3,1},{4,6},{5,7},{6,4},{7,5},{8,10},{9,11},{10,... | collective-permute-start | bytes 589832 | tf_op jit(solution)/shard_map/ppermute | solution.py:75
  87.3 6.1 %collective-permute-start.14 = (bf16[2,128,384]{2,1,0:T(8,128)(2,1)S(1)}, bf16[2,128,384]{2,1,0:T(8,128)(2,1)S(1)}, u32[]{:S(2)}, u32[]{:S(2)}) collective-permute-start(bf16[2,128,384]{2,1,0:T(8,128)(2,1)S(1)} %add_last.5), channel_id=1, source_target_pairs={{0,8},{1,9},{2,10},{3,11},{4,12},{5,13},{6,14},{7,15},{8,0},{9,1},... | collective-permute-start | bytes 589832 | tf_op jit(solution)/shard_map/ppermute | solution.py:75
  89.4 5.2 %collective-permute-start.19 = (bf16[4,128,384]{2,1,0:T(8,128)(2,1)S(1)}, bf16[4,128,384]{2,1,0:T(8,128)(2,1)S(1)}, u32[]{:S(2)}, u32[]{:S(2)}) collective-permute-start(bf16[4,128,384]{2,1,0:T(8,128)(2,1)S(1)} %pad_maximum_fusion.refs_0_), channel_id=1, source_target_pairs={{0,1},{1,0},{2,3},{3,2},{4,5},{5,4},{6,7},{7,6},{8,9},{9,8},{10,11... | collective-permute-start | bytes 1179656 | tf_op jit(solution)/shard_map/ppermute | solution.py:75
  89.5 12.0 %collective-permute-start.5 = (bf16[4,128,384]{2,1,0:T(8,128)(2,1)S(1)}, bf16[4,128,384]{2,1,0:T(8,128)(2,1)S(1)}, u32[]{:S(2)}, u32[]{:S(2)}) collective-permute-start(bf16[4,128,384]{2,1,0:T(8,128)(2,1)S(1)} %pad_maximum_fusion.refs_0_), channel_id=1, source_target_pairs={{0,8},{1,9},{2,10},{3,11},{4,12},{5,13},{6,14},{7,15},{8,0},{9,1},... | collective-permute-start | bytes 1179656 | tf_op jit(solution)/shard_map/ppermute | solution.py:75
  91.0 11.3 %collective-permute-start.10 = (bf16[4,128,384]{2,1,0:T(8,128)(2,1)S(1)}, bf16[4,128,384]{2,1,0:T(8,128)(2,1)S(1)}, u32[]{:S(2)}, u32[]{:S(2)}) collective-permute-start(bf16[4,128,384]{2,1,0:T(8,128)(2,1)S(1)} %pad_maximum_fusion.1.refs_1_), channel_id=1, source_target_pairs={{0,16},{1,17},{2,18},{3,19},{4,20},{5,21},{6,22},{7,23},{8,24},{9,... | collective-permute-start | bytes 1179656 | tf_op jit(solution)/shard_map/ppermute | solution.py:75
  93.5 9.6 %collective-permute-start.15 = (bf16[4,128,384]{2,1,0:T(8,128)(2,1)S(1)}, bf16[4,128,384]{2,1,0:T(8,128)(2,1)S(1)}, u32[]{:S(2)}, u32[]{:S(2)}) collective-permute-start(bf16[4,128,384]{2,1,0:T(8,128)(2,1)S(1)} %pad_maximum_fusion.2.refs_2_), channel_id=1, source_target_pairs={{0,2},{1,3},{2,0},{3,1},{4,6},{5,7},{6,4},{7,5},{8,10},{9,11},{10,... | collective-permute-start | bytes 1179656 | tf_op jit(solution)/shard_map/ppermute | solution.py:75
  94.7 8.4 %collective-permute-start.20 = (bf16[4,128,384]{2,1,0:T(8,128)(2,1)S(1)}, bf16[4,128,384]{2,1,0:T(8,128)(2,1)S(1)}, u32[]{:S(2)}, u32[]{:S(2)}) collective-permute-start(bf16[4,128,384]{2,1,0:T(8,128)(2,1)S(1)} %pad_maximum_fusion.1.refs_1_), channel_id=1, source_target_pairs={{0,1},{1,0},{2,3},{3,2},{4,5},{5,4},{6,7},{7,6},{8,9},{9,8},{10,11... | collective-permute-start | bytes 1179656 | tf_op jit(solution)/shard_map/ppermute | solution.py:75
  94.7 8.4 %collective-permute-start.21 = (bf16[4,128,384]{2,1,0:T(8,128)(2,1)S(1)}, bf16[4,128,384]{2,1,0:T(8,128)(2,1)S(1)}, u32[]{:S(2)}, u32[]{:S(2)}) collective-permute-start(bf16[4,128,384]{2,1,0:T(8,128)(2,1)S(1)} %pad_maximum_fusion.2.refs_2_), channel_id=1, source_target_pairs={{0,1},{1,0},{2,3},{3,2},{4,5},{5,4},{6,7},{7,6},{8,9},{9,8},{10,11... | collective-permute-start | bytes 1179656 | tf_op jit(solution)/shard_map/ppermute | solution.py:75
  101.5 3.3 %collective-permute-start.16 = (bf16[4,128,384]{2,1,0:T(8,128)(2,1)S(1)}, bf16[4,128,384]{2,1,0:T(8,128)(2,1)S(1)}, u32[]{:S(2)}, u32[]{:S(2)}) collective-permute-start(bf16[4,128,384]{2,1,0:T(8,128)(2,1)S(1)} %collective-permute-done.5.refs_6_.refs_0_), channel_id=1, source_target_pairs={{0,1},{1,0},{2,3},{3,2},{4,5},{5,4},{6,7},{7,6},{8,9},{9,8},{10,11... | collective-permute-start | bytes 1179656 | tf_op jit(solution)/shard_map/ppermute | solution.py:75
  111.7 42.8 %collective-permute-start.22 = (bf16[384,896]{1,0:T(8,128)(2,1)S(1)}, bf16[384,896]{1,0:T(8,128)(2,1)S(1)}, u32[]{:S(2)}, u32[]{:S(2)}) collective-permute-start(bf16[384,896]{1,0:T(8,128)(2,1)S(1)} %get-tuple-element.51), channel_id=1, source_target_pairs={{0,4},{1,6},{2,5},{3,7},{4,0},{5,2},{6,1},{7,3},{8,12},{9,14},{10,... | collective-permute-start | bytes 2064392 | tf_op jit(solution)/shard_map/ppermute | solution.py:75
  120.0 34.5 %collective-permute-start.24 = (bf16[256,896]{1,0:T(8,128)(2,1)S(1)}, bf16[256,896]{1,0:T(8,128)(2,1)S(1)}, u32[]{:S(2)}, u32[]{:S(2)}) collective-permute-start(bf16[256,896]{1,0:T(8,128)(2,1)S(1)} %get-tuple-element.53), channel_id=1, source_target_pairs={{0,0},{1,2},{2,1},{3,3},{4,4},{5,6},{6,5},{7,7},{8,8},{9,10},{10,9... | collective-permute-start | bytes 1376264 | tf_op jit(solution)/shard_map/ppermute | solution.py:75
  120.7 33.8 %collective-permute-start.25 = (bf16[256,896]{1,0:T(8,128)(2,1)S(1)}, bf16[256,896]{1,0:T(8,128)(2,1)S(1)}, u32[]{:S(2)}, u32[]{:S(2)}) collective-permute-start(bf16[256,896]{1,0:T(8,128)(2,1)S(1)} %get-tuple-element.54), channel_id=1, source_target_pairs={{0,0},{1,2},{2,1},{3,3},{4,4},{5,6},{6,5},{7,7},{8,8},{9,10},{10,9... | collective-permute-start | bytes 1376264 | tf_op jit(solution)/shard_map/ppermute | solution.py:75
  123.8 30.7 %collective-permute-start.23 = (bf16[128,896]{1,0:T(8,128)(2,1)S(1)}, bf16[128,896]{1,0:T(8,128)(2,1)S(1)}, u32[]{:S(2)}, u32[]{:S(2)}) collective-permute-start(bf16[128,896]{1,0:T(8,128)(2,1)S(1)} %more_rows.2), channel_id=1, source_target_pairs={{0,4},{1,6},{2,5},{3,7},{4,0},{5,2},{6,1},{7,3},{8,12},{9,14},{10,... | collective-permute-start | bytes 688136 | tf_op jit(solution)/shard_map/ppermute | solution.py:75
  (3 other events, 5.7 us)
